TPU v7x, 32 devices: a whole 2x2x4 slice. The times are simulated.
32 devices in a mesh: wide: 4 (over y, x), narrow: 8 (over z, core).
Axes of the slice: x: 2, y: 2, z: 4, core: 2. Of those that a mesh axis runs over, the one named last changes fastest.
Arguments:
- x_in: bfloat16 [64, 640, 768], P(('wide', 'narrow'))
- cotangent: bfloat16 [64, 640, 768], P(('wide', 'narrow')), may hold values from -6 to 6
- segment_ids: int32 [64, 640], P(('wide', 'narrow')), may hold values from 0 to 7, never falling along the last dimension, each value on 1 to 320 neighbouring positions
- type_ids: int32 [64, 640], P(('wide', 'narrow')), may hold values 0 or 1
- projection: float32 [768, 4608], P('narrow'), may hold values from -0.21875 to 0.21875
- context_out: float32 [768, 768], P('narrow'), may hold values from -2 to 2
- expand_weight: float32 [768, 3072], P('narrow'), may hold values from -0.21875 to 0.21875
- reduce_weight: float32 [3072, 768], P('narrow'), may hold values from -0.109375 to 0.109375
- vector_params: float32 [15, 768], P(None, 'narrow')
- first_projection: float32 [768, 4608], P('narrow'), may hold values from -0.00048828125 to 0.00048828125
- first_context: float32 [768, 768], P('narrow'), may hold values from -0.00048828125 to 0.00048828125
- first_expand: float32 [768, 3072], P('narrow'), may hold values from -0.00048828125 to 0.00048828125
- first_reduce: float32 [3072, 768], P('narrow'), may hold values from -0.00048828125 to 0.00048828125
- first_vectors: float32 [15, 768], P(None, 'narrow'), may hold values from -0.0017089844 to 0.0017089844
- second_projection: float32 [768, 4608], P('narrow'), may hold values from 1.12881086e-10 to 4.5152435e-10
- second_context: float32 [768, 768], P('narrow'), may hold values from 2.2576217e-11 to 9.030487e-11
- second_expand: float32 [768, 3072], P('narrow'), may hold values from 1.12881086e-10 to 4.5152435e-10
- second_reduce: float32 [3072, 768], P('narrow'), may hold values from 1.12881086e-10 to 4.5152435e-10
- second_vectors: float32 [15, 768], P(None, 'narrow'), may hold values from 1.1288108e-09 to 4.5152433e-09
Outputs:
- block_out: bfloat16 [64, 640, 768], P(('wide', 'narrow'))
- input_grad: bfloat16 [64, 640, 768], P(('wide', 'narrow'))
- grad_norm: float32 [], replicated
- new_projection: float32 [768, 4608], P('narrow')
- new_context: float32 [768, 768], P('narrow')
- new_expand: float32 [768, 3072], P('narrow')
- new_reduce: float32 [3072, 768], P('narrow')
- new_vectors: float32 [15, 768], P(None, 'narrow')
- next_first_projection: float32 [768, 4608], P('narrow')
- next_first_context: float32 [768, 768], P('narrow')
- next_first_expand: float32 [768, 3072], P('narrow')
- next_first_reduce: float32 [3072, 768], P('narrow')
- next_first_vectors: float32 [15, 768], P(None, 'narrow')
- next_second_projection: float32 [768, 4608], P('narrow')
- next_second_context: float32 [768, 768], P('narrow')
- next_second_expand: float32 [768, 3072], P('narrow')
- next_second_reduce: float32 [3072, 768], P('narrow')
- next_second_vectors: float32 [15, 768], P(None, 'narrow')
- copy_projection: bfloat16 [768, 4608], P('narrow')
- copy_context: bfloat16 [768, 768], P('narrow')
- copy_expand: bfloat16 [768, 3072], P('narrow')
- copy_reduce: bfloat16 [3072, 768], P('narrow')
- copy_vectors: bfloat16 [15, 768], P(None, 'narrow')
Inputs may be any that keep to these rules, and one draw needn't show every extreme that they name: `segment_ids`: ids never fall along a sequence; each document holds 1 to 320 positions.
All inputs are finite; a program needn't handle non-finite values. No bound on the sum of `type_ids` on one device may be relied on, other than what follows from the above.
Results may differ from a plain program's by a relative error of at most 0.017.
Values may be sent and summed in bfloat16 or wider, within the bound.
A program may use at most 256 MiB of HBM per device.

v0:
```python
import functools

import jax
import jax.numpy as jnp
from jax import lax
from jax.experimental import pallas as pl
from jax.experimental.pallas import tpu as pltpu
from jax.sharding import PartitionSpec as P

HEAD = 64
STEP = 10
LANES = 128
GROUP = 6 * HEAD
LOG2E = 1.4426950408889634
FAR = -1e30
VMEM_LIMIT = 60 * 1024 * 1024

beta_one = 0.9
beta_two = 0.999
adam_eps = 1e-08
norm_eps = 1e-05
clip_limit = 1.0
rate_table = (0.03, 0.3, 0.03, 0.015, 0.4)
decay_table = (0.01, 0.01, 0.01, 0.01, 0.0)

F32 = jnp.float32
BF16 = jnp.bfloat16


def mm(a, b):
    return lax.dot_general(a, b, (((1,), (0,)), ((), ())), preferred_element_type=F32)


def mm_nt(a, b):
    return lax.dot_general(a, b, (((1,), (1,)), ((), ())), preferred_element_type=F32)


def mm_tn(a, b):
    return lax.dot_general(a, b, (((0,), (0,)), ((), ())), preferred_element_type=F32)


def low_lanes(rows):
    return lax.broadcasted_iota(jnp.int32, (rows, LANES), 1) < HEAD


def swap_halves(tile):
    return pltpu.roll(tile, HEAD, 1)


def split_three(col):
    high = col.astype(BF16).astype(F32)
    rest = col - high
    mid = rest.astype(BF16).astype(F32)
    return high, mid, rest - mid


def qkv_tile(prod, bias, word):
    full = prod + bias
    query = jnp.where(word, full[:, 0:LANES], full[:, LANES : 2 * LANES])
    return (query.astype(BF16).astype(F32) * (HEAD**-0.5)).astype(BF16), full[
        :, 2 * LANES :
    ].astype(BF16)


def qkv_kernel(x_ref, w_ref, b_ref, word_ref, q_ref, kv_ref):
    word = word_ref[...] > 0
    for part in range(2):
        cols = slice(part * GROUP, (part + 1) * GROUP)
        query, keyval = qkv_tile(mm(x_ref[...], w_ref[:, cols]), b_ref[:, cols], word)
        out = slice(part * LANES, (part + 1) * LANES)
        q_ref[:, out] = query
        kv_ref[:, out] = keyval


def qkv_call(x, w, bias, word):
    rows, width = x.shape
    steps = w.shape[1] // (2 * GROUP)
    out = jax.ShapeDtypeStruct((rows, steps * 2 * LANES), BF16)
    return pl.pallas_call(
        qkv_kernel,
        grid=(steps,),
        in_specs=[
            pl.BlockSpec((rows, width), lambda i: (0, 0)),
            pl.BlockSpec((width, 2 * GROUP), lambda i: (0, i)),
            pl.BlockSpec((1, 2 * GROUP), lambda i: (0, i)),
            pl.BlockSpec((rows, LANES), lambda i: (0, 0)),
        ],
        out_specs=[pl.BlockSpec((rows, 2 * LANES), lambda i: (0, i))] * 2,
        out_shape=[out, out],
        compiler_params=pltpu.CompilerParams(vmem_limit_bytes=VMEM_LIMIT),
        name="qkv",
    )(x, w, bias, word)


class Links:
    def __init__(self, send, recv):
        self.send, self.recv = send, recv
        self.count = 0
        self.slots = {}
        self.open = []

    def slot(self, key):
        if key not in self.slots:
            self.slots[key] = len(self.slots)
        return self.slots[key]

    def copy(self, key, src, dst, device):
        index = self.slot(key)
        return pltpu.make_async_remote_copy(
            src_ref=src,
            dst_ref=dst,
            send_sem=self.send.at[index],
            recv_sem=self.recv.at[index],
            device_id=device,
            device_id_type=pl.DeviceIdType.MESH,
        )

    def start(self, key, src, dst, device):
        copy = self.copy(key, src, dst, device)
        copy.start()
        self.open.append(copy)

    def arrived(self, key, dst, device):
        self.copy(key, dst, dst, device).wait_recv()

    def finish(self):
        for copy in self.open:
            copy.wait_send()
        self.open = []


class Place:
    def __init__(self, narrow):
        self.wide, self.me = lax.axis_index("wide"), lax.axis_index("narrow")
        self.core = lax.rem(self.me, 2)
        self.z = self.me // 2
        self.depth = narrow // 2
        self.x_quarter = self.wide + 1 - 2 * lax.rem(self.wide, 2)
        self.y_quarter = lax.rem(self.wide + 2, 4)
        self.d_quarter = lax.rem(self.x_quarter + 2, 4)
        self.sib = self.me + 1 - 2 * self.core
        self.x_dev, self.y_dev = {"wide": self.x_quarter}, {"wide": self.y_quarter}
        self.sib_dev = {"narrow": self.sib}

    def ahead(self, k):
        return 2 * lax.rem(self.z + k, self.depth) + self.core

    def behind(self, k, other=False):
        core = 1 - self.core if other else self.core
        return 2 * lax.rem(self.z + self.depth - k, self.depth) + core

    def z_dev(self, k):
        return {"narrow": self.ahead(k)}

    def greet(self):
        barrier = pltpu.get_barrier_semaphore()
        partners = [self.x_dev, self.y_dev, self.sib_dev] + [self.z_dev(k) for k in range(1, self.depth)]
        for device in partners:
            pl.semaphore_signal(barrier, inc=1, device_id=device, device_id_type=pl.DeviceIdType.MESH)
        pl.semaphore_wait(barrier, len(partners))


def spot(start, size, unit):
    return pl.ds(pl.multiple_of(start, unit), size)


def gather_kernel(
    narrow, x_ref, proj_ref, wo_ref, w1_ref, w2_ref, vec_ref, seg_ref, type_ref,
    q_out, kv_out, ctx_out, aug_out, a_out, e_out, w2_out, vec_out, word_ref, km_ref, ka_ref,
    a_full, e_own, w2_own, v_all, bias, q_s, kv_s, ctx_s, aug_s, qa_ref, send, recv, local,
):
    rows, width = x_ref.shape
    share = proj_ref.shape[0]
    deep = w2_ref.shape[0]
    half, quarter, equarter, dquarter = share // 2, proj_ref.shape[1] // 4, e_own.shape[1] // 4, deep // 4
    heads = width // HEAD
    here = Place(narrow)
    links = Links(send, recv)
    me, steps = here.me, range(1, here.depth)

    def region(kind, owner, part, side=None):
        size, start = (share, 0) if side is None else (half, side * half)
        if kind == "a":
            return a_full.at[spot(owner * share + start, size, 16), spot(part * quarter, quarter, LANES)]
        if kind == "e":
            return e_out.at[spot(owner * share + start, size, 16), spot(part * equarter, equarter, LANES)]
        size, start = (dquarter, 0) if side is None else (dquarter // 2, side * (dquarter // 2))
        return w2_out.at[spot(owner * deep + part * dquarter + start, size, 16), :]

    def whole(kind, owner):
        if kind == "a":
            return a_full.at[spot(owner * share, share, 16), :]
        if kind == "e":
            return e_out.at[spot(owner * share, share, 16), :]
        if kind == "w":
            return w2_out.at[spot(owner * deep, deep, 16), :]
        return v_all.at[owner]

    def own(kind):
        return {"a": whole("a", me), "e": e_own, "w": w2_own, "v": v_all.at[me]}[kind]

    def own_quarter(kind):
        if kind == "a":
            return region("a", me, here.wide)
        if kind == "e":
            return e_own.at[:, spot(here.wide * equarter, equarter, LANES)]
        return w2_own.at[spot(here.wide * dquarter, dquarter, 16), :]

    def send_z(kind, k):
        links.start((kind, "z", k), own_quarter(kind), region(kind, me, here.wide), here.z_dev(k))

    def send_own(kind):
        links.start((kind, "o"), own(kind), whole(kind, me), here.sib_dev)

    def pass_z(kind, k):
        piece = region(kind, here.behind(k), here.wide)
        links.arrived((kind, "z", k), piece, here.z_dev(k))
        links.start((kind, "x", k), piece, piece, here.x_dev)
        links.start((kind, "y", k), piece, piece, here.y_dev)
        links.start((kind, "sz", k), piece, piece, here.sib_dev)

    def pass_xy(kind, k):
        owner = here.behind(k)
        piece = region(kind, owner, here.x_quarter)
        links.arrived((kind, "x", k), piece, here.x_dev)
        part = region(kind, owner, here.x_quarter, 0)
        links.start((kind, "dy", k), part, part, here.y_dev)
        links.start((kind, "sx", k), piece, piece, here.sib_dev)
        piece = region(kind, owner, here.y_quarter)
        links.arrived((kind, "y", k), piece, here.y_dev)
        part = region(kind, owner, here.y_quarter, 1)
        links.start((kind, "dx", k), part, part, here.x_dev)
        links.start((kind, "sy", k), piece, piece, here.sib_dev)

    def pass_d(kind, k):
        owner = here.behind(k)
        links.arrived((kind, "dy", k), region(kind, owner, here.d_quarter, 0), here.y_dev)
        links.arrived((kind, "dx", k), region(kind, owner, here.d_quarter, 1), here.x_dev)
        piece = region(kind, owner, here.d_quarter)
        links.start((kind, "sd", k), piece, piece, here.sib_dev)

    def from_sib(kind, way, part):
        for k in steps:
            links.arrived((kind, way, k), region(kind, here.behind(k, True), part), here.sib_dev)

    low = low_lanes(share)
    for pair in range(heads // 2):
        tiles = [proj_ref[:, slice(b * width + pair * LANES, b * width + (pair + 1) * LANES)] for b in range(6)]
        turned = [swap_halves(tile) for tile in tiles]
        for odd in range(2):
            for b in range(3):
                left, right = (turned[2 * b], tiles[2 * b + 1]) if odd else (tiles[2 * b], turned[2 * b + 1])
                at = (2 * pair + odd) * GROUP + b * LANES
                a_full[spot(me * share, share, 16), at : at + LANES] = jnp.where(low, left, right).astype(BF16)
    v_all[me] = jnp.zeros_like(v_all[me])
    v_all[me, 0 : vec_ref.shape[0], 0 : vec_ref.shape[1]] = vec_ref[...].astype(BF16)

    here.greet()
    for k in steps:
        send_z("a", k)
        links.start(("v", "z", k), v_all.at[me], v_all.at[me], here.z_dev(k))
    send_own("v")
    send_own("a")

    inner = w1_ref.shape[1]
    e_own[:, 0:inner] = w1_ref[...].astype(BF16)
    e_own[:, inner : inner + width] = wo_ref[...].astype(BF16)
    e_own[:, inner + width :] = jnp.zeros((share, e_own.shape[1] - inner - width), BF16)
    w2_own[...] = w2_ref[...].astype(BF16)
    copy_e = pltpu.make_async_copy(e_own, whole("e", me), local.at[0])
    copy_w = pltpu.make_async_copy(w2_own, whole("w", me), local.at[1])
    copy_e.start()
    copy_w.start()

    length = seg_ref.shape[1]
    lane = lax.broadcasted_iota(jnp.int32, (length, LANES), 1)
    for seq in range(seg_ref.shape[0]):
        at = slice(seq * length, (seq + 1) * length)
        segment, kind = (
            jnp.transpose(jnp.broadcast_to(ref[seq : seq + 1, :].astype(F32), (LANES, length)))
            for ref in (seg_ref, type_ref)
        )
        same = segment == lane.astype(F32)
        word = jnp.where(kind == 0.0, 1.0, 0.0)
        word_ref[at] = word.astype(BF16)
        km_ref[at] = jnp.where(lane < HEAD, word, 1.0 - word).astype(BF16)
        qa_ref[at] = jnp.where(same & (lane < 8), 1.0, 0.0).astype(BF16)
        ka_ref[at] = jnp.where(
            lane < 8, jnp.where(same, 0.0, FAR), jnp.where(lane < 11, 1.0, 0.0)
        ).astype(BF16)

    for k in steps:
        pass_z("a", k)
        send_z("e", k)
        owner = here.behind(k)
        links.arrived(("v", "z", k), v_all.at[owner], here.z_dev(k))
        links.start(("v", "sz", k), v_all.at[owner], v_all.at[owner], here.sib_dev)
    for k in steps:
        pass_xy("a", k)
    send_own("e")
    send_own("w")

    links.arrived(("v", "o"), v_all.at[here.sib], here.sib_dev)
    for k in steps:
        owner = here.behind(k, True)
        links.arrived(("v", "sz", k), v_all.at[owner], here.sib_dev)
    span = vec_ref.shape[1]
    vec_out[...] = jnp.concatenate([v_all[n].astype(F32)[:, 0:span] for n in range(narrow)], axis=1)
    low1 = low_lanes(1)
    for head in range(heads):
        cols = slice((head // 2) * LANES, (head // 2 + 1) * LANES)
        row = [vec_out[r : r + 1, cols] for r in range(4)] + [jnp.zeros((1, LANES), F32), vec_out[4:5, cols]]
        for b in range(3):
            left, right = row[2 * b], row[2 * b + 1]
            left, right = (swap_halves(left), right) if head % 2 else (left, swap_halves(right))
            at = head * GROUP + b * LANES
            bias[0:1, at : at + LANES] = jnp.where(low1, left, right)

    links.arrived(("a", "o"), whole("a", here.sib), here.sib_dev)
    outs = []

    def project(index, part):
        size = 256
        cols = spot(part * quarter, quarter, LANES)
        add = bias[0:1, cols]

        def tile(i, carry):
            at = spot(i * size, size, size)
            prod = mm(x_ref[at, :], a_full[:, cols])
            word = word_ref[at, :] > 0
            for head in range(quarter // GROUP):
                group = slice(head * GROUP, (head + 1) * GROUP)
                out = slice(head * LANES, (head + 1) * LANES)
                query, keyval = qkv_tile(prod[:, group], add[:, group], word)
                q_s[part, at, out] = query
                kv_s[part, at, out] = keyval
            return carry

        lax.fori_loop(0, rows // size, tile, 0)
        wide = q_s.shape[2]
        for number, (source, target) in enumerate(((q_s, q_out), (kv_s, kv_out))):
            copy = pltpu.make_async_copy(
                source.at[part], target.at[:, spot(part * wide, wide, LANES)], local.at[2 + 2 * index + number]
            )
            copy.start()
            outs.append(copy)

    from_sib("a", "sz", here.wide)
    project(0, here.wide)
    for k in steps:
        pass_z("e", k)
        send_z("w", k)
    for k in steps:
        pass_d("a", k)
    from_sib("a", "sx", here.x_quarter)
    project(1, here.x_quarter)
    for k in steps:
        pass_xy("e", k)
    from_sib("a", "sy", here.y_quarter)
    project(2, here.y_quarter)
    from_sib("a", "sd", here.d_quarter)
    project(3, here.d_quarter)
    copy_a = pltpu.make_async_copy(a_full, a_out, local.at[10])
    copy_a.start()
    low_seq = low_lanes(length)
    per = quarter // GROUP

    def attend(pair):
        for seq in range(seg_ref.shape[0]):
            at = slice(seq * length, (seq + 1) * length)
            contexts = []
            for head in (2 * pair, 2 * pair + 1):
                cols = slice(head % per * LANES, (head % per + 1) * LANES)
                context, extra = attend_head(
                    q_s[head // per, at, cols], kv_s[head // per, at, cols], qa_ref[at], ka_ref[at], km_ref[at]
                )
                aug_s[at, head * LANES : (head + 1) * LANES] = extra
                contexts.append(context)
            both = jnp.where(low_seq, swap_halves(contexts[0]), contexts[1])
            ctx_s[at, pair * LANES : (pair + 1) * LANES] = both.astype(BF16)
        for number, (source, target, wide) in enumerate(((ctx_s, ctx_out, LANES), (aug_s, aug_out, 2 * LANES))):
            cols = slice(pair * wide, (pair + 1) * wide)
            copy = pltpu.make_async_copy(source.at[:, cols], target.at[:, cols], local.at[11 + 2 * pair + number])
            copy.start()
            outs.append(copy)

    between = [
        lambda: [pass_z("w", k) for k in steps],
        lambda: [pass_d("e", k) for k in steps],
        lambda: [pass_xy("w", k) for k in steps],
        lambda: [pass_d("w", k) for k in steps],
    ]
    for pair in range(heads // 2):
        attend(pair)
        if pair < len(between):
            between[pair]()
    for later in between[heads // 2 :]:
        later()
    for kind in ("e", "w"):
        links.arrived((kind, "o"), whole(kind, here.sib), here.sib_dev)
        for way, part in (("sz", here.wide), ("sx", here.x_quarter), ("sy", here.y_quarter), ("sd", here.d_quarter)):
            from_sib(kind, way, part)
    links.finish()
    for copy in (copy_e, copy_w, copy_a, *outs):
        copy.wait()


def gather_call(narrow, x, proj, wo, w1, w2, vec, segments, types):
    rows, width = x.shape
    share, deep, inner = proj.shape[0], w2.shape[0], w1.shape[1]
    ecols = inner + width + 2 * LANES
    heads = width // HEAD
    depth = narrow // 2
    count = 3 * (1 + 9 * (depth - 1)) + 1 + 2 * (depth - 1)
    vmem = pl.BlockSpec(memory_space=pltpu.VMEM)
    hbm = pl.BlockSpec(memory_space=pl.ANY)
    shape = jax.ShapeDtypeStruct
    part = heads // 4 * LANES
    return pl.pallas_call(
        functools.partial(gather_kernel, narrow),
        in_specs=[vmem] * 8,
        out_specs=[hbm] * 7 + [vmem] * 4,
        out_shape=[
            shape((rows, heads * LANES), BF16),
            shape((rows, heads * LANES), BF16),
            shape((rows, width), BF16),
            shape((rows, heads * LANES), BF16),
            shape((width, proj.shape[1]), BF16),
            shape((width, ecols), BF16),
            shape((deep * narrow, width), BF16),
            shape((16, width), F32),
            shape((rows, LANES), BF16),
            shape((rows, LANES), BF16),
            shape((rows, LANES), BF16),
        ],
        scratch_shapes=[
            pltpu.VMEM((width, proj.shape[1]), BF16),
            pltpu.VMEM((share, ecols), BF16),
            pltpu.VMEM((deep, width), BF16),
            pltpu.VMEM((narrow, 16, LANES), BF16),
            pltpu.VMEM((8, proj.shape[1]), F32),
            pltpu.VMEM((4, rows, part), BF16),
            pltpu.VMEM((4, rows, part), BF16),
            pltpu.VMEM((rows, width), BF16),
            pltpu.VMEM((rows, heads * LANES), BF16),
            pltpu.VMEM((rows, LANES), BF16),
            pltpu.SemaphoreType.DMA((count,)),
            pltpu.SemaphoreType.DMA((count,)),
            pltpu.SemaphoreType.DMA((11 + heads,)),
        ],
        compiler_params=pltpu.CompilerParams(
            vmem_limit_bytes=VMEM_LIMIT, collective_id=0, has_side_effects=True
        ),
        name="gather",
    )(x, proj, wo, w1, w2, vec, segments, types)


def key_pair(keyval, kmask, low):
    wide = keyval.astype(F32)
    return (jnp.where(low, wide, swap_halves(wide)) * kmask.astype(F32)).astype(BF16)


def attend_head(query, keyval, qaug, kaug, kmask):
    rows = query.shape[0]
    low = low_lanes(rows)
    lane = lax.broadcasted_iota(jnp.int32, (rows, LANES), 1)
    keys = jnp.concatenate([key_pair(keyval, kmask, low), kaug], axis=1)
    scores = mm_nt(jnp.concatenate([query, qaug], axis=1), keys)
    top = jnp.max(scores, axis=1, keepdims=True)
    weight = jnp.exp2((scores - top) * LOG2E).astype(BF16)
    ones_val = jnp.where(low, 1.0, keyval.astype(F32)).astype(BF16)
    both = mm(weight, ones_val)
    total = swap_halves(both)
    log_total = top + jnp.log(jnp.where(low, both, total))
    high, mid, rest = split_three(log_total)
    extra = jnp.where(lane == 8, -high, jnp.where(lane == 9, -mid, jnp.where(lane == 10, -rest, 0.0)))
    return both / total, jnp.where(lane < 8, qaug.astype(F32), extra).astype(BF16)


def attend_kernel(q_ref, kv_ref, qa_ref, ka_ref, km_ref, ctx_ref, aug_ref):
    outs = []
    for part in range(2):
        cols = slice(part * LANES, (part + 1) * LANES)
        out, aug_ref[:, cols] = attend_head(q_ref[:, cols], kv_ref[:, cols], qa_ref[...], ka_ref[...], km_ref[...])
        outs.append(out)
    ctx_ref[...] = jnp.where(low_lanes(q_ref.shape[0]), swap_halves(outs[0]), outs[1]).astype(BF16)


def attend_call(q, kv, qa, ka, km, length):
    rows, cols = q.shape
    seqs, steps = rows // length, cols // (2 * LANES)
    pair = pl.BlockSpec((length, 2 * LANES), lambda s, i: (s, i))
    one = pl.BlockSpec((length, LANES), lambda s, i: (s, 0))
    return pl.pallas_call(
        attend_kernel,
        grid=(seqs, steps),
        in_specs=[pair, pair, one, one, one],
        out_specs=[pl.BlockSpec((length, LANES), lambda s, i: (s, i)), pair],
        out_shape=[
            jax.ShapeDtypeStruct((rows, cols // 2), BF16),
            jax.ShapeDtypeStruct((rows, cols), BF16),
        ],
        compiler_params=pltpu.CompilerParams(vmem_limit_bytes=VMEM_LIMIT),
        name="attend",
    )(q, kv, qa, ka, km)


def attend_back_head(query, keyval, aug, gcon, con, kaug, kmask, word, odd, low, lane):
    keys = key_pair(keyval, kmask, low)
    scores_t = mm_nt(jnp.concatenate([keys, kaug], axis=1), jnp.concatenate([query, aug], axis=1))
    probs_t = jnp.exp2(scores_t * LOG2E)
    gwide = gcon.astype(F32)
    prod = gwide * con.astype(F32)
    mine = low != odd
    delta = jnp.sum(jnp.where(mine, prod, 0.0), axis=1, keepdims=True)
    high, mid, rest = split_three(delta)
    extra = jnp.where(lane == 0, -high, jnp.where(lane == 1, -mid, jnp.where(lane == 2, -rest, 0.0)))
    ghead = jnp.where(low, extra, jnp.where(odd, gwide, swap_halves(gwide))).astype(BF16)
    ones_val = jnp.where(low, jnp.where(lane < 3, 1.0, 0.0), keyval.astype(F32)).astype(BF16)
    gscores_t = (probs_t * mm_nt(ones_val, ghead)).astype(BF16)
    gval = mm(probs_t.astype(BF16), ghead)
    gkey = mm(gscores_t, query)
    gquery = (jnp.transpose(mm_tn(keys, gscores_t)) * (HEAD**-0.5)).astype(BF16)
    zero = jnp.zeros_like(gquery)
    gkey = jnp.where(kmask.astype(F32) > 0, gkey, 0.0)
    gkey = gkey + swap_halves(gkey)
    return (
        jnp.where(word, gquery, zero),
        jnp.where(word, zero, gquery),
        jnp.where(low, gkey, gval).astype(BF16),
    )


def attend_back_kernel(
    length, x_ref, q_ref, kv_ref, aug_ref, gc_ref, ctx_ref, ka_ref, km_ref, word_ref, gp_ref, gw_ref, sum_ref, xt
):
    step = pl.program_id(0)
    rows = x_ref.shape[0]

    @pl.when(step == 0)
    def _():
        xt[...] = jnp.transpose(x_ref[...])

    low = low_lanes(length)
    lane = lax.broadcasted_iota(jnp.int32, (length, LANES), 1)
    odd = lax.rem(step, 2) == 1
    for seq in range(rows // length):
        here = slice(seq * length, (seq + 1) * length)
        tiles = attend_back_head(
            q_ref[here], kv_ref[here], aug_ref[here], gc_ref[here], ctx_ref[here],
            ka_ref[here], km_ref[here], word_ref[here] > 0, odd, low, lane,
        )
        for index, tile in enumerate(tiles):
            gp_ref[here, index * LANES : (index + 1) * LANES] = tile
    grads = gp_ref[...]
    gw_ref[...] = mm(xt[...], grads).astype(BF16)
    sums = jnp.sum(grads.astype(F32).reshape(rows // 8, 8, GROUP), axis=0)
    sum_ref[...] = jnp.sum(sums, axis=0, keepdims=True)


def attend_back_call(x, q, kv, aug, gc, ctx, ka, km, word, length):
    rows, width = x.shape
    heads = q.shape[1] // LANES
    head = pl.BlockSpec((rows, LANES), lambda h: (0, h))
    pair = pl.BlockSpec((rows, LANES), lambda h: (0, h // 2))
    one = pl.BlockSpec((rows, LANES), lambda h: (0, 0))
    return pl.pallas_call(
        functools.partial(attend_back_kernel, length),
        grid=(heads,),
        in_specs=[pl.BlockSpec((rows, width), lambda h: (0, 0)), head, head, head, pair, pair, one, one, one],
        out_specs=[
            pl.BlockSpec((rows, GROUP), lambda h: (0, h)),
            pl.BlockSpec((width, GROUP), lambda h: (0, h)),
            pl.BlockSpec((1, GROUP), lambda h: (0, h)),
        ],
        out_shape=[
            jax.ShapeDtypeStruct((rows, heads * GROUP), BF16),
            jax.ShapeDtypeStruct((width, heads * GROUP), BF16),
            jax.ShapeDtypeStruct((1, heads * GROUP), F32),
        ],
        scratch_shapes=[pltpu.VMEM((width, rows), BF16)],
        compiler_params=pltpu.CompilerParams(vmem_limit_bytes=VMEM_LIMIT),
        name="attend_back",
    )(x, q, kv, aug, gc, ctx, ka, km, word)


class Chunk:
    def __init__(self, name, refs, by_rows):
        self.name = name
        self.total, self.r1a, self.r1b, self.r2a, self.r2b, self.rz, self.final = refs
        self.by_rows = by_rows
        _, self.rows, self.cols = self.total.shape

    def cut(self, part, side=None):
        if self.by_rows:
            size = self.rows // 4
            if side is None:
                return spot(part * size, size, 16), slice(None)
            return spot(part * size + side * (size // 2), size // 2, 16), slice(None)
        size, half = self.cols // 4, self.rows // 2
        rows = slice(0, self.rows) if side is None else slice(side * half, (side + 1) * half)
        return rows, spot(part * size, size, LANES)


def chunk_scratch(depth, rows, cols, by_rows):
    if by_rows:
        piece, half = (rows // 4, cols), (rows // 8, cols)
    else:
        piece, half = (rows, cols // 4), (rows // 2, cols // 4)
    return [
        pltpu.VMEM((depth, rows, cols), BF16),
        pltpu.VMEM((2, depth, *half), BF16),
        pltpu.VMEM((2, depth, *half), BF16),
        pltpu.VMEM((depth, *half), BF16),
        pltpu.VMEM((depth, *half), BF16),
        pltpu.VMEM((depth - 1, *piece), BF16),
        pltpu.VMEM((rows, cols), BF16),
    ]


class Reducer:
    def __init__(self, here, send, recv):
        self.here = here
        self.links = Links(send, recv)
        self.sent = []

    def send(self, key, build):
        copy = self.links.copy(key, *build())
        copy.start()
        self.sent.append((key, build))

    def arrived(self, key, dst, device):
        self.links.arrived(key, dst, device)

    def finish(self):
        for key, build in self.sent:
            self.links.copy(key, *build()).wait_send()

    def pair_send(self, chunk, sources):
        here = self.here
        for z in range(here.depth):
            for part, (_, cols) in enumerate(sources(0)):

                def build(z=z, part=part, cols=cols):
                    owner = 2 * z + 1 - here.core
                    return sources(owner)[part][0], chunk.total.at[z, :, cols], here.sib_dev

                self.send((chunk.name, "s", z, part), build)

    def pair_wait(self, chunk, sources):
        for z in range(self.here.depth):
            for part, (_, cols) in enumerate(sources(0)):
                self.arrived((chunk.name, "s", z, part), chunk.total.at[z, :, cols], self.here.sib_dev)

    def plane_send(self, chunk):
        here = self.here
        for index, (a, b) in enumerate(((here.x_quarter, here.y_quarter), (here.d_quarter, here.d_quarter))):

            def first(index=index, part=a):
                rows, cols = chunk.cut(part, 0)
                return chunk.total.at[:, rows, cols], chunk.r1a.at[index], here.x_dev

            def second(index=index, part=b):
                rows, cols = chunk.cut(part, 1)
                return chunk.total.at[:, rows, cols], chunk.r1b.at[index], here.y_dev

            self.send((chunk.name, "1a", index), first)
            self.send((chunk.name, "1b", index), second)

    def add(self, chunk, part, side, value):
        rows, cols = chunk.cut(part, side)
        chunk.total[:, rows, cols] = chunk.total[:, rows, cols] + value

    def plane_turn(self, chunk):
        here = self.here
        for index in range(2):
            self.arrived((chunk.name, "1a", index), chunk.r1a.at[index], here.x_dev)
            self.arrived((chunk.name, "1b", index), chunk.r1b.at[index], here.y_dev)
        self.add(chunk, here.y_quarter, 0, chunk.r1a[1])
        self.add(chunk, here.x_quarter, 1, chunk.r1b[1])

        def first():
            rows, cols = chunk.cut(here.y_quarter, 0)
            return chunk.total.at[:, rows, cols], chunk.r2a, here.y_dev

        def second():
            rows, cols = chunk.cut(here.x_quarter, 1)
            return chunk.total.at[:, rows, cols], chunk.r2b, here.x_dev

        self.send((chunk.name, "2a"), first)
        self.send((chunk.name, "2b"), second)
        self.add(chunk, here.wide, 0, chunk.r1a[0])
        self.add(chunk, here.wide, 1, chunk.r1b[0])

    def depth_send(self, chunk):
        here = self.here
        self.arrived((chunk.name, "2a"), chunk.r2a, here.y_dev)
        self.arrived((chunk.name, "2b"), chunk.r2b, here.x_dev)
        self.add(chunk, here.wide, 0, chunk.r2a[...])
        self.add(chunk, here.wide, 1, chunk.r2b[...])
        for k in range(1, here.depth):

            def build(k=k):
                rows, cols = chunk.cut(here.wide)
                return chunk.total.at[lax.rem(here.z + k, here.depth), rows, cols], chunk.rz.at[k - 1], here.z_dev(k)

            self.send((chunk.name, "z", k), build)

    def share_send(self, chunk):
        here = self.here
        for k in range(1, here.depth):
            self.arrived((chunk.name, "z", k), chunk.rz.at[k - 1], here.z_dev(k))
        rows, cols = chunk.cut(here.wide)
        done = chunk.total[here.z, rows, cols].astype(F32)
        for k in range(1, here.depth):
            done = done + chunk.rz[k - 1].astype(F32)
        chunk.final[rows, cols] = done.astype(BF16)

        def build(device):
            rows, cols = chunk.cut(here.wide)
            return chunk.final.at[rows, cols], chunk.final.at[rows, cols], device

        self.send((chunk.name, "fx"), lambda: build(here.x_dev))
        self.send((chunk.name, "fy"), lambda: build(here.y_dev))

    def share_pass(self, chunk):
        here = self.here

        def part(quarter, side, device):
            rows, cols = chunk.cut(quarter, side)
            return chunk.final.at[rows, cols], chunk.final.at[rows, cols], device

        self.arrived((chunk.name, "fx"), *part(here.x_quarter, None, here.x_dev)[1:])
        self.send((chunk.name, "fdy"), lambda: part(here.x_quarter, 0, here.y_dev))
        self.arrived((chunk.name, "fy"), *part(here.y_quarter, None, here.y_dev)[1:])
        self.send((chunk.name, "fdx"), lambda: part(here.y_quarter, 1, here.x_dev))

    def share_wait(self, chunk):
        here = self.here
        for key, side, device in (("fdy", 0, here.y_dev), ("fdx", 1, here.x_dev)):
            rows, cols = chunk.cut(here.d_quarter, side)
            self.arrived((chunk.name, key), chunk.final.at[rows, cols], device)


CHUNK_HEADS = 4


def squares(ref, cols):
    total = jnp.zeros((8, LANES), F32)
    rows = ref.shape[0]
    for start in range(0, cols, LANES):
        tile = ref[:, start : start + LANES].astype(F32)
        total = total + jnp.sum((tile * tile).reshape(rows // 8, 8, LANES), axis=0)
    return total


def reduce_kernel(
    narrow, length, groups,
    x_ref, q_ref, kv_ref, aug_ref, gc_ref, ctx_ref, wp_ref, ka_ref, km_ref, word_ref, gvec_ref,
    gr1_ref, gw1_ref, gwo_ref, gw2_ref,
    ig_ref, fw_ref, fe_ref, fa_ref, v_ref, n_ref,
    xt, gw, gp_ref, ig, *scratch,
):
    step = pl.program_id(0)
    rows, width = x_ref.shape
    heads = groups * CHUNK_HEADS
    inner = gw1_ref.shape[1]
    here = Place(narrow)
    scratch = list(scratch)
    chunk_w = Chunk("w", scratch[0:7], True)
    chunk_e = Chunk("e", scratch[7:14], False)
    chunk_a = [Chunk(("a", j), scratch[14 + 7 * j : 21 + 7 * j], False) for j in range(groups)]
    own_w, own_e, v0, v1, v2, vs, vx, vy, vz, n0, ns, nz, send, recv, local = scratch[14 + 7 * groups :]
    red = Reducer(here, send, recv)
    share, deep = chunk_e.rows, chunk_w.rows

    def sources_w(owner):
        return [(gw2_ref.at[spot(owner * deep, deep, 16), :], slice(0, width))]

    def sources_e(owner):
        at = spot(owner * share, share, 16)
        return [(gw1_ref.at[at, :], slice(0, inner)), (gwo_ref.at[at, :], slice(inner, inner + width))]

    def sources_a(j):
        return lambda owner: [(gw.at[j, spot(owner * share, share, 16), :], slice(0, CHUNK_HEADS * GROUP))]

    def own_copies():
        copies = []
        for own, sources in ((own_w, sources_w), (own_e, sources_e)):
            for z in range(here.depth):
                for source, cols in sources(2 * z + here.core):
                    copies.append(pltpu.make_async_copy(source, own.at[z, :, cols], local.at[len(copies)]))
        return copies

    def out_copies():
        copies = [(chunk_w.final, fw_ref), (chunk_e.final, fe_ref)]
        wide = CHUNK_HEADS * GROUP
        copies += [(chunk.final, fa_ref.at[:, j * wide : (j + 1) * wide]) for j, chunk in enumerate(chunk_a)]
        base = 3 * here.depth
        return [pltpu.make_async_copy(a, b, local.at[base + i]) for i, (a, b) in enumerate(copies)]

    def copy_ig():
        return pltpu.make_async_copy(gr1_ref, ig, local.at[3 * here.depth + 2 + groups])

    def merge(chunk, own):
        def one(z, carry):
            chunk.total[z] = chunk.total[z] + own(z)
            return carry

        lax.fori_loop(0, here.depth, one, 0)

    def own_a(j):
        return lambda z: gw[j, spot((2 * z + here.core) * share, share, 16), :]

    @pl.when(step == 0)
    def _():
        for copy in own_copies():
            copy.start()
        copy_ig().start()
        here.greet()
        red.pair_send(chunk_w, sources_w)
        red.pair_send(chunk_e, sources_e)
        pad = chunk_e.cols - inner - width
        chunk_e.total[:, :, inner + width :] = jnp.zeros((here.depth, share, pad), BF16)
        own_e[:, :, inner + width :] = jnp.zeros((here.depth, share, pad), BF16)
        xt[...] = jnp.transpose(x_ref[...])
        v0[...] = gvec_ref[...]

    def advance(at, action):
        pl.when(step == at)(action)

    def act_w1():
        for copy in own_copies():
            copy.wait()
        red.pair_wait(chunk_w, sources_w)
        merge(chunk_w, lambda z: own_w[z])
        red.plane_send(chunk_w)

    def act_e1():
        red.pair_wait(chunk_e, sources_e)
        merge(chunk_e, lambda z: own_e[z])
        red.plane_send(chunk_e)

    def act_a1(j):
        red.pair_wait(chunk_a[j], sources_a(j))
        merge(chunk_a[j], own_a(j))
        red.plane_send(chunk_a[j])

    advance(1, act_w1)
    advance(2, act_e1)
    advance(4, lambda: red.plane_turn(chunk_w))
    advance(5, lambda: act_a1(0))
    advance(6, lambda: red.depth_send(chunk_w))
    advance(8, lambda: red.plane_turn(chunk_e))
    advance(9, lambda: act_a1(1))
    advance(10, lambda: red.depth_send(chunk_e))
    advance(11, lambda: red.share_send(chunk_w))

    low = low_lanes(length)
    lane = lax.broadcasted_iota(jnp.int32, (length, LANES), 1)
    odd = lax.rem(step, 2) == 1
    for seq in range(rows // length):
        at = slice(seq * length, (seq + 1) * length)
        tiles = attend_back_head(
            q_ref[at], kv_ref[at], aug_ref[at], gc_ref[at], ctx_ref[at],
            ka_ref[at], km_ref[at], word_ref[at] > 0, odd, low, lane,
        )
        for index, tile in enumerate(tiles):
            gp_ref[at, index * LANES : (index + 1) * LANES] = tile
    grads = gp_ref[...]
    group, inside = step // CHUNK_HEADS, lax.rem(step, CHUNK_HEADS)
    gw[group, :, spot(inside * GROUP, GROUP, LANES)] = mm(xt[...], grads).astype(BF16)
    sums = jnp.sum(jnp.sum(grads.astype(F32).reshape(rows // 8, 8, GROUP), axis=0), axis=0, keepdims=True)

    @pl.when(step == 0)
    def _():
        copy_ig().wait()

    ig[...] += mm_nt(grads, wp_ref[...])

    low1 = low_lanes(1)
    pair = spot(step // 2 * LANES, LANES, LANES)
    mine = low1 != odd
    for b in range(3):
        tile = sums[:, b * LANES : (b + 1) * LANES]
        turned = swap_halves(tile)
        first = jnp.where(odd, turned, tile)
        second = jnp.where(odd, tile, turned)
        if b < 2:
            v0[2 * b : 2 * b + 1, pair] = jnp.where(mine, first, v0[2 * b : 2 * b + 1, pair])
            v0[2 * b + 1 : 2 * b + 2, pair] = jnp.where(mine, second, v0[2 * b + 1 : 2 * b + 2, pair])
        else:
            v0[4:5, pair] = jnp.where(mine, second, v0[4:5, pair])

    for j in range(groups):
        advance((j + 1) * CHUNK_HEADS - 1, lambda j=j: red.pair_send(chunk_a[j], sources_a(j)))

    @pl.when(step == heads - 1)
    def _():
        ig_ref[...] = ig[...].astype(BF16)
        last = chunk_a[-1]
        red.send(("v", "s"), lambda: (v0, vs, here.sib_dev))
        red.plane_turn(chunk_a[0])
        red.share_send(chunk_e)
        red.share_pass(chunk_w)
        act_a1(groups - 1)
        red.arrived(("v", "s"), vs, here.sib_dev)
        v1[...] = v0[...] + vs[...]
        red.send(("v", "x"), lambda: (v1, vx, here.x_dev))
        red.depth_send(chunk_a[0])
        for chunk in chunk_a[1:-1]:
            red.plane_turn(chunk)
        red.share_pass(chunk_e)
        for chunk in chunk_a[1:-1]:
            red.depth_send(chunk)
        red.plane_turn(last)
        red.arrived(("v", "x"), vx, here.x_dev)
        v2[...] = v1[...] + vx[...]
        red.send(("v", "y"), lambda: (v2, vy, here.y_dev))
        for chunk in chunk_a[:-1]:
            red.share_send(chunk)
        red.depth_send(last)
        red.arrived(("v", "y"), vy, here.y_dev)
        vz[here.z] = v2[...] + vy[...]
        for k in range(1, here.depth):
            red.send(("v", "z", k), lambda k=k: (vz.at[here.z], vz.at[here.z], here.z_dev(k)))
        red.share_wait(chunk_w)
        red.share_wait(chunk_e)
        for chunk in chunk_a[:-1]:
            red.share_pass(chunk)
        norm = squares(chunk_w.final, width) + squares(chunk_e.final, inner + width)
        for chunk in chunk_a[:-1]:
            red.share_wait(chunk)
            norm = norm + squares(chunk.final, chunk.cols)
        red.share_send(last)
        for k in range(1, here.depth):
            source = here.behind(k) // 2
            red.arrived(("v", "z", k), vz.at[source], here.z_dev(k))
        vec = vz[0]
        for z in range(1, here.depth):
            vec = vec + vz[z]
        v_ref[...] = vec
        red.share_pass(last)
        red.share_wait(last)
        for copy in out_copies():
            copy.start()
        n0[...] = norm + squares(last.final, last.cols)
        red.send(("n", "s"), lambda: (n0, ns, here.sib_dev))
        red.arrived(("n", "s"), ns, here.sib_dev)
        nz[here.z] = n0[...] + ns[...]
        for k in range(1, here.depth):
            red.send(("n", "z", k), lambda k=k: (nz.at[here.z], nz.at[here.z], here.z_dev(k)))
        for k in range(1, here.depth):
            source = here.behind(k) // 2
            red.arrived(("n", "z", k), nz.at[source], here.z_dev(k))
        total = nz[0]
        for z in range(1, here.depth):
            total = total + nz[z]
        every = jnp.sum(jnp.sum(total, axis=0, keepdims=True), axis=1, keepdims=True)
        square = jnp.sum(jnp.sum(vec * vec, axis=0, keepdims=True), axis=1, keepdims=True)
        n_ref[...] = jnp.broadcast_to(every + square, n_ref.shape)
        red.finish()
        for copy in out_copies():
            copy.wait()


def reduce_call(narrow, x, q, kv, aug, gc, ctx, wp, ka, km, word, gvec, gr1, gw1, gwo, gw2, length):
    rows, width = x.shape
    inner = gw2.shape[0]
    heads = q.shape[1] // LANES
    groups = heads // CHUNK_HEADS
    depth = narrow // 2
    share, deep, ecols, acols = width // narrow, inner // narrow, inner + width + 2 * LANES, CHUNK_HEADS * GROUP
    head = pl.BlockSpec((rows, LANES), lambda h: (0, h))
    pair = pl.BlockSpec((rows, LANES), lambda h: (0, h // 2))
    one = pl.BlockSpec((rows, LANES), lambda h: (0, 0), pipeline_mode=pl.Buffered(1))
    hbm = pl.BlockSpec(memory_space=pl.ANY)
    shape = jax.ShapeDtypeStruct
    vec = pltpu.VMEM((16, width), F32)
    tile = pltpu.VMEM((8, LANES), F32)
    scratch = [pltpu.VMEM((width, rows), BF16), pltpu.VMEM((groups, width, acols), BF16)]
    scratch += [pltpu.VMEM((rows, GROUP), BF16), pltpu.VMEM((rows, width), F32)]
    scratch += chunk_scratch(depth, deep, width, True)
    scratch += chunk_scratch(depth, share, ecols, False)
    for _ in range(groups):
        scratch += chunk_scratch(depth, share, acols, False)
    scratch += [pltpu.VMEM((depth, deep, width), BF16), pltpu.VMEM((depth, share, ecols), BF16)]
    scratch += [vec] * 6 + [pltpu.VMEM((depth, 16, width), F32), tile, tile, pltpu.VMEM((depth, 8, LANES), F32)]
    count = (2 + groups) * (depth + 10 + depth - 1) + depth + 2 * (3 + depth)
    scratch += [pltpu.SemaphoreType.DMA((count,))] * 2 + [pltpu.SemaphoreType.DMA((3 * depth + 3 + groups,))]
    return pl.pallas_call(
        functools.partial(reduce_kernel, narrow, length, groups),
        grid=(heads,),
        in_specs=[
            pl.BlockSpec((rows, width), lambda h: (0, 0), pipeline_mode=pl.Buffered(1)),
            head, head, head, pair, pair, pl.BlockSpec((width, GROUP), lambda h: (0, h)), one, one, one,
            pl.BlockSpec((16, width), lambda h: (0, 0), pipeline_mode=pl.Buffered(1)),
            hbm, hbm, hbm, hbm,
        ],
        out_specs=[
            pl.BlockSpec((rows, width), lambda h: (0, 0), pipeline_mode=pl.Buffered(1)),
            hbm, hbm, hbm,
            pl.BlockSpec((16, width), lambda h: (0, 0)),
            pl.BlockSpec((8, LANES), lambda h: (0, 0)),
        ],
        out_shape=[
            shape((rows, width), BF16),
            shape((deep, width), BF16),
            shape((share, ecols), BF16),
            shape((share, heads * GROUP), BF16),
            shape((16, width), F32),
            shape((8, LANES), F32),
        ],
        scratch_shapes=scratch,
        compiler_params=pltpu.CompilerParams(
            vmem_limit_bytes=VMEM_LIMIT, collective_id=1, has_side_effects=True
        ),
        name="reduce",
    )(x, q, kv, aug, gc, ctx, wp, ka, km, word, gvec, gr1, gw1, gwo, gw2)


def gelu_pair(pre):
    size = jnp.abs(pre) * (0.5**0.5)
    bell = jnp.exp2(pre * pre * (-0.5 * LOG2E))
    t = 1.0 / (1.0 + 0.3275911 * size)
    poly = t * (0.254829592 + t * (-0.284496736 + t * (1.421413741 + t * (-1.453152027 + t * 1.061405429))))
    tail = 0.5 * poly * bell
    share = jnp.where(pre >= 0, 1.0 - tail, tail)
    return pre * share, share + pre * bell * 0.3989422804014327


def fold(array_in):
    rows, cols = array_in.shape
    return jnp.sum(array_in.reshape(rows // 8, 8, cols), axis=0)


def middle_kernel(
    tiles, x_ref, ctx_ref, cot_ref, vec_ref, e_hbm, w2_hbm,
    out_ref, gr1_ref, gctx_ref, gw2_ref, gw1_ref, gwo_ref, gvec_ref,
    wo, w1, w2, h1_s, act_s, gb_s, gp_s, ga_s, ctx_s, dg_s, acc, sems,
):
    step = pl.program_id(0)
    size, width = x_ref.shape
    inner = w1.shape[1]
    chunks = inner // width

    def weight_copies(index):
        source, target = (
            (e_hbm.at[:, inner : inner + width], wo),
            (e_hbm.at[:, 0:inner], w1),
            (w2_hbm, w2),
        )[index]
        return pltpu.make_async_copy(source, target, sems.at[index])

    @pl.when(step == 0)
    def _():
        for index in range(3):
            weight_copies(index).start()
        acc[...] = jnp.zeros_like(acc)

    def vec(row):
        return vec_ref[row : row + 1, :].astype(F32)

    @pl.when(step < tiles)
    def _():
        here = pl.ds(pl.multiple_of(step * size, size), size)

        @pl.when(step == 0)
        def _():
            weight_copies(0).wait()

        ctx_s[here, :] = ctx_ref[...]
        resid = x_ref[...].astype(F32) + mm(ctx_ref[...], wo[...]) + vec(5)
        center = resid - jnp.mean(resid, axis=1, keepdims=True)
        inv1 = lax.rsqrt(jnp.mean(center * center, axis=1, keepdims=True) + norm_eps)
        n1 = center * inv1
        h1 = n1 * vec(6) + vec(7)
        h1b = h1.astype(BF16)
        h1_s[here, :] = h1b

        @pl.when(step == 0)
        def _():
            weight_copies(1).wait()
            weight_copies(2).wait()

        branch = h1 + vec(8)
        for c in range(chunks):
            cols = slice(c * width, (c + 1) * width)
            act, slope = gelu_pair(mm(h1b, w1[:, cols]) + vec(11 + c))
            act = act.astype(BF16)
            act_s[here, cols] = act
            dg_s[:, cols] = slope
            branch = branch + mm(act, w2[cols, :])
        center = branch - jnp.mean(branch, axis=1, keepdims=True)
        inv2 = lax.rsqrt(jnp.mean(center * center, axis=1, keepdims=True) + norm_eps)
        n2 = center * inv2
        out_ref[...] = (n2 * vec(9) + vec(10)).astype(BF16)
        grad = cot_ref[...].astype(F32)
        gn = grad * n2
        acc[9] += fold(gn)
        acc[10] += fold(grad)
        scaled = grad * vec(9)
        gr2 = inv2 * (
            scaled
            - jnp.mean(scaled, axis=1, keepdims=True)
            - n2 * jnp.mean(scaled * n2, axis=1, keepdims=True)
        )
        gb = gr2.astype(BF16)
        gb_s[here, :] = gb
        acc[8] += fold(gb.astype(F32))
        gh1 = gr2
        for c in range(chunks):
            cols = slice(c * width, (c + 1) * width)
            gpre = (mm_nt(gb, w2[cols, :]) * dg_s[:, cols]).astype(BF16)
            gp_s[here, cols] = gpre
            acc[11 + c] += fold(gpre.astype(F32))
            gh1 = gh1 + mm_nt(gpre, w1[:, cols])
        acc[6] += fold(gh1 * n1)
        acc[7] += fold(gh1)
        scaled = gh1 * vec(6)
        gr1 = inv1 * (
            scaled
            - jnp.mean(scaled, axis=1, keepdims=True)
            - n1 * jnp.mean(scaled * n1, axis=1, keepdims=True)
        )
        gr1_ref[...] = gr1
        ga = gr1.astype(BF16)
        ga_s[here, :] = ga
        acc[5] += fold(ga.astype(F32))
        gctx_ref[...] = mm_nt(ga, wo[...]).astype(BF16)

    for c in range(chunks):
        cols = slice(c * width, (c + 1) * width)

        @pl.when(step == tiles + c)
        def _():
            gw2_ref[...] = mm_tn(act_s[:, cols], gb_s[...]).astype(BF16)

        @pl.when(step == tiles + chunks + c)
        def _():
            gw1_ref[...] = mm_tn(h1_s[...], gp_s[:, cols]).astype(BF16)

    @pl.when(step == tiles + 2 * chunks)
    def _():
        gwo_ref[...] = mm_tn(ctx_s[...], ga_s[...]).astype(BF16)
        for row in range(acc.shape[0]):
            gvec_ref[row : row + 1, :] = jnp.sum(acc[row], axis=0, keepdims=True)


def middle_call(x, ctx, cot, vec, e, w2, size):
    rows, width = x.shape
    inner = w2.shape[0]
    tiles, chunks = rows // size, inner // width
    tile = pl.BlockSpec((size, width), lambda i: (jnp.minimum(i, tiles - 1), 0))
    hbm = pl.BlockSpec(memory_space=pl.ANY)

    def after(start):
        return lambda i: jnp.clip(i - start, 0, chunks - 1)

    shape = jax.ShapeDtypeStruct
    return pl.pallas_call(
        functools.partial(middle_kernel, tiles),
        grid=(tiles + 2 * chunks + 1,),
        in_specs=[tile, tile, tile, pl.BlockSpec(vec.shape, lambda i: (0, 0)), hbm, hbm],
        out_specs=[
            tile,
            tile,
            tile,
            pl.BlockSpec((width, width), lambda i: (after(tiles)(i), 0)),
            pl.BlockSpec((width, width), lambda i: (0, after(tiles + chunks)(i))),
            pl.BlockSpec((width, width), lambda i: (0, 0)),
            pl.BlockSpec(vec.shape, lambda i: (0, 0)),
        ],
        out_shape=[
            shape((rows, width), BF16),
            shape((rows, width), F32),
            shape((rows, width), BF16),
            shape((inner, width), BF16),
            shape((width, inner), BF16),
            shape((width, width), BF16),
            shape(vec.shape, F32),
        ],
        scratch_shapes=[
            pltpu.VMEM((width, width), BF16),
            pltpu.VMEM((width, inner), BF16),
            pltpu.VMEM((inner, width), BF16),
            pltpu.VMEM((rows, width), BF16),
            pltpu.VMEM((rows, inner), BF16),
            pltpu.VMEM((rows, width), BF16),
            pltpu.VMEM((rows, inner), BF16),
            pltpu.VMEM((rows, width), BF16),
            pltpu.VMEM((rows, width), BF16),
            pltpu.VMEM((size, inner), F32),
            pltpu.VMEM((vec.shape[0], 8, width), F32),
            pltpu.SemaphoreType.DMA((3,)),
        ],
        compiler_params=pltpu.CompilerParams(vmem_limit_bytes=VMEM_LIMIT),
        name="middle",
    )(x, ctx, cot, vec, e, w2)


def input_grad_kernel(gp_ref, w_ref, gr1_ref, out_ref):
    out_ref[...] = (gr1_ref[...] + mm_nt(gp_ref[...], w_ref[...])).astype(BF16)


def input_grad_call(gp, w, gr1, size):
    rows, cols = gp.shape
    width = w.shape[0]
    return pl.pallas_call(
        input_grad_kernel,
        grid=(rows // size,),
        in_specs=[
            pl.BlockSpec((size, cols), lambda i: (i, 0)),
            pl.BlockSpec((width, cols), lambda i: (0, 0)),
            pl.BlockSpec((size, width), lambda i: (i, 0)),
        ],
        out_specs=pl.BlockSpec((size, width), lambda i: (i, 0)),
        out_shape=jax.ShapeDtypeStruct((rows, width), BF16),
        compiler_params=pltpu.CompilerParams(vmem_limit_bytes=VMEM_LIMIT),
        name="input_grad",
    )(gp, w, gr1)


def adam_update(master, first_old, second_old, grad_shard, factor, index):
    clipped = grad_shard * factor
    new_first = beta_one * first_old + (1.0 - beta_one) * clipped
    new_second = beta_two * second_old + (1.0 - beta_two) * clipped * clipped
    direction = (
        new_first
        / (1.0 - beta_one**STEP)
        / (jnp.sqrt(new_second / (1.0 - beta_two**STEP)) + adam_eps)
    )
    new_weight = master - rate_table[index] * (direction + decay_table[index] * master)
    return (new_weight, new_first, new_second)


def update_tile(master, first, second, grad, factor, index):
    weight, first, second = adam_update(master, first, second, grad.astype(F32), factor, index)
    return weight, first, second, weight.astype(BF16)


def update_kernel(narrow, n_ref, fa_ref, fe_ref, fw_ref, v_ref, *refs):
    ins, outs = refs[0:15], refs[15:35]
    heads = fa_ref.shape[1] // GROUP
    width = heads * HEAD
    norm = jnp.sqrt(n_ref[0:1, 0:1])
    factor = jnp.minimum(1.0, clip_limit / (norm + 1e-06))

    def store(index, rows, cols, grad):
        news = update_tile(*(ins[5 * t + index][rows, cols] for t in range(3)), grad, factor, index)
        for t, new in enumerate(news):
            outs[5 * t + index][rows, cols] = new

    every = slice(None)
    low = low_lanes(fa_ref.shape[0])
    for pair in range(heads // 2):
        at = 2 * pair * GROUP
        for b in range(3):
            even = fa_ref[:, at + b * LANES : at + (b + 1) * LANES].astype(F32)
            odd = fa_ref[:, at + GROUP + b * LANES : at + GROUP + (b + 1) * LANES].astype(F32)
            for second in range(2):
                if second:
                    grad = jnp.where(low, swap_halves(even), odd)
                else:
                    grad = jnp.where(low, even, swap_halves(odd))
                start = (2 * b + second) * width + pair * LANES
                store(0, every, slice(start, start + LANES), grad)
    inner = ins[2].shape[1]
    store(1, every, every, fe_ref[:, inner : inner + width])
    store(2, every, every, fe_ref[:, 0:inner])
    store(3, every, every, fw_ref[...])

    @pl.when(pl.program_id(0) == 0)
    def _():
        count, span = ins[4].shape
        me = lax.axis_index("narrow")
        turned = pltpu.roll(v_ref[...], lax.rem(width - me * span, width), 1)
        store(4, every, every, turned[0:count, 0:span])


def update_call(narrow, norm, fa, fe, fw, vec, masters, firsts, seconds):
    share = fa.shape[0]
    steps = share // 16

    def rows_of(array_in):
        return pl.BlockSpec((array_in.shape[0] // steps, array_in.shape[1]), lambda i: (i, 0))

    def fixed(array_in):
        return pl.BlockSpec(array_in.shape, lambda i: (0, 0))

    def group(arrays):
        return [rows_of(a) for a in arrays[:4]] + [fixed(arrays[4])]

    def shapes(arrays, dtype):
        return [jax.ShapeDtypeStruct(a.shape, dtype) for a in arrays]

    return pl.pallas_call(
        functools.partial(update_kernel, narrow),
        grid=(steps,),
        in_specs=[fixed(norm), rows_of(fa), rows_of(fe), rows_of(fw), fixed(vec)] + group(masters) * 3,
        out_specs=group(masters) * 4,
        out_shape=shapes(masters, F32) * 3 + shapes(masters, BF16),
        compiler_params=pltpu.CompilerParams(vmem_limit_bytes=VMEM_LIMIT),
        name="update",
    )(norm, fa, fe, fw, vec, *masters, *firsts, *seconds)


def by_head(array_in):
    rows, cols = array_in.shape
    heads = cols // GROUP
    return array_in.reshape(rows, 6, heads, HEAD).transpose(0, 2, 1, 3).reshape(rows, cols)


def by_block(array_in):
    rows, cols = array_in.shape
    heads = cols // GROUP
    return array_in.reshape(rows, heads, 6, HEAD).transpose(0, 2, 1, 3).reshape(rows, cols)


def can_pass_pieces(wide, narrow, width, deep):
    share = width // narrow
    return wide == 4 and narrow % 2 == 0 and narrow > 2 and share % 32 == 0 and deep % 128 == 0


def body(
    x_in, cotangent, segment_ids, type_ids,
    projection, context_out, expand_weight, reduce_weight, vector_params,
    first_projection, first_context, first_expand, first_reduce, first_vectors,
    second_projection, second_context, second_expand, second_reduce, second_vectors,
):
    seq_count, seq_len, width = x_in.shape
    rows = seq_count * seq_len

    def gather(array_in, axis):
        return lax.all_gather(array_in.astype(BF16), "narrow", axis=axis, tiled=True)

    hidden = x_in.reshape(rows, width)
    cot = cotangent.reshape(rows, width)
    narrow = lax.axis_size("narrow")
    pieces = can_pass_pieces(lax.axis_size("wide"), narrow, width, reduce_weight.shape[0])
    if pieces:
        query, keyval, context, aug, proj_w, mid_w, reduce_w, vec_rows, word, kmask, kaug = gather_call(
            narrow, hidden, projection, context_out, expand_weight, reduce_weight, vector_params,
            segment_ids, type_ids,
        )
    else:
        word_col = (type_ids == 0).reshape(rows, 1)
        lane = lax.broadcasted_iota(jnp.int32, (rows, LANES), 1)
        word = jnp.broadcast_to(word_col, (rows, LANES)).astype(BF16)
        kmask = ((lane < HEAD) == word_col).astype(BF16)
        same = segment_ids.reshape(rows, 1) == lane
        qaug = jnp.where(same & (lane < 8), 1.0, 0.0).astype(BF16)
        kaug = jnp.where(lane < 8, jnp.where(same, 0.0, FAR), jnp.where(lane < 11, 1.0, 0.0)).astype(BF16)
        proj_w, vec_half = gather(by_head(projection), 0), gather(vector_params, 1)
        reduce_w = gather(reduce_weight, 0)
        mid_w = jnp.concatenate(
            [gather(expand_weight, 0), gather(context_out, 0), jnp.zeros((width, 2 * LANES), BF16)], axis=1
        )
        zero_row = jnp.zeros((1, width), BF16)
        bias = by_head(jnp.concatenate([vec_half[0:4], zero_row, vec_half[4:5]]).reshape(1, -1)).astype(F32)
        vec_rows = jnp.pad(vec_half.astype(F32), ((0, 1), (0, 0)))
        query, keyval = qkv_call(hidden, proj_w, bias, word)
        context, aug = attend_call(query, keyval, qaug, kaug, kmask, seq_len)
    block_out, grad_r1, grad_context, grad_reduce, grad_expand, grad_ctx_w, grad_mid = middle_call(
        hidden, context, cot, vec_rows, mid_w, reduce_w, 256
    )
    masters = (projection, context_out, expand_weight, reduce_weight, vector_params)
    firsts = (first_projection, first_context, first_expand, first_reduce, first_vectors)
    seconds = (second_projection, second_context, second_expand, second_reduce, second_vectors)
    out_shape = (seq_count, seq_len, width)
    if pieces:
        input_grad, shard_w, shard_e, shard_a, grad_vectors, norm = reduce_call(
            narrow, hidden, query, keyval, aug, grad_context, context, proj_w, kaug, kmask, word, grad_mid,
            grad_r1, grad_expand, grad_ctx_w, grad_reduce, seq_len,
        )
        updated = update_call(narrow, norm, shard_a, shard_e, shard_w, grad_vectors, masters, firsts, seconds)
        return (
            block_out.reshape(out_shape),
            input_grad.reshape(out_shape),
            jnp.sqrt(norm[0, 0]),
            *updated,
        )
    grad_proj, grad_proj_w, grad_sums = attend_back_call(
        hidden, query, keyval, aug, grad_context, context, kaug, kmask, word, seq_len
    )
    input_grad = input_grad_call(grad_proj, proj_w, grad_r1, 256)
    sum_rows = by_block(grad_sums).reshape(6, width)
    grad_vectors = jnp.concatenate([sum_rows[0:4], sum_rows[5:6], grad_mid[5:15]], axis=0)

    def scatter(array_in, axis):
        return lax.psum_scatter(array_in, "narrow", scatter_dimension=axis, tiled=True)

    def over_wide(array_in):
        return lax.psum(array_in.astype(BF16), "wide").astype(F32)

    shards = (
        by_block(over_wide(scatter(grad_proj_w, 0))),
        over_wide(scatter(grad_ctx_w, 0)),
        over_wide(scatter(grad_expand, 0)),
        over_wide(scatter(grad_reduce, 0)),
        over_wide(scatter(grad_vectors, 1)),
    )
    local_squares = sum((jnp.sum(shard_item * shard_item) for shard_item in shards))
    total_squares = lax.psum(local_squares, "narrow")
    grad_norm = jnp.sqrt(total_squares)
    factor = jnp.minimum(1.0, clip_limit / (grad_norm + 1e-06))
    results = [
        adam_update(masters[index], firsts[index], seconds[index], shards[index], factor, index)
        for index in range(5)
    ]
    return (
        block_out.reshape(out_shape),
        input_grad.reshape(out_shape),
        grad_norm,
        *(item[0] for item in results),
        *(item[1] for item in results),
        *(item[2] for item in results),
        *(item[0].astype(BF16) for item in results),
    )


def solution(mesh):
    shard, col = P("narrow", None), P(None, "narrow")
    seqs = P(("wide", "narrow"), None, None)
    group = (shard, shard, shard, shard, col)
    return jax.shard_map(
        body,
        mesh=mesh,
        in_specs=(seqs, seqs, P(("wide", "narrow"), None), P(("wide", "narrow"), None), *group, *group, *group),
        out_specs=(seqs, seqs, P(), *group, *group, *group, *group),
        check_vma=False,
    )
```

profile of v0, /device:TPU:0, one launch (start us, length us, event | category | flops | bytes accessed | tf_op | source)
XLA Modules:
  0.0 330.6 jit_solution(14818550687779363288)
XLA Ops:
  0.7 93.1 %gather.1 = (bf16[1280,1536]{1,0:T(8,128)(2,1)}, bf16[1280,1536]{1,0:T(8,128)(2,1)}, bf16[1280,768]{1,0:T(8,128)(2,1)}, bf16[1280,1536]{1,0:T(8,128)(2,1)}, bf16...) custom-call(bf16[1280,768]{1,0:T(8,128)(2,1)} %bitcast.5, ...), custom_call_target="tpu_custom_call" | custom-call | tf_op jit(solution)/shard_map/gather/pallas_call | solution.py:419
  93.8 72.5 %middle.1 = (bf16[1280,768]{1,0:T(8,128)(2,1)}, f32[1280,768]{1,0:T(8,128)}, bf16[1280,768]{1,0:T(8,128)(2,1)}, bf16[3072,768]{1,0:T(8,128)(2,1)}, bf16[768,3072...) custom-call(bf16[1280,768]{1,0:T(8,128)(2,1)} %bitcast.6, bf16[1280,768]{1,0:T(8,128)(2,1)} %get-tuple-element.67.ctx_ref, ...), custom_call_target="tpu_custom_call" | custom-call | tf_op jit(solution)/shard_map/middle/pallas_call | solution.py:1161
  166.3 144.9 %reduce.1 = (bf16[1280,768]{1,0:T(8,128)(2,1)}, bf16[384,768]{1,0:T(8,128)(2,1)}, bf16[96,4096]{1,0:T(8,128)(2,1)}, bf16[96,4608]{1,0:T(8,128)(2,1)}, f32[16,768]{1,0:T(8,128)}, /*index=5*/f32[8,128]{1,0:T(8,128)}) custom-call(bf16[1280,768]{1,0:T(8,128)(2,1)} %bitcast.7, bf16[1280,1536]{1,0:T(8,128)(2,1)} %get-tuple-element.72.q_ref, ...), custom_call_target="tpu_custom_call" | custom-call | tf_op jit(solution)/shard_map/reduce/pallas_call | solution.py:991
  311.3 1.2 slice.3
  313.2 0.0 copy-start
  313.2 14.7 %update.1 = (f32[96,4608]{1,0:T(8,128)}, f32[96,768]{1,0:T(8,128)}, f32[96,3072]{1,0:T(8,128)}, f32[384,768]{1,0:T(8,128)}, f32[15,96]{1,0:T(8,128)}, /*index=5*...) custom-call(f32[8,128]{1,0:T(8,128)} %get-tuple-element.86.n_ref, ...), custom_call_target="tpu_custom_call" | custom-call | tf_op jit(solution)/shard_map/update/pallas_call | solution.py:1297
  327.9 0.0 copy-done
  327.9 1.3 copy.43
Async XLA Ops:
  313.2 14.7 %copy-start = (bf16[1280,768]{1,0:T(8,128)(2,1)S(1)}, bf16[1280,768]{1,0:T(8,128)(2,1)}, u32[]{:S(2)}) copy-start(bf16[1280,768]{1,0:T(8,128)(2,1)} %get-tuple-element.85) | copy-start | bytes 5898244
where the time goes:
time: 334 us; the launch traced here: 331 us
  Pallas kernels  325 us (97%)
    pallas_call x1, Pallas kernels, reduce_call(): pl.pallas_call(functools.partial(reduce_kernel, narrow, length, groups),...  145 us
    pallas_call x1, Pallas kernels, gather_call(): pl.pallas_call(functools.partial(gather_kernel, narrow), in_specs=[vmem]...  93.1 us
    pallas_call x1, Pallas kernels, middle_call(): pl.pallas_call(functools.partial(middle_kernel, tiles), grid=(tiles + 2 *...  72.5 us
    pallas_call x1, Pallas kernels, update_call(): pl.pallas_call(functools.partial(update_kernel, narrow), grid=(steps,), i...  14.7 us

commit v1 on v0

--- a/solution.py
+++ b/solution.py
@@ -94,39 +94,48 @@
 
 class Links:
     def __init__(self, send, recv):
-        self.send, self.recv = send, recv
-        self.count = 0
+        self.send_sem, self.recv_sem = send, recv
         self.slots = {}
-        self.open = []
-
-    def slot(self, key):
-        if key not in self.slots:
-            self.slots[key] = len(self.slots)
-        return self.slots[key]
+        self.sent = []
 
     def copy(self, key, src, dst, device):
-        index = self.slot(key)
+        index = self.slots.setdefault(key, len(self.slots))
         return pltpu.make_async_remote_copy(
             src_ref=src,
             dst_ref=dst,
-            send_sem=self.send.at[index],
-            recv_sem=self.recv.at[index],
+            send_sem=self.send_sem.at[index],
+            recv_sem=self.recv_sem.at[index],
             device_id=device,
             device_id_type=pl.DeviceIdType.MESH,
         )
 
-    def start(self, key, src, dst, device):
-        copy = self.copy(key, src, dst, device)
-        copy.start()
-        self.open.append(copy)
+    def send(self, key, build, *guards):
+        def start():
+            self.copy(key, *build()).start()
+
+        guarded(start, guards)
+        self.sent.append((key, build, guards))
 
     def arrived(self, key, dst, device):
         self.copy(key, dst, dst, device).wait_recv()
 
     def finish(self):
-        for copy in self.open:
-            copy.wait_send()
-        self.open = []
+        for key, build, guards in self.sent:
+
+            def wait(key=key, build=build):
+                self.copy(key, *build()).wait_send()
+
+            guarded(wait, guards)
+
+
+def guarded(action, guards):
+    if not guards:
+        action()
+        return
+    holds = guards[0]()
+    for guard in guards[1:]:
+        holds = jnp.logical_and(holds, guard())
+    pl.when(holds)(action)
 
 
 class Place:
@@ -152,6 +161,31 @@
     def z_dev(self, k):
         return {"narrow": self.ahead(k)}
 
+    def has_next(self, way):
+        return lambda: self.z + 1 < self.depth if way == 0 else self.z > 0
+
+    def comes(self, way, hop):
+        return lambda: self.z >= hop if way == 0 else self.z + hop < self.depth
+
+    def origin(self, way, hop, other=False):
+        core = 1 - self.core if other else self.core
+        return 2 * (self.z - hop if way == 0 else self.z + hop) + core
+
+    def next_dev(self, way):
+        return {"narrow": self.me + 2 if way == 0 else self.me - 2}
+
+    def greet_near(self):
+        barrier = pltpu.get_barrier_semaphore()
+
+        def greet(device):
+            pl.semaphore_signal(barrier, inc=1, device_id=device, device_id_type=pl.DeviceIdType.MESH)
+
+        for device in (self.x_dev, self.y_dev, self.sib_dev):
+            greet(device)
+        for way in range(2):
+            guarded(lambda way=way: greet(self.next_dev(way)), (self.has_next(way),))
+        pl.semaphore_wait(barrier, 3 + jnp.minimum(self.z, 1) + jnp.minimum(self.depth - 1 - self.z, 1))
+
     def greet(self):
         barrier = pltpu.get_barrier_semaphore()
         partners = [self.x_dev, self.y_dev, self.sib_dev] + [self.z_dev(k) for k in range(1, self.depth)]
@@ -176,7 +210,8 @@
     heads = width // HEAD
     here = Place(narrow)
     links = Links(send, recv)
-    me, steps = here.me, range(1, here.depth)
+    me, hops = here.me, range(1, here.depth)
+    routes = [(way, hop) for hop in hops for way in range(2)]
 
     def region(kind, owner, part, side=None):
         size, start = (share, 0) if side is None else (half, side * half)
@@ -199,49 +234,91 @@
     def own(kind):
         return {"a": whole("a", me), "e": e_own, "w": w2_own, "v": v_all.at[me]}[kind]
 
-    def own_quarter(kind):
+    def own_part(kind, part, side=None):
         if kind == "a":
-            return region("a", me, here.wide)
+            return region("a", me, part, side)
         if kind == "e":
-            return e_own.at[:, spot(here.wide * equarter, equarter, LANES)]
-        return w2_own.at[spot(here.wide * dquarter, dquarter, 16), :]
-
-    def send_z(kind, k):
-        links.start((kind, "z", k), own_quarter(kind), region(kind, me, here.wide), here.z_dev(k))
+            rows = slice(0, share) if side is None else slice(side * half, (side + 1) * half)
+            return e_own.at[rows, spot(part * equarter, equarter, LANES)]
+        size, start = (dquarter, 0) if side is None else (dquarter // 2, side * (dquarter // 2))
+        return w2_own.at[spot(part * dquarter + start, size, 16), :]
 
     def send_own(kind):
-        links.start((kind, "o"), own(kind), whole(kind, me), here.sib_dev)
-
-    def pass_z(kind, k):
-        piece = region(kind, here.behind(k), here.wide)
-        links.arrived((kind, "z", k), piece, here.z_dev(k))
-        links.start((kind, "x", k), piece, piece, here.x_dev)
-        links.start((kind, "y", k), piece, piece, here.y_dev)
-        links.start((kind, "sz", k), piece, piece, here.sib_dev)
-
-    def pass_xy(kind, k):
-        owner = here.behind(k)
-        piece = region(kind, owner, here.x_quarter)
-        links.arrived((kind, "x", k), piece, here.x_dev)
-        part = region(kind, owner, here.x_quarter, 0)
-        links.start((kind, "dy", k), part, part, here.y_dev)
-        links.start((kind, "sx", k), piece, piece, here.sib_dev)
-        piece = region(kind, owner, here.y_quarter)
-        links.arrived((kind, "y", k), piece, here.y_dev)
-        part = region(kind, owner, here.y_quarter, 1)
-        links.start((kind, "dx", k), part, part, here.x_dev)
-        links.start((kind, "sy", k), piece, piece, here.sib_dev)
-
-    def pass_d(kind, k):
-        owner = here.behind(k)
-        links.arrived((kind, "dy", k), region(kind, owner, here.d_quarter, 0), here.y_dev)
-        links.arrived((kind, "dx", k), region(kind, owner, here.d_quarter, 1), here.x_dev)
-        piece = region(kind, owner, here.d_quarter)
-        links.start((kind, "sd", k), piece, piece, here.sib_dev)
-
-    def from_sib(kind, way, part):
-        for k in steps:
-            links.arrived((kind, way, k), region(kind, here.behind(k, True), part), here.sib_dev)
+        links.send((kind, "o"), lambda: (own(kind), whole(kind, me), here.sib_dev))
+
+    def send_z(kind):
+        for way in range(2):
+            ahead = here.has_next(way)
+            if kind == "v":
+                links.send(("v", "z", way, 1), lambda way=way: (own("v"), own("v"), here.next_dev(way)), ahead)
+                continue
+            links.send(
+                (kind, "z", way, 1),
+                lambda way=way: (own_part(kind, here.wide), region(kind, me, here.wide), here.next_dev(way)),
+                ahead,
+            )
+            links.send(
+                (kind, "h", way, 1),
+                lambda way=way: (
+                    own_part(kind, here.d_quarter, 0), region(kind, me, here.d_quarter, 0), here.next_dev(way)
+                ),
+                ahead,
+            )
+
+    def relay(key, target, device, *guards):
+        links.send(key, lambda: (target(), target(), device()), *guards)
+
+    def receive(key, target, guard):
+        guarded(lambda: links.arrived(key, target(), here.sib_dev), (guard,))
+
+    def pass_z(kind, hop):
+        for way in range(2):
+            comes, ahead = here.comes(way, hop), here.has_next(way)
+            onward = lambda way=way: here.next_dev(way)
+            if kind == "v":
+                piece = lambda way=way: whole("v", here.origin(way, hop))
+            else:
+                piece = lambda way=way: region(kind, here.origin(way, hop), here.wide)
+            receive((kind, "z", way, hop), piece, comes)
+            if hop + 1 < here.depth:
+                relay((kind, "z", way, hop + 1), piece, onward, comes, ahead)
+            if kind != "v":
+                relay((kind, "x", way, hop), piece, lambda: here.x_dev, comes)
+                relay((kind, "y", way, hop), piece, lambda: here.y_dev, comes)
+            relay((kind, "sz", way, hop), piece, lambda: here.sib_dev, comes)
+            if kind != "v":
+                other = lambda way=way: region(kind, here.origin(way, hop), here.d_quarter, 0)
+                receive((kind, "h", way, hop), other, comes)
+                if hop + 1 < here.depth:
+                    relay((kind, "h", way, hop + 1), other, onward, comes, ahead)
+                relay((kind, "sh", way, hop), other, lambda: here.sib_dev, comes)
+
+    def by_x(kind, hop):
+        return kind == "a" or (kind == "w" and hop % 2 == 1)
+
+    def pass_xy(kind, hop):
+        for way in range(2):
+            comes = here.comes(way, hop)
+            for name, part, back in (("x", here.x_quarter, "y"), ("y", here.y_quarter, "x")):
+                piece = lambda way=way, part=part: region(kind, here.origin(way, hop), part)
+                receive((kind, name, way, hop), piece, comes)
+                if by_x(kind, hop) == (back == "x"):
+                    device = here.x_dev if back == "x" else here.y_dev
+                    rest = lambda way=way, part=part: region(kind, here.origin(way, hop), part, 1)
+                    relay((kind, "d", way, hop), rest, lambda device=device: device, comes)
+                relay((kind, "s" + name, way, hop), piece, lambda: here.sib_dev, comes)
+
+    def pass_d(kind):
+        for way, hop in routes:
+            comes = here.comes(way, hop)
+            rest = lambda way=way, hop=hop: region(kind, here.origin(way, hop), here.d_quarter, 1)
+            receive((kind, "d", way, hop), rest, comes)
+            relay((kind, "sd", way, hop), rest, lambda: here.sib_dev, comes)
+
+    def from_sib(kind, name, part, side=None):
+        for way, hop in routes:
+            piece = lambda way=way, hop=hop: region(kind, here.origin(way, hop, True), part, side)
+            receive((kind, name, way, hop), piece, here.comes(way, hop))
 
     low = low_lanes(share)
     for pair in range(heads // 2):
@@ -255,10 +332,9 @@
     v_all[me] = jnp.zeros_like(v_all[me])
     v_all[me, 0 : vec_ref.shape[0], 0 : vec_ref.shape[1]] = vec_ref[...].astype(BF16)
 
-    here.greet()
-    for k in steps:
-        send_z("a", k)
-        links.start(("v", "z", k), v_all.at[me], v_all.at[me], here.z_dev(k))
+    here.greet_near()
+    send_z("a")
+    send_z("v")
     send_own("v")
     send_own("a")
 
@@ -289,21 +365,42 @@
             lane < 8, jnp.where(same, 0.0, FAR), jnp.where(lane < 11, 1.0, 0.0)
         ).astype(BF16)
 
-    for k in steps:
-        pass_z("a", k)
-        send_z("e", k)
-        owner = here.behind(k)
-        links.arrived(("v", "z", k), v_all.at[owner], here.z_dev(k))
-        links.start(("v", "sz", k), v_all.at[owner], v_all.at[owner], here.sib_dev)
-    for k in steps:
-        pass_xy("a", k)
+    def hop(kind, number):
+        if number < here.depth:
+            pass_z(kind, number)
+            if kind == "a":
+                pass_z("v", number)
+
+    def turn(kind, number):
+        if number < here.depth:
+            pass_xy(kind, number)
+
+    hop("a", 1)
+    hop("a", 2)
+    send_z("e")
     send_own("e")
+    turn("a", 1)
+    hop("a", 3)
+    turn("a", 2)
+    hop("e", 1)
+    turn("a", 3)
+    for number in range(4, here.depth):
+        hop("a", number)
+        turn("a", number)
+    hop("e", 2)
+    send_z("w")
     send_own("w")
+    hop("e", 3)
+    for number in range(4, here.depth):
+        hop("e", number)
 
     links.arrived(("v", "o"), v_all.at[here.sib], here.sib_dev)
-    for k in steps:
-        owner = here.behind(k, True)
-        links.arrived(("v", "sz", k), v_all.at[owner], here.sib_dev)
+    for way, number in routes:
+        receive(
+            ("v", "sz", way, number),
+            lambda way=way, number=number: v_all.at[here.origin(way, number, True)],
+            here.comes(way, number),
+        )
     span = vec_ref.shape[1]
     vec_out[...] = jnp.concatenate([v_all[n].astype(F32)[:, 0:span] for n in range(narrow)], axis=1)
     low1 = low_lanes(1)
@@ -347,18 +444,22 @@
 
     from_sib("a", "sz", here.wide)
     project(0, here.wide)
-    for k in steps:
-        pass_z("e", k)
-        send_z("w", k)
-    for k in steps:
-        pass_d("a", k)
+    turn("e", 1)
+    pass_d("a")
     from_sib("a", "sx", here.x_quarter)
     project(1, here.x_quarter)
-    for k in steps:
-        pass_xy("e", k)
+    hop("w", 1)
+    turn("e", 2)
+    hop("w", 2)
     from_sib("a", "sy", here.y_quarter)
     project(2, here.y_quarter)
-    from_sib("a", "sd", here.d_quarter)
+    turn("e", 3)
+    hop("w", 3)
+    for number in range(4, here.depth):
+        turn("e", number)
+        hop("w", number)
+    from_sib("a", "sh", here.d_quarter, 0)
+    from_sib("a", "sd", here.d_quarter, 1)
     project(3, here.d_quarter)
     copy_a = pltpu.make_async_copy(a_full, a_out, local.at[10])
     copy_a.start()
@@ -385,10 +486,10 @@
             outs.append(copy)
 
     between = [
-        lambda: [pass_z("w", k) for k in steps],
-        lambda: [pass_d("e", k) for k in steps],
-        lambda: [pass_xy("w", k) for k in steps],
-        lambda: [pass_d("w", k) for k in steps],
+        lambda: [pass_d("e"), turn("w", 1)],
+        lambda: turn("w", 2),
+        lambda: [turn("w", number) for number in range(3, here.depth)],
+        lambda: pass_d("w"),
     ]
     for pair in range(heads // 2):
         attend(pair)
@@ -398,8 +499,10 @@
         later()
     for kind in ("e", "w"):
         links.arrived((kind, "o"), whole(kind, here.sib), here.sib_dev)
-        for way, part in (("sz", here.wide), ("sx", here.x_quarter), ("sy", here.y_quarter), ("sd", here.d_quarter)):
-            from_sib(kind, way, part)
+        for name, part in (("sz", here.wide), ("sx", here.x_quarter), ("sy", here.y_quarter)):
+            from_sib(kind, name, part)
+        from_sib(kind, "sh", here.d_quarter, 0)
+        from_sib(kind, "sd", here.d_quarter, 1)
     links.finish()
     for copy in (copy_e, copy_w, copy_a, *outs):
         copy.wait()
@@ -411,7 +514,7 @@
     ecols = inner + width + 2 * LANES
     heads = width // HEAD
     depth = narrow // 2
-    count = 3 * (1 + 9 * (depth - 1)) + 1 + 2 * (depth - 1)
+    count = 3 * (1 + 20 * (depth - 1)) + 1 + 4 * (depth - 1)
     vmem = pl.BlockSpec(memory_space=pltpu.VMEM)
     hbm = pl.BlockSpec(memory_space=pl.ANY)
     shape = jax.ShapeDtypeStruct
@@ -585,11 +688,20 @@
 
 
 class Chunk:
-    def __init__(self, name, refs, by_rows):
-        self.name = name
-        self.total, self.r1a, self.r1b, self.r2a, self.r2b, self.rz, self.final = refs
-        self.by_rows = by_rows
-        _, self.rows, self.cols = self.total.shape
+    def __init__(self, name, by_rows, shape, total, plane=None, end=None):
+        self.name, self.by_rows = name, by_rows
+        self.rows, self.cols = shape
+        self.total = total
+        if plane is not None:
+            self.r1a, self.r1b, self.r2a, self.r2b = plane
+        if end is not None:
+            self.rz, self.final = end
+
+    def mine(self, z, wide):
+        if self.total.shape[1:] != (self.rows, self.cols):
+            return self.total.at[z]
+        rows, cols = self.cut(wide)
+        return self.total.at[z, rows, cols]
 
     def cut(self, part, side=None):
         if self.by_rows:
@@ -602,43 +714,36 @@
         return rows, spot(part * size, size, LANES)
 
 
-def chunk_scratch(depth, rows, cols, by_rows):
+def piece_shapes(rows, cols, by_rows):
     if by_rows:
-        piece, half = (rows // 4, cols), (rows // 8, cols)
-    else:
-        piece, half = (rows, cols // 4), (rows // 2, cols // 4)
+        return (rows // 4, cols), (rows // 8, cols)
+    return (rows, cols // 4), (rows // 2, cols // 4)
+
+
+def plane_scratch(depth, rows, cols, by_rows):
+    _, half = piece_shapes(rows, cols, by_rows)
     return [
-        pltpu.VMEM((depth, rows, cols), BF16),
         pltpu.VMEM((2, depth, *half), BF16),
         pltpu.VMEM((2, depth, *half), BF16),
         pltpu.VMEM((depth, *half), BF16),
         pltpu.VMEM((depth, *half), BF16),
-        pltpu.VMEM((depth - 1, *piece), BF16),
-        pltpu.VMEM((rows, cols), BF16),
     ]
+
+
+def end_scratch(depth, rows, cols, by_rows):
+    piece, _ = piece_shapes(rows, cols, by_rows)
+    return [pltpu.VMEM((depth - 1, *piece), BF16), pltpu.VMEM((rows, cols), BF16)]
 
 
 class Reducer:
     def __init__(self, here, send, recv):
         self.here = here
         self.links = Links(send, recv)
-        self.sent = []
-
-    def send(self, key, build):
-        copy = self.links.copy(key, *build())
-        copy.start()
-        self.sent.append((key, build))
-
-    def arrived(self, key, dst, device):
-        self.links.arrived(key, dst, device)
-
-    def finish(self):
-        for key, build in self.sent:
-            self.links.copy(key, *build()).wait_send()
-
-    def pair_send(self, chunk, sources):
+        self.send, self.arrived, self.finish = self.links.send, self.links.arrived, self.links.finish
+
+    def pair_send(self, chunk, sources, only=None):
         here = self.here
-        for z in range(here.depth):
+        for z in range(here.depth) if only is None else (only,):
             for part, (_, cols) in enumerate(sources(0)):
 
                 def build(z=z, part=part, cols=cols):
@@ -692,17 +797,20 @@
         self.add(chunk, here.wide, 0, chunk.r1a[0])
         self.add(chunk, here.wide, 1, chunk.r1b[0])
 
-    def depth_send(self, chunk):
+    def plane_done(self, chunk):
         here = self.here
         self.arrived((chunk.name, "2a"), chunk.r2a, here.y_dev)
         self.arrived((chunk.name, "2b"), chunk.r2b, here.x_dev)
         self.add(chunk, here.wide, 0, chunk.r2a[...])
         self.add(chunk, here.wide, 1, chunk.r2b[...])
+
+    def depth_send(self, chunk):
+        here = self.here
         for k in range(1, here.depth):
 
             def build(k=k):
-                rows, cols = chunk.cut(here.wide)
-                return chunk.total.at[lax.rem(here.z + k, here.depth), rows, cols], chunk.rz.at[k - 1], here.z_dev(k)
+                piece = chunk.mine(lax.rem(here.z + k, here.depth), here.wide)
+                return piece, chunk.rz.at[k - 1], here.z_dev(k)
 
             self.send((chunk.name, "z", k), build)
 
@@ -711,7 +819,7 @@
         for k in range(1, here.depth):
             self.arrived((chunk.name, "z", k), chunk.rz.at[k - 1], here.z_dev(k))
         rows, cols = chunk.cut(here.wide)
-        done = chunk.total[here.z, rows, cols].astype(F32)
+        done = chunk.mine(here.z, here.wide)[...].astype(F32)
         for k in range(1, here.depth):
             done = done + chunk.rz[k - 1].astype(F32)
         chunk.final[rows, cols] = done.astype(BF16)
@@ -755,258 +863,269 @@
 
 
 def reduce_kernel(
-    narrow, length, groups,
+    narrow, length, groups, deep,
     x_ref, q_ref, kv_ref, aug_ref, gc_ref, ctx_ref, wp_ref, ka_ref, km_ref, word_ref, gvec_ref,
-    gr1_ref, gw1_ref, gwo_ref, gw2_ref,
-    ig_ref, fw_ref, fe_ref, fa_ref, v_ref, n_ref,
-    xt, gw, gp_ref, ig, *scratch,
+    gr1_ref, t1_ref, tw_ref, gwo_ref,
+    ig_ref, f1_ref, fo_ref, fw_ref, fa_ref, v_ref, n_ref,
+    xt, gp, ig, *scratch,
 ):
     step = pl.program_id(0)
     rows, width = x_ref.shape
     heads = groups * CHUNK_HEADS
-    inner = gw1_ref.shape[1]
+    share, inner = t1_ref.shape[1:]
     here = Place(narrow)
     scratch = list(scratch)
-    chunk_w = Chunk("w", scratch[0:7], True)
-    chunk_e = Chunk("e", scratch[7:14], False)
-    chunk_a = [Chunk(("a", j), scratch[14 + 7 * j : 21 + 7 * j], False) for j in range(groups)]
-    own_w, own_e, v0, v1, v2, vs, vx, vy, vz, n0, ns, nz, send, recv, local = scratch[14 + 7 * groups :]
-    red = Reducer(here, send, recv)
-    share, deep = chunk_e.rows, chunk_w.rows
-
-    def sources_w(owner):
-        return [(gw2_ref.at[spot(owner * deep, deep, 16), :], slice(0, width))]
-
-    def sources_e(owner):
-        at = spot(owner * share, share, 16)
-        return [(gw1_ref.at[at, :], slice(0, inner)), (gwo_ref.at[at, :], slice(inner, inner + width))]
+    red = Reducer(here, scratch[-3], scratch[-2])
+    local = scratch[-1]
+
+    def take(count):
+        taken, scratch[:count] = scratch[:count], []
+        return taken
+
+    chunk_w = Chunk("w", True, (deep, width), take(1)[0], None, take(2))
+    chunk_1 = Chunk("1", False, (share, inner), take(1)[0], take(4), take(2))
+    gw, chunk_a = [], []
+    for j in range(groups):
+        gw += take(1)
+        chunk_a.append(Chunk(("a", j), False, (share, gw[j].shape[1]), take(1)[0], take(4), take(2)))
+    v0, v1, v2, vs, vx, vy, vz, n0, ns, nz = take(10)
+    wide = CHUNK_HEADS * GROUP
 
     def sources_a(j):
-        return lambda owner: [(gw.at[j, spot(owner * share, share, 16), :], slice(0, CHUNK_HEADS * GROUP))]
-
-    def own_copies():
-        copies = []
-        for own, sources in ((own_w, sources_w), (own_e, sources_e)):
-            for z in range(here.depth):
-                for source, cols in sources(2 * z + here.core):
-                    copies.append(pltpu.make_async_copy(source, own.at[z, :, cols], local.at[len(copies)]))
-        return copies
-
-    def out_copies():
-        copies = [(chunk_w.final, fw_ref), (chunk_e.final, fe_ref)]
-        wide = CHUNK_HEADS * GROUP
-        copies += [(chunk.final, fa_ref.at[:, j * wide : (j + 1) * wide]) for j, chunk in enumerate(chunk_a)]
-        base = 3 * here.depth
-        return [pltpu.make_async_copy(a, b, local.at[base + i]) for i, (a, b) in enumerate(copies)]
-
-    def copy_ig():
-        return pltpu.make_async_copy(gr1_ref, ig, local.at[3 * here.depth + 2 + groups])
-
-    def merge(chunk, own):
+        return lambda owner: [(gw[j].at[spot(owner * share, share, 16), :], slice(0, gw[j].shape[1]))]
+
+    def load(index):
+        source, target = (
+            (t1_ref, chunk_1.total),
+            (tw_ref, chunk_w.total),
+            (gwo_ref, gw[0].at[:, wide : wide + width]),
+            (gr1_ref, ig),
+        )[index]
+        return pltpu.make_async_copy(source, target, local.at[index])
+
+    def stores():
+        copies = [(chunk_w.final, fw_ref), (chunk_1.final, f1_ref)]
+        copies += [(chunk_a[0].final.at[:, wide : wide + width], fo_ref)]
+        copies += [
+            (chunk.final.at[:, 0:wide], fa_ref.at[:, j * wide : (j + 1) * wide]) for j, chunk in enumerate(chunk_a)
+        ]
+        return [pltpu.make_async_copy(a, b, local.at[4 + i]) for i, (a, b) in enumerate(copies)]
+
+    def merge(j):
         def one(z, carry):
-            chunk.total[z] = chunk.total[z] + own(z)
+            mine = spot((2 * z + here.core) * share, share, 16)
+            chunk_a[j].total[z] = chunk_a[j].total[z] + gw[j][mine, :]
             return carry
 
+        red.pair_wait(chunk_a[j], sources_a(j))
         lax.fori_loop(0, here.depth, one, 0)
-
-    def own_a(j):
-        return lambda z: gw[j, spot((2 * z + here.core) * share, share, 16), :]
+        red.plane_send(chunk_a[j])
+
+    def turn_z(chunk):
+        red.plane_done(chunk)
+        red.depth_send(chunk)
 
     @pl.when(step == 0)
     def _():
-        for copy in own_copies():
-            copy.start()
-        copy_ig().start()
+        for index in range(4):
+            load(index).start()
         here.greet()
-        red.pair_send(chunk_w, sources_w)
-        red.pair_send(chunk_e, sources_e)
-        pad = chunk_e.cols - inner - width
-        chunk_e.total[:, :, inner + width :] = jnp.zeros((here.depth, share, pad), BF16)
-        own_e[:, :, inner + width :] = jnp.zeros((here.depth, share, pad), BF16)
+        load(0).wait()
+        red.plane_send(chunk_1)
+        load(1).wait()
+        red.depth_send(chunk_w)
+        v0[...] = gvec_ref[...]
+        pad = gw[0].shape[1] - wide - width
+        gw[0][:, wide + width :] = jnp.zeros((width, pad), BF16)
         xt[...] = jnp.transpose(x_ref[...])
-        v0[...] = gvec_ref[...]
-
-    def advance(at, action):
-        pl.when(step == at)(action)
-
-    def act_w1():
-        for copy in own_copies():
-            copy.wait()
-        red.pair_wait(chunk_w, sources_w)
-        merge(chunk_w, lambda z: own_w[z])
-        red.plane_send(chunk_w)
-
-    def act_e1():
-        red.pair_wait(chunk_e, sources_e)
-        merge(chunk_e, lambda z: own_e[z])
-        red.plane_send(chunk_e)
-
-    def act_a1(j):
-        red.pair_wait(chunk_a[j], sources_a(j))
-        merge(chunk_a[j], own_a(j))
-        red.plane_send(chunk_a[j])
-
-    advance(1, act_w1)
-    advance(2, act_e1)
-    advance(4, lambda: red.plane_turn(chunk_w))
-    advance(5, lambda: act_a1(0))
-    advance(6, lambda: red.depth_send(chunk_w))
-    advance(8, lambda: red.plane_turn(chunk_e))
-    advance(9, lambda: act_a1(1))
-    advance(10, lambda: red.depth_send(chunk_e))
-    advance(11, lambda: red.share_send(chunk_w))
-
-    low = low_lanes(length)
-    lane = lax.broadcasted_iota(jnp.int32, (length, LANES), 1)
-    odd = lax.rem(step, 2) == 1
-    for seq in range(rows // length):
-        at = slice(seq * length, (seq + 1) * length)
-        tiles = attend_back_head(
-            q_ref[at], kv_ref[at], aug_ref[at], gc_ref[at], ctx_ref[at],
-            ka_ref[at], km_ref[at], word_ref[at] > 0, odd, low, lane,
-        )
-        for index, tile in enumerate(tiles):
-            gp_ref[at, index * LANES : (index + 1) * LANES] = tile
-    grads = gp_ref[...]
-    group, inside = step // CHUNK_HEADS, lax.rem(step, CHUNK_HEADS)
-    gw[group, :, spot(inside * GROUP, GROUP, LANES)] = mm(xt[...], grads).astype(BF16)
-    sums = jnp.sum(jnp.sum(grads.astype(F32).reshape(rows // 8, 8, GROUP), axis=0), axis=0, keepdims=True)
-
-    @pl.when(step == 0)
+
+    def at(when):
+        def run(action):
+            def body():
+                action()
+
+            pl.when(step == when)(body)
+
+        return run
+
+    at(2)(lambda: load(2).wait())
+    at(3)(lambda: red.plane_turn(chunk_1))
+    at(4)(lambda: red.share_send(chunk_w))
+    at(5)(lambda: merge(0))
+    at(6)(lambda: [turn_z(chunk_1), red.share_pass(chunk_w)])
+    at(8)(lambda: [red.plane_turn(chunk_a[0]), red.share_wait(chunk_w)])
+    at(9)(lambda: [merge(1), red.share_send(chunk_1)])
+    at(10)(lambda: turn_z(chunk_a[0]))
+    at(11)(lambda: [red.plane_turn(chunk_a[1]), red.share_pass(chunk_1)])
+
+    @pl.when(step < heads)
     def _():
-        copy_ig().wait()
-
-    ig[...] += mm_nt(grads, wp_ref[...])
-
-    low1 = low_lanes(1)
-    pair = spot(step // 2 * LANES, LANES, LANES)
-    mine = low1 != odd
-    for b in range(3):
-        tile = sums[:, b * LANES : (b + 1) * LANES]
-        turned = swap_halves(tile)
-        first = jnp.where(odd, turned, tile)
-        second = jnp.where(odd, tile, turned)
-        if b < 2:
-            v0[2 * b : 2 * b + 1, pair] = jnp.where(mine, first, v0[2 * b : 2 * b + 1, pair])
-            v0[2 * b + 1 : 2 * b + 2, pair] = jnp.where(mine, second, v0[2 * b + 1 : 2 * b + 2, pair])
-        else:
-            v0[4:5, pair] = jnp.where(mine, second, v0[4:5, pair])
+        low = low_lanes(length)
+        lane = lax.broadcasted_iota(jnp.int32, (length, LANES), 1)
+        odd = lax.rem(step, 2) == 1
+        for seq in range(rows // length):
+            here_rows = slice(seq * length, (seq + 1) * length)
+            tiles = attend_back_head(
+                q_ref[here_rows], kv_ref[here_rows], aug_ref[here_rows], gc_ref[here_rows], ctx_ref[here_rows],
+                ka_ref[here_rows], km_ref[here_rows], word_ref[here_rows] > 0, odd, low, lane,
+            )
+            for index, tile in enumerate(tiles):
+                gp[step, here_rows, index * LANES : (index + 1) * LANES] = tile
+        grads = gp[step]
+        product = mm(xt[...], grads).astype(BF16)
+        inside = spot(lax.rem(step, CHUNK_HEADS) * GROUP, GROUP, LANES)
+        for j in range(groups):
+
+            @pl.when(step // CHUNK_HEADS == j)
+            def _():
+                gw[j][:, inside] = product
+
+        sums = jnp.sum(jnp.sum(grads.astype(F32).reshape(rows // 8, 8, GROUP), axis=0), axis=0, keepdims=True)
+
+        low1 = low_lanes(1)
+        pair = spot(step // 2 * LANES, LANES, LANES)
+        mine = low1 != odd
+        for b in range(3):
+            tile = sums[:, b * LANES : (b + 1) * LANES]
+            turned = swap_halves(tile)
+            first = jnp.where(odd, turned, tile)
+            second = jnp.where(odd, tile, turned)
+            if b < 2:
+                v0[2 * b : 2 * b + 1, pair] = jnp.where(mine, first, v0[2 * b : 2 * b + 1, pair])
+                v0[2 * b + 1 : 2 * b + 2, pair] = jnp.where(mine, second, v0[2 * b + 1 : 2 * b + 2, pair])
+            else:
+                v0[4:5, pair] = jnp.where(mine, second, v0[4:5, pair])
 
     for j in range(groups):
-        advance((j + 1) * CHUNK_HEADS - 1, lambda j=j: red.pair_send(chunk_a[j], sources_a(j)))
-
-    @pl.when(step == heads - 1)
-    def _():
-        ig_ref[...] = ig[...].astype(BF16)
-        last = chunk_a[-1]
-        red.send(("v", "s"), lambda: (v0, vs, here.sib_dev))
-        red.plane_turn(chunk_a[0])
-        red.share_send(chunk_e)
-        red.share_pass(chunk_w)
-        act_a1(groups - 1)
+        at((j + 1) * CHUNK_HEADS - 1)(lambda j=j: red.pair_send(chunk_a[j], sources_a(j)))
+
+    last = chunk_a[-1]
+
+    def vec_pair():
         red.arrived(("v", "s"), vs, here.sib_dev)
         v1[...] = v0[...] + vs[...]
         red.send(("v", "x"), lambda: (v1, vx, here.x_dev))
-        red.depth_send(chunk_a[0])
-        for chunk in chunk_a[1:-1]:
-            red.plane_turn(chunk)
-        red.share_pass(chunk_e)
-        for chunk in chunk_a[1:-1]:
-            red.depth_send(chunk)
-        red.plane_turn(last)
+
+    def vec_plane():
         red.arrived(("v", "x"), vx, here.x_dev)
         v2[...] = v1[...] + vx[...]
         red.send(("v", "y"), lambda: (v2, vy, here.y_dev))
-        for chunk in chunk_a[:-1]:
-            red.share_send(chunk)
-        red.depth_send(last)
+
+    def vec_depth():
         red.arrived(("v", "y"), vy, here.y_dev)
         vz[here.z] = v2[...] + vy[...]
         for k in range(1, here.depth):
             red.send(("v", "z", k), lambda k=k: (vz.at[here.z], vz.at[here.z], here.z_dev(k)))
-        red.share_wait(chunk_w)
-        red.share_wait(chunk_e)
-        for chunk in chunk_a[:-1]:
-            red.share_pass(chunk)
-        norm = squares(chunk_w.final, width) + squares(chunk_e.final, inner + width)
-        for chunk in chunk_a[:-1]:
-            red.share_wait(chunk)
-            norm = norm + squares(chunk.final, chunk.cols)
-        red.share_send(last)
+
+    def vec_done():
         for k in range(1, here.depth):
-            source = here.behind(k) // 2
-            red.arrived(("v", "z", k), vz.at[source], here.z_dev(k))
+            red.arrived(("v", "z", k), vz.at[here.behind(k) // 2], here.z_dev(k))
         vec = vz[0]
         for z in range(1, here.depth):
             vec = vec + vz[z]
         v_ref[...] = vec
+
+    at(heads - 1)(lambda: red.send(("v", "s"), lambda: (v0, vs, here.sib_dev)))
+    at(heads)(lambda: load(3).wait())
+
+    @pl.when(step >= heads)
+    def _():
+        ig[...] += mm_nt(gp[step - heads], wp_ref[...])
+
+    at(heads + 1)(lambda: [merge(groups - 1), vec_pair()])
+    at(heads + 2)(lambda: [red.share_send(chunk_a[0]), red.share_wait(chunk_1)])
+    at(heads + 3)(lambda: turn_z(chunk_a[1]))
+    at(heads + 4)(lambda: [red.share_pass(chunk_a[0]), vec_plane()])
+    at(heads + 6)(lambda: [red.plane_turn(last), red.share_wait(chunk_a[0])])
+    at(heads + 8)(lambda: [red.share_send(chunk_a[1]), vec_depth()])
+    at(heads + 9)(lambda: turn_z(last))
+    at(heads + 10)(lambda: [red.share_pass(chunk_a[1]), vec_done()])
+
+    @pl.when(step == 2 * heads - 1)
+    def _():
+        ig_ref[...] = ig[...].astype(BF16)
+        red.share_wait(chunk_a[1])
+        norm = squares(chunk_w.final, width) + squares(chunk_1.final, inner)
+        norm = norm + squares(chunk_a[0].final, wide + width)
+        for chunk in chunk_a[1:-1]:
+            norm = norm + squares(chunk.final, wide)
+        red.share_send(last)
+        vec = v_ref[...]
+        square = jnp.sum(jnp.sum(vec * vec, axis=0, keepdims=True), axis=1, keepdims=True)
         red.share_pass(last)
         red.share_wait(last)
-        for copy in out_copies():
+        for copy in stores():
             copy.start()
-        n0[...] = norm + squares(last.final, last.cols)
+        n0[...] = norm + squares(last.final, wide)
         red.send(("n", "s"), lambda: (n0, ns, here.sib_dev))
         red.arrived(("n", "s"), ns, here.sib_dev)
         nz[here.z] = n0[...] + ns[...]
         for k in range(1, here.depth):
             red.send(("n", "z", k), lambda k=k: (nz.at[here.z], nz.at[here.z], here.z_dev(k)))
         for k in range(1, here.depth):
-            source = here.behind(k) // 2
-            red.arrived(("n", "z", k), nz.at[source], here.z_dev(k))
+            red.arrived(("n", "z", k), nz.at[here.behind(k) // 2], here.z_dev(k))
         total = nz[0]
         for z in range(1, here.depth):
             total = total + nz[z]
         every = jnp.sum(jnp.sum(total, axis=0, keepdims=True), axis=1, keepdims=True)
-        square = jnp.sum(jnp.sum(vec * vec, axis=0, keepdims=True), axis=1, keepdims=True)
         n_ref[...] = jnp.broadcast_to(every + square, n_ref.shape)
         red.finish()
-        for copy in out_copies():
+        for copy in stores():
             copy.wait()
 
 
-def reduce_call(narrow, x, q, kv, aug, gc, ctx, wp, ka, km, word, gvec, gr1, gw1, gwo, gw2, length):
+def reduce_call(narrow, x, q, kv, aug, gc, ctx, wp, ka, km, word, gvec, gr1, t1, tw, gwo, deep, length):
     rows, width = x.shape
-    inner = gw2.shape[0]
     heads = q.shape[1] // LANES
     groups = heads // CHUNK_HEADS
-    depth = narrow // 2
-    share, deep, ecols, acols = width // narrow, inner // narrow, inner + width + 2 * LANES, CHUNK_HEADS * GROUP
-    head = pl.BlockSpec((rows, LANES), lambda h: (0, h))
-    pair = pl.BlockSpec((rows, LANES), lambda h: (0, h // 2))
-    one = pl.BlockSpec((rows, LANES), lambda h: (0, 0), pipeline_mode=pl.Buffered(1))
+    depth, share, inner = t1.shape
+    acols = CHUNK_HEADS * GROUP
+
+    def now(h):
+        return jnp.minimum(h, heads - 1)
+
+    def fixed(shape):
+        return pl.BlockSpec(shape, lambda h: (0, 0), pipeline_mode=pl.Buffered(1))
+
+    head = pl.BlockSpec((rows, LANES), lambda h: (0, now(h)))
+    pair = pl.BlockSpec((rows, LANES), lambda h: (0, now(h) // 2))
+    later = pl.BlockSpec((width, GROUP), lambda h: (0, jnp.maximum(h - heads, 0)))
+    one = fixed((rows, LANES))
     hbm = pl.BlockSpec(memory_space=pl.ANY)
     shape = jax.ShapeDtypeStruct
     vec = pltpu.VMEM((16, width), F32)
     tile = pltpu.VMEM((8, LANES), F32)
-    scratch = [pltpu.VMEM((width, rows), BF16), pltpu.VMEM((groups, width, acols), BF16)]
-    scratch += [pltpu.VMEM((rows, GROUP), BF16), pltpu.VMEM((rows, width), F32)]
-    scratch += chunk_scratch(depth, deep, width, True)
-    scratch += chunk_scratch(depth, share, ecols, False)
-    for _ in range(groups):
-        scratch += chunk_scratch(depth, share, acols, False)
-    scratch += [pltpu.VMEM((depth, deep, width), BF16), pltpu.VMEM((depth, share, ecols), BF16)]
+    scratch = [pltpu.VMEM((width, rows), BF16), pltpu.VMEM((heads, rows, GROUP), BF16), pltpu.VMEM((rows, width), F32)]
+    scratch += [pltpu.VMEM(tw.shape, BF16), *end_scratch(depth, deep, width, True)]
+    scratch += [
+        pltpu.VMEM(t1.shape, BF16),
+        *plane_scratch(depth, share, inner, False),
+        *end_scratch(depth, share, inner, False),
+    ]
+    for j in range(groups):
+        cols = acols + (width + 2 * LANES if j == 0 else 0)
+        scratch += [
+            pltpu.VMEM((width, cols), BF16),
+            pltpu.VMEM((depth, share, cols), BF16),
+            *plane_scratch(depth, share, cols, False),
+            *end_scratch(depth, share, cols, False),
+        ]
     scratch += [vec] * 6 + [pltpu.VMEM((depth, 16, width), F32), tile, tile, pltpu.VMEM((depth, 8, LANES), F32)]
-    count = (2 + groups) * (depth + 10 + depth - 1) + depth + 2 * (3 + depth)
-    scratch += [pltpu.SemaphoreType.DMA((count,))] * 2 + [pltpu.SemaphoreType.DMA((3 * depth + 3 + groups,))]
+    count = (2 + groups) * (depth + 10 + depth - 1) + 2 * (3 + depth)
+    scratch += [pltpu.SemaphoreType.DMA((count,))] * 2 + [pltpu.SemaphoreType.DMA((7 + groups,))]
     return pl.pallas_call(
-        functools.partial(reduce_kernel, narrow, length, groups),
-        grid=(heads,),
+        functools.partial(reduce_kernel, narrow, length, groups, deep),
+        grid=(2 * heads,),
         in_specs=[
-            pl.BlockSpec((rows, width), lambda h: (0, 0), pipeline_mode=pl.Buffered(1)),
-            head, head, head, pair, pair, pl.BlockSpec((width, GROUP), lambda h: (0, h)), one, one, one,
-            pl.BlockSpec((16, width), lambda h: (0, 0), pipeline_mode=pl.Buffered(1)),
+            fixed((rows, width)), head, head, head, pair, pair, later, one, one, one, fixed((16, width)),
             hbm, hbm, hbm, hbm,
         ],
-        out_specs=[
-            pl.BlockSpec((rows, width), lambda h: (0, 0), pipeline_mode=pl.Buffered(1)),
-            hbm, hbm, hbm,
-            pl.BlockSpec((16, width), lambda h: (0, 0)),
-            pl.BlockSpec((8, LANES), lambda h: (0, 0)),
-        ],
+        out_specs=[fixed((rows, width)), hbm, hbm, hbm, hbm, fixed((16, width)), fixed((8, LANES))],
         out_shape=[
             shape((rows, width), BF16),
+            shape((share, inner), BF16),
+            shape((share, width), BF16),
             shape((deep, width), BF16),
-            shape((share, ecols), BF16),
             shape((share, heads * GROUP), BF16),
             shape((16, width), F32),
             shape((8, LANES), F32),
@@ -1016,16 +1135,12 @@
             vmem_limit_bytes=VMEM_LIMIT, collective_id=1, has_side_effects=True
         ),
         name="reduce",
-    )(x, q, kv, aug, gc, ctx, wp, ka, km, word, gvec, gr1, gw1, gwo, gw2)
+    )(x, q, kv, aug, gc, ctx, wp, ka, km, word, gvec, gr1, t1, tw, gwo)
 
 
 def gelu_pair(pre):
-    size = jnp.abs(pre) * (0.5**0.5)
     bell = jnp.exp2(pre * pre * (-0.5 * LOG2E))
-    t = 1.0 / (1.0 + 0.3275911 * size)
-    poly = t * (0.254829592 + t * (-0.284496736 + t * (1.421413741 + t * (-1.453152027 + t * 1.061405429))))
-    tail = 0.5 * poly * bell
-    share = jnp.where(pre >= 0, 1.0 - tail, tail)
+    share = 0.5 + 0.5 * lax.erf(pre * (0.5**0.5))
     return pre * share, share + pre * bell * 0.3989422804014327
 
 
@@ -1035,149 +1150,227 @@
 
 
 def middle_kernel(
-    tiles, x_ref, ctx_ref, cot_ref, vec_ref, e_hbm, w2_hbm,
-    out_ref, gr1_ref, gctx_ref, gw2_ref, gw1_ref, gwo_ref, gvec_ref,
-    wo, w1, w2, h1_s, act_s, gb_s, gp_s, ga_s, ctx_s, dg_s, acc, sems,
+    narrow, x_hbm, ctx_hbm, cot_hbm, vec_ref, e_hbm, w2_hbm,
+    out_hbm, gr1_hbm, gctx_hbm, gw1_hbm, gwo_hbm, gw2_hbm, gvec_ref,
+    wo, w1, w2, io, ctx, h1_s, n1_s, inv_s, act_s, slope_s, gb_s, sum_s, gw2_s, gwo_s, acc, sems, *scratch,
 ):
-    step = pl.program_id(0)
-    size, width = x_ref.shape
+    rows, width = io.shape
     inner = w1.shape[1]
-    chunks = inner // width
-
-    def weight_copies(index):
+    blocks, size, block = inner // width, 256, 256
+    red = None
+
+    def load(index):
         source, target = (
+            (x_hbm, io),
+            (ctx_hbm, ctx),
             (e_hbm.at[:, inner : inner + width], wo),
             (e_hbm.at[:, 0:inner], w1),
             (w2_hbm, w2),
+            (cot_hbm, io),
         )[index]
         return pltpu.make_async_copy(source, target, sems.at[index])
 
-    @pl.when(step == 0)
-    def _():
-        for index in range(3):
-            weight_copies(index).start()
-        acc[...] = jnp.zeros_like(acc)
+    def store(index):
+        source, target = (
+            (io, out_hbm),
+            (sum_s, gr1_hbm),
+            (io, gctx_hbm),
+            (gwo_s, gwo_hbm),
+            (gw2_s, gw2_hbm) if red is None else (chunk.total.at[:, chunk.cut(here.wide)[0], :], gw2_hbm),
+            (act_s.at[0:width, :] if red is None else chunk_1.total, gw1_hbm),
+        )[index]
+        return pltpu.make_async_copy(source, target, sems.at[6 + index])
 
     def vec(row):
         return vec_ref[row : row + 1, :].astype(F32)
 
-    @pl.when(step < tiles)
-    def _():
-        here = pl.ds(pl.multiple_of(step * size, size), size)
-
-        @pl.when(step == 0)
-        def _():
-            weight_copies(0).wait()
-
-        ctx_s[here, :] = ctx_ref[...]
-        resid = x_ref[...].astype(F32) + mm(ctx_ref[...], wo[...]) + vec(5)
+    def over_rows(step):
+        def one(i, carry):
+            step(spot(i * size, size, size))
+            return carry
+
+        lax.fori_loop(0, rows // size, one, 0)
+
+    def over_cols(first, last, step):
+        def one(i, carry):
+            step(spot(i * block, block, block), i)
+            return carry
+
+        lax.fori_loop(first, last, one, 0)
+
+    for index in (1, 2, 0, 3, 4):
+        load(index).start()
+    acc[...] = jnp.zeros_like(acc)
+    if narrow is not None:
+        here = Place(narrow)
+        red = Reducer(here, scratch[0], scratch[1])
+        deep, share = scratch[2].shape[1], scratch[7].shape[1]
+        chunk = Chunk("w", True, (deep, width), scratch[2], scratch[3:7])
+        chunk_1 = Chunk("1", False, (share, inner), scratch[7])
+        here.greet()
+
+        def sources(owner):
+            return [(gw2_s.at[spot(owner * deep, deep, 16), :], slice(0, width))]
+
+        def sources_1(owner):
+            return [(act_s.at[spot(owner * share, share, 16), :], slice(0, inner))]
+
+    for index in (1, 2, 0):
+        load(index).wait()
+
+    def norm_one(at):
+        resid = io[at, :].astype(F32) + mm(ctx[at, :], wo[...]) + vec(5)
         center = resid - jnp.mean(resid, axis=1, keepdims=True)
-        inv1 = lax.rsqrt(jnp.mean(center * center, axis=1, keepdims=True) + norm_eps)
-        n1 = center * inv1
-        h1 = n1 * vec(6) + vec(7)
-        h1b = h1.astype(BF16)
-        h1_s[here, :] = h1b
-
-        @pl.when(step == 0)
-        def _():
-            weight_copies(1).wait()
-            weight_copies(2).wait()
-
-        branch = h1 + vec(8)
-        for c in range(chunks):
-            cols = slice(c * width, (c + 1) * width)
-            act, slope = gelu_pair(mm(h1b, w1[:, cols]) + vec(11 + c))
-            act = act.astype(BF16)
-            act_s[here, cols] = act
-            dg_s[:, cols] = slope
-            branch = branch + mm(act, w2[cols, :])
-        center = branch - jnp.mean(branch, axis=1, keepdims=True)
-        inv2 = lax.rsqrt(jnp.mean(center * center, axis=1, keepdims=True) + norm_eps)
-        n2 = center * inv2
-        out_ref[...] = (n2 * vec(9) + vec(10)).astype(BF16)
-        grad = cot_ref[...].astype(F32)
-        gn = grad * n2
-        acc[9] += fold(gn)
+        inverse = lax.rsqrt(jnp.mean(center * center, axis=1, keepdims=True) + norm_eps)
+        unit = center * inverse
+        hidden = unit * vec(6) + vec(7)
+        n1_s[at, :] = unit.astype(BF16)
+        inv_s[at, :] = jnp.broadcast_to(inverse, (size, LANES))
+        h1_s[at, :] = hidden.astype(BF16)
+        sum_s[at, :] = hidden + vec(8)
+
+    over_rows(norm_one)
+    load(5).start()
+    load(3).wait()
+    per = width // block
+
+    def expand(at, i):
+        bias = vec_ref[11 + i // per, spot(lax.rem(i, per) * block, block, LANES)].astype(F32).reshape(1, block)
+        act, slope = gelu_pair(mm(h1_s[...], w1[:, at]) + bias)
+        act_s[:, at] = act.astype(BF16)
+        slope_s[:, at] = slope.astype(BF16)
+
+    over_cols(0, inner // block, expand)
+    load(4).wait()
+
+    def reduce(at, i):
+        sum_s[:, at] += mm(act_s[...], w2[:, at])
+
+    over_cols(0, per, reduce)
+    load(5).wait()
+
+    def norm_two(at):
+        resid = sum_s[at, :]
+        center = resid - jnp.mean(resid, axis=1, keepdims=True)
+        inverse = lax.rsqrt(jnp.mean(center * center, axis=1, keepdims=True) + norm_eps)
+        unit = center * inverse
+        grad = io[at, :].astype(F32)
+        io[at, :] = (unit * vec(9) + vec(10)).astype(BF16)
+        acc[9] += fold(grad * unit)
         acc[10] += fold(grad)
         scaled = grad * vec(9)
-        gr2 = inv2 * (
+        back = inverse * (
             scaled
             - jnp.mean(scaled, axis=1, keepdims=True)
-            - n2 * jnp.mean(scaled * n2, axis=1, keepdims=True)
+            - unit * jnp.mean(scaled * unit, axis=1, keepdims=True)
         )
-        gb = gr2.astype(BF16)
-        gb_s[here, :] = gb
-        acc[8] += fold(gb.astype(F32))
-        gh1 = gr2
-        for c in range(chunks):
-            cols = slice(c * width, (c + 1) * width)
-            gpre = (mm_nt(gb, w2[cols, :]) * dg_s[:, cols]).astype(BF16)
-            gp_s[here, cols] = gpre
-            acc[11 + c] += fold(gpre.astype(F32))
-            gh1 = gh1 + mm_nt(gpre, w1[:, cols])
-        acc[6] += fold(gh1 * n1)
-        acc[7] += fold(gh1)
-        scaled = gh1 * vec(6)
-        gr1 = inv1 * (
+        sum_s[at, :] = back
+        half = back.astype(BF16)
+        gb_s[at, :] = half
+        acc[8] += fold(half.astype(F32))
+
+    over_rows(norm_two)
+    store(0).start()
+    for z in range(blocks):
+        cols = slice(z * width, (z + 1) * width)
+        gw2_s[cols, :] = mm_tn(act_s[:, cols], gb_s[...]).astype(BF16)
+        if red is not None:
+            red.pair_send(chunk, sources, z)
+
+    def expand_back(at, i):
+        grad = (mm_nt(gb_s[...], w2[at, :]) * slope_s[:, at].astype(F32)).astype(BF16)
+        slope_s[:, at] = grad
+        row = 11 + i // per
+        cols = spot(lax.rem(i, per) * block, block, LANES)
+        acc[row, :, cols] = acc[row, :, cols] + fold(grad.astype(F32))
+
+    def hidden_back(at, i):
+        sum_s[:, at] += mm_nt(slope_s[...], w1[at, :])
+
+    def norm_one_back(at):
+        grad, unit = sum_s[at, :], n1_s[at, :].astype(F32)
+        acc[6] += fold(grad * unit)
+        acc[7] += fold(grad)
+        scaled = grad * vec(6)
+        back = inv_s[at, 0:1] * (
             scaled
             - jnp.mean(scaled, axis=1, keepdims=True)
-            - n1 * jnp.mean(scaled * n1, axis=1, keepdims=True)
+            - unit * jnp.mean(scaled * unit, axis=1, keepdims=True)
         )
-        gr1_ref[...] = gr1
-        ga = gr1.astype(BF16)
-        ga_s[here, :] = ga
-        acc[5] += fold(ga.astype(F32))
-        gctx_ref[...] = mm_nt(ga, wo[...]).astype(BF16)
-
-    for c in range(chunks):
+        sum_s[at, :] = back
+        half = back.astype(BF16)
+        gb_s[at, :] = half
+        acc[5] += fold(half.astype(F32))
+
+    def merge(target, source, size):
+        def one(z, carry):
+            mine = spot((2 * z + here.core) * size, size, 16)
+            target[z] = target[z] + source[mine, :]
+            return carry
+
+        lax.fori_loop(0, here.depth, one, 0)
+
+    count = inner // block
+    over_cols(0, count // 3, expand_back)
+    if red is not None:
+        red.pair_wait(chunk, sources)
+        merge(chunk.total, gw2_s, deep)
+        red.plane_send(chunk)
+    over_cols(count // 3, count, expand_back)
+    for c in range(blocks):
         cols = slice(c * width, (c + 1) * width)
-
-        @pl.when(step == tiles + c)
-        def _():
-            gw2_ref[...] = mm_tn(act_s[:, cols], gb_s[...]).astype(BF16)
-
-        @pl.when(step == tiles + chunks + c)
-        def _():
-            gw1_ref[...] = mm_tn(h1_s[...], gp_s[:, cols]).astype(BF16)
-
-    @pl.when(step == tiles + 2 * chunks)
-    def _():
-        gwo_ref[...] = mm_tn(ctx_s[...], ga_s[...]).astype(BF16)
-        for row in range(acc.shape[0]):
-            gvec_ref[row : row + 1, :] = jnp.sum(acc[row], axis=0, keepdims=True)
-
-
-def middle_call(x, ctx, cot, vec, e, w2, size):
+        act_s[0:width, cols] = mm_tn(h1_s[...], slope_s[:, cols]).astype(BF16)
+    if red is not None:
+        red.pair_send(chunk_1, sources_1)
+    over_cols(0, per, hidden_back)
+    if red is not None:
+        red.plane_turn(chunk)
+        red.pair_wait(chunk_1, sources_1)
+        merge(chunk_1.total, act_s, share)
+    store(5).start()
+    over_rows(norm_one_back)
+    store(1).start()
+    store(0).wait()
+    io[...] = mm_nt(gb_s[...], wo[...]).astype(BF16)
+    store(2).start()
+    gwo_s[...] = mm_tn(ctx[...], gb_s[...]).astype(BF16)
+    store(3).start()
+    for row in range(acc.shape[0]):
+        gvec_ref[row : row + 1, :] = jnp.sum(acc[row], axis=0, keepdims=True)
+    if red is not None:
+        red.plane_done(chunk)
+    store(4).start()
+    if red is not None:
+        red.finish()
+    for index in range(1, 6):
+        store(index).wait()
+
+
+def middle_call(narrow, x, ctx, cot, vec, e, w2):
     rows, width = x.shape
     inner = w2.shape[0]
-    tiles, chunks = rows // size, inner // width
-    tile = pl.BlockSpec((size, width), lambda i: (jnp.minimum(i, tiles - 1), 0))
-    hbm = pl.BlockSpec(memory_space=pl.ANY)
-
-    def after(start):
-        return lambda i: jnp.clip(i - start, 0, chunks - 1)
-
+    hbm, vmem = pl.BlockSpec(memory_space=pl.ANY), pl.BlockSpec(memory_space=pltpu.VMEM)
     shape = jax.ShapeDtypeStruct
+    scratch, params = [], {}
+    shape_w, shape_1 = (inner, width), (width, inner)
+    if narrow is not None:
+        depth, deep, share = narrow // 2, inner // narrow, width // narrow
+        shape_w, shape_1 = (depth, deep // 4, width), (depth, share, inner)
+        scratch = [pltpu.SemaphoreType.DMA((2 * depth + 6,))] * 2
+        scratch += [pltpu.VMEM((depth, deep, width), BF16), *plane_scratch(depth, deep, width, True)]
+        scratch += [pltpu.VMEM((depth, share, inner), BF16)]
+        params = dict(collective_id=2, has_side_effects=True)
     return pl.pallas_call(
-        functools.partial(middle_kernel, tiles),
-        grid=(tiles + 2 * chunks + 1,),
-        in_specs=[tile, tile, tile, pl.BlockSpec(vec.shape, lambda i: (0, 0)), hbm, hbm],
-        out_specs=[
-            tile,
-            tile,
-            tile,
-            pl.BlockSpec((width, width), lambda i: (after(tiles)(i), 0)),
-            pl.BlockSpec((width, width), lambda i: (0, after(tiles + chunks)(i))),
-            pl.BlockSpec((width, width), lambda i: (0, 0)),
-            pl.BlockSpec(vec.shape, lambda i: (0, 0)),
-        ],
+        functools.partial(middle_kernel, narrow),
+        in_specs=[hbm, hbm, hbm, vmem, hbm, hbm],
+        out_specs=[hbm] * 6 + [vmem],
         out_shape=[
             shape((rows, width), BF16),
             shape((rows, width), F32),
             shape((rows, width), BF16),
-            shape((inner, width), BF16),
-            shape((width, inner), BF16),
+            shape(shape_1, BF16),
             shape((width, width), BF16),
+            shape(shape_w, BF16),
             shape(vec.shape, F32),
         ],
         scratch_shapes=[
@@ -1185,16 +1378,21 @@
             pltpu.VMEM((width, inner), BF16),
             pltpu.VMEM((inner, width), BF16),
             pltpu.VMEM((rows, width), BF16),
+            pltpu.VMEM((rows, width), BF16),
+            pltpu.VMEM((rows, width), BF16),
+            pltpu.VMEM((rows, width), BF16),
+            pltpu.VMEM((rows, LANES), F32),
+            pltpu.VMEM((rows, inner), BF16),
             pltpu.VMEM((rows, inner), BF16),
             pltpu.VMEM((rows, width), BF16),
-            pltpu.VMEM((rows, inner), BF16),
-            pltpu.VMEM((rows, width), BF16),
-            pltpu.VMEM((rows, width), BF16),
-            pltpu.VMEM((size, inner), F32),
+            pltpu.VMEM((rows, width), F32),
+            pltpu.VMEM((inner, width), BF16),
+            pltpu.VMEM((width, width), BF16),
             pltpu.VMEM((vec.shape[0], 8, width), F32),
-            pltpu.SemaphoreType.DMA((3,)),
+            pltpu.SemaphoreType.DMA((12,)),
+            *scratch,
         ],
-        compiler_params=pltpu.CompilerParams(vmem_limit_bytes=VMEM_LIMIT),
+        compiler_params=pltpu.CompilerParams(vmem_limit_bytes=VMEM_LIMIT, **params),
         name="middle",
     )(x, ctx, cot, vec, e, w2)
 
@@ -1239,7 +1437,7 @@
     return weight, first, second, weight.astype(BF16)
 
 
-def update_kernel(narrow, n_ref, fa_ref, fe_ref, fw_ref, v_ref, *refs):
+def update_kernel(narrow, n_ref, fa_ref, fo_ref, f1_ref, fw_ref, v_ref, *refs):
     ins, outs = refs[0:15], refs[15:35]
     heads = fa_ref.shape[1] // GROUP
     width = heads * HEAD
@@ -1265,9 +1463,8 @@
                     grad = jnp.where(low, even, swap_halves(odd))
                 start = (2 * b + second) * width + pair * LANES
                 store(0, every, slice(start, start + LANES), grad)
-    inner = ins[2].shape[1]
-    store(1, every, every, fe_ref[:, inner : inner + width])
-    store(2, every, every, fe_ref[:, 0:inner])
+    store(1, every, every, fo_ref[...])
+    store(2, every, every, f1_ref[...])
     store(3, every, every, fw_ref[...])
 
     @pl.when(pl.program_id(0) == 0)
@@ -1278,8 +1475,8 @@
         store(4, every, every, turned[0:count, 0:span])
 
 
-def update_call(narrow, norm, fa, fe, fw, vec, masters, firsts, seconds):
-    share = fa.shape[0]
+def update_call(narrow, norm, shards, vec, masters, firsts, seconds):
+    share = shards[0].shape[0]
     steps = share // 16
 
     def rows_of(array_in):
@@ -1297,12 +1494,12 @@
     return pl.pallas_call(
         functools.partial(update_kernel, narrow),
         grid=(steps,),
-        in_specs=[fixed(norm), rows_of(fa), rows_of(fe), rows_of(fw), fixed(vec)] + group(masters) * 3,
+        in_specs=[fixed(norm), *(rows_of(a) for a in shards), fixed(vec)] + group(masters) * 3,
         out_specs=group(masters) * 4,
         out_shape=shapes(masters, F32) * 3 + shapes(masters, BF16),
         compiler_params=pltpu.CompilerParams(vmem_limit_bytes=VMEM_LIMIT),
         name="update",
-    )(norm, fa, fe, fw, vec, *masters, *firsts, *seconds)
+    )(norm, *shards, vec, *masters, *firsts, *seconds)
 
 
 def by_head(array_in):
@@ -1319,7 +1516,7 @@
 
 def can_pass_pieces(wide, narrow, width, deep):
     share = width // narrow
-    return wide == 4 and narrow % 2 == 0 and narrow > 2 and share % 32 == 0 and deep % 128 == 0
+    return wide == 4 and narrow % 2 == 0 and narrow > 2 and share % 32 == 0 and deep % 128 == 0 and 2 * deep == width
 
 
 def body(
@@ -1361,19 +1558,20 @@
         vec_rows = jnp.pad(vec_half.astype(F32), ((0, 1), (0, 0)))
         query, keyval = qkv_call(hidden, proj_w, bias, word)
         context, aug = attend_call(query, keyval, qaug, kaug, kmask, seq_len)
-    block_out, grad_r1, grad_context, grad_reduce, grad_expand, grad_ctx_w, grad_mid = middle_call(
-        hidden, context, cot, vec_rows, mid_w, reduce_w, 256
+    block_out, grad_r1, grad_context, grad_expand, grad_ctx_w, grad_reduce, grad_mid = middle_call(
+        narrow if pieces else None, hidden, context, cot, vec_rows, mid_w, reduce_w
     )
     masters = (projection, context_out, expand_weight, reduce_weight, vector_params)
     firsts = (first_projection, first_context, first_expand, first_reduce, first_vectors)
     seconds = (second_projection, second_context, second_expand, second_reduce, second_vectors)
     out_shape = (seq_count, seq_len, width)
     if pieces:
-        input_grad, shard_w, shard_e, shard_a, grad_vectors, norm = reduce_call(
+        input_grad, shard_1, shard_o, shard_w, shard_a, grad_vectors, norm = reduce_call(
             narrow, hidden, query, keyval, aug, grad_context, context, proj_w, kaug, kmask, word, grad_mid,
-            grad_r1, grad_expand, grad_ctx_w, grad_reduce, seq_len,
+            grad_r1, grad_expand, grad_reduce, grad_ctx_w, reduce_weight.shape[0], seq_len,
         )
-        updated = update_call(narrow, norm, shard_a, shard_e, shard_w, grad_vectors, masters, firsts, seconds)
+        shards = (shard_a, shard_o, shard_1, shard_w)
+        updated = update_call(narrow, norm, shards, grad_vectors, masters, firsts, seconds)
         return (
             block_out.reshape(out_shape),
             input_grad.reshape(out_shape),

time: 334 us -> 300 us (0.90)
  Pallas kernels: 325 us -> 288 us
    pallas_call x2, Pallas kernels: 217 us -> 177 us  [the longest x1 107 us: reduce_call(): pl.pallas_call(functools.partial(reduce_kernel, narrow, length, groups, d...]
where the time goes in v1:
time: 300 us; the launch traced here: 296 us
  Pallas kernels  288 us (96%)
  local copies, waits for them, and re-layouts  4.71 us (2%)
    pallas_call x1, Pallas kernels, reduce_call(): pl.pallas_call(functools.partial(reduce_kernel, narrow, length, groups, d...  107 us
    pallas_call x1, Pallas kernels, gather_call(): pl.pallas_call(functools.partial(gather_kernel, narrow), in_specs=[vmem]...  95.9 us
    pallas_call x1, Pallas kernels, middle_call(): pl.pallas_call(functools.partial(middle_kernel, narrow), in_specs=[hbm, h...  70.1 us
    pallas_call x1, Pallas kernels, update_call(): pl.pallas_call(functools.partial(update_kernel, narrow), grid=(steps,), i...  14.9 us

profile of v1, /device:TPU:0, one launch (start us, length us, event | category | flops | bytes accessed | tf_op | source)
XLA Modules:
  0.0 295.7 jit_solution(12438424881928275165)
XLA Ops:
  0.7 95.9 %gather.1 = (bf16[1280,1536]{1,0:T(8,128)(2,1)}, bf16[1280,1536]{1,0:T(8,128)(2,1)}, bf16[1280,768]{1,0:T(8,128)(2,1)}, bf16[1280,1536]{1,0:T(8,128)(2,1)}, bf16...) custom-call(bf16[1280,768]{1,0:T(8,128)(2,1)} %bitcast.5, ...), custom_call_target="tpu_custom_call" | custom-call | tf_op jit(solution)/shard_map/gather/pallas_call | solution.py:522
  96.5 70.1 %middle.1 = (bf16[1280,768]{1,0:T(8,128)(2,1)}, f32[1280,768]{1,0:T(8,128)}, bf16[1280,768]{1,0:T(8,128)(2,1)}, bf16[4,96,3072]{2,1,0:T(8,128)(2,1)}, bf16[768,7...) custom-call(bf16[1280,768]{1,0:T(8,128)(2,1)} %bitcast.6, ...), custom_call_target="tpu_custom_call" | custom-call | tf_op jit(solution)/shard_map/middle/pallas_call | solution.py:1363
  166.6 107.4 %reduce.1 = (bf16[1280,768]{1,0:T(8,128)(2,1)}, bf16[96,3072]{1,0:T(8,128)(2,1)}, bf16[96,768]{1,0:T(8,128)(2,1)}, bf16[384,768]{1,0:T(8,128)(2,1)}, bf16[96,460...) custom-call(bf16[1280,768]{1,0:T(8,128)(2,1)} %bitcast.7, bf16[1280,1536]{1,0:T(8,128)(2,1)} %get-tuple-element.73.q_ref, ...), custom_call_target="tpu_custom_call" | custom-call | tf_op jit(solution)/shard_map/reduce/pallas_call | solution.py:1116
  274.0 1.2 slice.3
  275.9 0.0 copy-start
  275.9 14.9 %update.1 = (f32[96,4608]{1,0:T(8,128)}, f32[96,768]{1,0:T(8,128)}, f32[96,3072]{1,0:T(8,128)}, f32[384,768]{1,0:T(8,128)}, f32[15,96]{1,0:T(8,128)}, /*index=5*...) custom-call(f32[8,128]{1,0:T(8,128)} %get-tuple-element.87.n_ref, ...), custom_call_target="tpu_custom_call" | custom-call | tf_op jit(solution)/shard_map/update/pallas_call | solution.py:1494
  290.8 0.0 copy-done
  290.8 0.0 copy-start.1
  290.8 1.3 copy.44
  292.1 1.0 copy-done.1
  293.1 1.3 copy.45
Async XLA Ops:
  275.9 14.9 %copy-start = (bf16[1280,768]{1,0:T(8,128)(2,1)S(1)}, bf16[1280,768]{1,0:T(8,128)(2,1)}, u32[]{:S(2)}) copy-start(bf16[1280,768]{1,0:T(8,128)(2,1)} %get-tuple-element.72) | copy-start | bytes 5898244
  290.8 2.3 copy-start.1

commit v2 on v1

--- a/solution.py
+++ b/solution.py
@@ -149,6 +149,7 @@
         self.d_quarter = lax.rem(self.x_quarter + 2, 4)
         self.sib = self.me + 1 - 2 * self.core
         self.x_dev, self.y_dev = {"wide": self.x_quarter}, {"wide": self.y_quarter}
+        self.d_dev = {"wide": self.d_quarter}
         self.sib_dev = {"narrow": self.sib}
 
     def ahead(self, k):
@@ -188,7 +189,7 @@
 
     def greet(self):
         barrier = pltpu.get_barrier_semaphore()
-        partners = [self.x_dev, self.y_dev, self.sib_dev] + [self.z_dev(k) for k in range(1, self.depth)]
+        partners = [self.x_dev, self.y_dev, self.d_dev, self.sib_dev] + [self.z_dev(k) for k in range(1, self.depth)]
         for device in partners:
             pl.semaphore_signal(barrier, inc=1, device_id=device, device_id_type=pl.DeviceIdType.MESH)
         pl.semaphore_wait(barrier, len(partners))
@@ -257,6 +258,8 @@
                 lambda way=way: (own_part(kind, here.wide), region(kind, me, here.wide), here.next_dev(way)),
                 ahead,
             )
+            if kind == "a":
+                continue
             links.send(
                 (kind, "h", way, 1),
                 lambda way=way: (
@@ -286,39 +289,51 @@
                 relay((kind, "x", way, hop), piece, lambda: here.x_dev, comes)
                 relay((kind, "y", way, hop), piece, lambda: here.y_dev, comes)
             relay((kind, "sz", way, hop), piece, lambda: here.sib_dev, comes)
-            if kind != "v":
+            if kind not in "va":
                 other = lambda way=way: region(kind, here.origin(way, hop), here.d_quarter, 0)
                 receive((kind, "h", way, hop), other, comes)
                 if hop + 1 < here.depth:
                     relay((kind, "h", way, hop + 1), other, onward, comes, ahead)
                 relay((kind, "sh", way, hop), other, lambda: here.sib_dev, comes)
 
-    def by_x(kind, hop):
-        return kind == "a" or (kind == "w" and hop % 2 == 1)
+    def diagonal(kind, hop):
+        by_y, by_x = ("x", 0 if kind == "a" else 1, here.y_dev), ("y", 1, here.x_dev)
+        if kind == "a":
+            return [by_y, by_x]
+        return [by_x if (kind == "e") == (hop % 2 == 1) else by_y]
 
     def pass_xy(kind, hop):
         for way in range(2):
             comes = here.comes(way, hop)
-            for name, part, back in (("x", here.x_quarter, "y"), ("y", here.y_quarter, "x")):
+            for name, part in (("x", here.x_quarter), ("y", here.y_quarter)):
                 piece = lambda way=way, part=part: region(kind, here.origin(way, hop), part)
                 receive((kind, name, way, hop), piece, comes)
-                if by_x(kind, hop) == (back == "x"):
-                    device = here.x_dev if back == "x" else here.y_dev
-                    rest = lambda way=way, part=part: region(kind, here.origin(way, hop), part, 1)
-                    relay((kind, "d", way, hop), rest, lambda device=device: device, comes)
+                for back, side, device in diagonal(kind, hop):
+                    if back == name:
+                        rest = lambda way=way, part=part, side=side: region(kind, here.origin(way, hop), part, side)
+                        relay((kind, "d", side, way, hop), rest, lambda device=device: device, comes)
                 relay((kind, "s" + name, way, hop), piece, lambda: here.sib_dev, comes)
 
-    def pass_d(kind):
-        for way, hop in routes:
-            comes = here.comes(way, hop)
-            rest = lambda way=way, hop=hop: region(kind, here.origin(way, hop), here.d_quarter, 1)
-            receive((kind, "d", way, hop), rest, comes)
-            relay((kind, "sd", way, hop), rest, lambda: here.sib_dev, comes)
+    def pass_d(kind, number):
+        for way in range(2):
+            comes = here.comes(way, number)
+            for _, side, _ in diagonal(kind, number):
+                rest = lambda way=way, side=side: region(kind, here.origin(way, number), here.d_quarter, side)
+                receive((kind, "d", side, way, number), rest, comes)
+                relay((kind, "sd", side, way, number), rest, lambda: here.sib_dev, comes)
 
     def from_sib(kind, name, part, side=None):
+        if name == "sd":
+            for side in range(2):
+                if kind == "a" or side == 1:
+                    from_sib(kind, ("sd", side), part, side)
+                else:
+                    from_sib(kind, "sh", part, side)
+            return
+        name = name if isinstance(name, tuple) else (name,)
         for way, hop in routes:
             piece = lambda way=way, hop=hop: region(kind, here.origin(way, hop, True), part, side)
-            receive((kind, name, way, hop), piece, here.comes(way, hop))
+            receive((kind, *name, way, hop), piece, here.comes(way, hop))
 
     low = low_lanes(share)
     for pair in range(heads // 2):
@@ -375,6 +390,7 @@
         if number < here.depth:
             pass_xy(kind, number)
 
+    deeper = range(4, here.depth)
     hop("a", 1)
     hop("a", 2)
     send_z("e")
@@ -382,17 +398,9 @@
     turn("a", 1)
     hop("a", 3)
     turn("a", 2)
-    hop("e", 1)
-    turn("a", 3)
-    for number in range(4, here.depth):
+    for number in deeper:
         hop("a", number)
-        turn("a", number)
-    hop("e", 2)
-    send_z("w")
-    send_own("w")
-    hop("e", 3)
-    for number in range(4, here.depth):
-        hop("e", number)
+        turn("a", number - 1)
 
     links.arrived(("v", "o"), v_all.at[here.sib], here.sib_dev)
     for way, number in routes:
@@ -444,65 +452,76 @@
 
     from_sib("a", "sz", here.wide)
     project(0, here.wide)
-    turn("e", 1)
-    pass_d("a")
+    hop("e", 1)
+    turn("a", here.depth - 1)
     from_sib("a", "sx", here.x_quarter)
     project(1, here.x_quarter)
-    hop("w", 1)
-    turn("e", 2)
-    hop("w", 2)
+    for number in hops:
+        pass_d("a", number)
+    hop("e", 2)
+    send_z("w")
+    send_own("w")
+    turn("e", 1)
     from_sib("a", "sy", here.y_quarter)
     project(2, here.y_quarter)
-    turn("e", 3)
-    hop("w", 3)
-    for number in range(4, here.depth):
-        turn("e", number)
-        hop("w", number)
-    from_sib("a", "sh", here.d_quarter, 0)
-    from_sib("a", "sd", here.d_quarter, 1)
+    hop("e", 3)
+    from_sib("a", "sd", here.d_quarter)
     project(3, here.d_quarter)
     copy_a = pltpu.make_async_copy(a_full, a_out, local.at[10])
     copy_a.start()
     low_seq = low_lanes(length)
     per = quarter // GROUP
 
-    def attend(pair):
-        for seq in range(seg_ref.shape[0]):
-            at = slice(seq * length, (seq + 1) * length)
-            contexts = []
-            for head in (2 * pair, 2 * pair + 1):
-                cols = slice(head % per * LANES, (head % per + 1) * LANES)
-                context, extra = attend_head(
-                    q_s[head // per, at, cols], kv_s[head // per, at, cols], qa_ref[at], ka_ref[at], km_ref[at]
-                )
-                aug_s[at, head * LANES : (head + 1) * LANES] = extra
-                contexts.append(context)
-            both = jnp.where(low_seq, swap_halves(contexts[0]), contexts[1])
-            ctx_s[at, pair * LANES : (pair + 1) * LANES] = both.astype(BF16)
+    def attend(pair, seq):
+        at = slice(seq * length, (seq + 1) * length)
+        contexts = []
+        for head in (2 * pair, 2 * pair + 1):
+            cols = slice(head % per * LANES, (head % per + 1) * LANES)
+            context, extra = attend_head(
+                q_s[head // per, at, cols], kv_s[head // per, at, cols], qa_ref[at], ka_ref[at], km_ref[at]
+            )
+            aug_s[at, head * LANES : (head + 1) * LANES] = extra
+            contexts.append(context)
+        both = jnp.where(low_seq, swap_halves(contexts[0]), contexts[1])
+        ctx_s[at, pair * LANES : (pair + 1) * LANES] = both.astype(BF16)
+
+    def attended(pair):
         for number, (source, target, wide) in enumerate(((ctx_s, ctx_out, LANES), (aug_s, aug_out, 2 * LANES))):
             cols = slice(pair * wide, (pair + 1) * wide)
             copy = pltpu.make_async_copy(source.at[:, cols], target.at[:, cols], local.at[11 + 2 * pair + number])
             copy.start()
             outs.append(copy)
 
+    def later(kind, first, last):
+        for number in range(first, last):
+            turn(kind, number)
+
     between = [
-        lambda: [pass_d("e"), turn("w", 1)],
-        lambda: turn("w", 2),
-        lambda: [turn("w", number) for number in range(3, here.depth)],
-        lambda: pass_d("w"),
+        lambda: [turn("e", 2), pass_d("e", 1)],
+        lambda: hop("w", 1),
+        lambda: [turn("e", 3), pass_d("e", 2)],
+        lambda: [hop("w", 2), [hop("e", number) for number in deeper], later("e", 4, here.depth)],
+        lambda: [turn("w", 1), [pass_d("e", number) for number in range(3, here.depth)]],
+        lambda: hop("w", 3),
+        lambda: [turn("w", 2), pass_d("w", 1)],
+        lambda: [hop("w", number) for number in deeper],
+        lambda: [later("w", 3, here.depth), pass_d("w", 2)],
+        lambda: [pass_d("w", number) for number in range(3, here.depth)],
     ]
-    for pair in range(heads // 2):
-        attend(pair)
-        if pair < len(between):
-            between[pair]()
-    for later in between[heads // 2 :]:
-        later()
+    units = [(pair, seq) for pair in range(heads // 2) for seq in range(seg_ref.shape[0])]
+    for index, (pair, seq) in enumerate(units):
+        attend(pair, seq)
+        if seq == seg_ref.shape[0] - 1:
+            attended(pair)
+        if index < len(between):
+            between[index]()
+    for action in between[len(units) :]:
+        action()
     for kind in ("e", "w"):
         links.arrived((kind, "o"), whole(kind, here.sib), here.sib_dev)
         for name, part in (("sz", here.wide), ("sx", here.x_quarter), ("sy", here.y_quarter)):
             from_sib(kind, name, part)
-        from_sib(kind, "sh", here.d_quarter, 0)
-        from_sib(kind, "sd", here.d_quarter, 1)
+        from_sib(kind, "sd", here.d_quarter)
     links.finish()
     for copy in (copy_e, copy_w, copy_a, *outs):
         copy.wait()
@@ -688,8 +707,8 @@
 
 
 class Chunk:
-    def __init__(self, name, by_rows, shape, total, plane=None, end=None):
-        self.name, self.by_rows = name, by_rows
+    def __init__(self, name, shape, total, plane=None, end=None):
+        self.name = name
         self.rows, self.cols = shape
         self.total = total
         if plane is not None:
@@ -697,42 +716,33 @@
         if end is not None:
             self.rz, self.final = end
 
+    def row_half(self, wide):
+        return spot(wide // 2 * (self.rows // 2), self.rows // 2, 16)
+
+    def col_half(self, wide):
+        return spot(lax.rem(wide, 2) * (self.cols // 2), self.cols // 2, LANES)
+
+    def quarter(self, wide):
+        return self.row_half(wide), self.col_half(wide)
+
     def mine(self, z, wide):
         if self.total.shape[1:] != (self.rows, self.cols):
             return self.total.at[z]
-        rows, cols = self.cut(wide)
-        return self.total.at[z, rows, cols]
-
-    def cut(self, part, side=None):
-        if self.by_rows:
-            size = self.rows // 4
-            if side is None:
-                return spot(part * size, size, 16), slice(None)
-            return spot(part * size + side * (size // 2), size // 2, 16), slice(None)
-        size, half = self.cols // 4, self.rows // 2
-        rows = slice(0, self.rows) if side is None else slice(side * half, (side + 1) * half)
-        return rows, spot(part * size, size, LANES)
-
-
-def piece_shapes(rows, cols, by_rows):
-    if by_rows:
-        return (rows // 4, cols), (rows // 8, cols)
-    return (rows, cols // 4), (rows // 2, cols // 4)
-
-
-def plane_scratch(depth, rows, cols, by_rows):
-    _, half = piece_shapes(rows, cols, by_rows)
+        return self.total.at[(z, *self.quarter(wide))]
+
+
+def plane_scratch(depth, rows, cols):
+    half = depth // 2
     return [
-        pltpu.VMEM((2, depth, *half), BF16),
-        pltpu.VMEM((2, depth, *half), BF16),
-        pltpu.VMEM((depth, *half), BF16),
-        pltpu.VMEM((depth, *half), BF16),
+        pltpu.VMEM((half, rows, cols // 2), BF16),
+        pltpu.VMEM((half, rows // 2, cols), BF16),
+        pltpu.VMEM((half, rows // 2, cols // 2), BF16),
+        pltpu.VMEM((half, rows // 2, cols // 2), BF16),
     ]
 
 
-def end_scratch(depth, rows, cols, by_rows):
-    piece, _ = piece_shapes(rows, cols, by_rows)
-    return [pltpu.VMEM((depth - 1, *piece), BF16), pltpu.VMEM((rows, cols), BF16)]
+def end_scratch(depth, rows, cols):
+    return [pltpu.VMEM((depth - 1, rows // 2, cols // 2), BF16), pltpu.VMEM((rows, cols), BF16)]
 
 
 class Reducer:
@@ -757,52 +767,43 @@
             for part, (_, cols) in enumerate(sources(0)):
                 self.arrived((chunk.name, "s", z, part), chunk.total.at[z, :, cols], self.here.sib_dev)
 
+    def lower(self):
+        return slice(0, self.here.depth // 2)
+
+    def upper(self):
+        return slice(self.here.depth // 2, self.here.depth)
+
     def plane_send(self, chunk):
         here = self.here
-        for index, (a, b) in enumerate(((here.x_quarter, here.y_quarter), (here.d_quarter, here.d_quarter))):
-
-            def first(index=index, part=a):
-                rows, cols = chunk.cut(part, 0)
-                return chunk.total.at[:, rows, cols], chunk.r1a.at[index], here.x_dev
-
-            def second(index=index, part=b):
-                rows, cols = chunk.cut(part, 1)
-                return chunk.total.at[:, rows, cols], chunk.r1b.at[index], here.y_dev
-
-            self.send((chunk.name, "1a", index), first)
-            self.send((chunk.name, "1b", index), second)
-
-    def add(self, chunk, part, side, value):
-        rows, cols = chunk.cut(part, side)
-        chunk.total[:, rows, cols] = chunk.total[:, rows, cols] + value
+        cols, rows = (lambda: chunk.col_half(here.x_quarter)), (lambda: chunk.row_half(here.y_quarter))
+        self.send((chunk.name, "1a"), lambda: (chunk.total.at[self.lower(), :, cols()], chunk.r1a, here.x_dev))
+        self.send((chunk.name, "1b"), lambda: (chunk.total.at[self.upper(), rows(), :], chunk.r1b, here.y_dev))
 
     def plane_turn(self, chunk):
         here = self.here
-        for index in range(2):
-            self.arrived((chunk.name, "1a", index), chunk.r1a.at[index], here.x_dev)
-            self.arrived((chunk.name, "1b", index), chunk.r1b.at[index], here.y_dev)
-        self.add(chunk, here.y_quarter, 0, chunk.r1a[1])
-        self.add(chunk, here.x_quarter, 1, chunk.r1b[1])
+        total = chunk.total
+        self.arrived((chunk.name, "1a"), chunk.r1a, here.x_dev)
+        self.arrived((chunk.name, "1b"), chunk.r1b, here.y_dev)
+        rows, cols = chunk.quarter(here.wide)
+        total[self.lower(), :, cols] = total[self.lower(), :, cols] + chunk.r1a[...]
+        total[self.upper(), rows, :] = total[self.upper(), rows, :] + chunk.r1b[...]
 
         def first():
-            rows, cols = chunk.cut(here.y_quarter, 0)
-            return chunk.total.at[:, rows, cols], chunk.r2a, here.y_dev
+            return total.at[(self.lower(), *chunk.quarter(here.y_quarter))], chunk.r2a, here.y_dev
 
         def second():
-            rows, cols = chunk.cut(here.x_quarter, 1)
-            return chunk.total.at[:, rows, cols], chunk.r2b, here.x_dev
+            return total.at[(self.upper(), *chunk.quarter(here.x_quarter))], chunk.r2b, here.x_dev
 
         self.send((chunk.name, "2a"), first)
         self.send((chunk.name, "2b"), second)
-        self.add(chunk, here.wide, 0, chunk.r1a[0])
-        self.add(chunk, here.wide, 1, chunk.r1b[0])
 
     def plane_done(self, chunk):
         here = self.here
         self.arrived((chunk.name, "2a"), chunk.r2a, here.y_dev)
         self.arrived((chunk.name, "2b"), chunk.r2b, here.x_dev)
-        self.add(chunk, here.wide, 0, chunk.r2a[...])
-        self.add(chunk, here.wide, 1, chunk.r2b[...])
+        rows, cols = chunk.quarter(here.wide)
+        for part, value in ((self.lower(), chunk.r2a), (self.upper(), chunk.r2b)):
+            chunk.total[part, rows, cols] = chunk.total[part, rows, cols] + value[...]
 
     def depth_send(self, chunk):
         here = self.here
@@ -818,48 +819,39 @@
         here = self.here
         for k in range(1, here.depth):
             self.arrived((chunk.name, "z", k), chunk.rz.at[k - 1], here.z_dev(k))
-        rows, cols = chunk.cut(here.wide)
         done = chunk.mine(here.z, here.wide)[...].astype(F32)
         for k in range(1, here.depth):
             done = done + chunk.rz[k - 1].astype(F32)
-        chunk.final[rows, cols] = done.astype(BF16)
+        done = done.astype(BF16)
+        rows, cols = chunk.quarter(here.wide)
+        chunk.final[rows, cols] = done
 
         def build(device):
-            rows, cols = chunk.cut(here.wide)
-            return chunk.final.at[rows, cols], chunk.final.at[rows, cols], device
-
-        self.send((chunk.name, "fx"), lambda: build(here.x_dev))
-        self.send((chunk.name, "fy"), lambda: build(here.y_dev))
-
-    def share_pass(self, chunk):
-        here = self.here
-
-        def part(quarter, side, device):
-            rows, cols = chunk.cut(quarter, side)
-            return chunk.final.at[rows, cols], chunk.final.at[rows, cols], device
-
-        self.arrived((chunk.name, "fx"), *part(here.x_quarter, None, here.x_dev)[1:])
-        self.send((chunk.name, "fdy"), lambda: part(here.x_quarter, 0, here.y_dev))
-        self.arrived((chunk.name, "fy"), *part(here.y_quarter, None, here.y_dev)[1:])
-        self.send((chunk.name, "fdx"), lambda: part(here.y_quarter, 1, here.x_dev))
+            piece = chunk.final.at[chunk.quarter(here.wide)]
+            return piece, piece, device
+
+        for name, device in (("fx", here.x_dev), ("fy", here.y_dev), ("fd", here.d_dev)):
+            self.send((chunk.name, name), lambda device=device: build(device))
+        return squares(done)
 
     def share_wait(self, chunk):
         here = self.here
-        for key, side, device in (("fdy", 0, here.y_dev), ("fdx", 1, here.x_dev)):
-            rows, cols = chunk.cut(here.d_quarter, side)
-            self.arrived((chunk.name, key), chunk.final.at[rows, cols], device)
-
-
-CHUNK_HEADS = 4
-
-
-def squares(ref, cols):
+        ways = (("fx", here.x_quarter, here.x_dev), ("fy", here.y_quarter, here.y_dev), ("fd", here.d_quarter, here.d_dev))
+        for name, quarter, device in ways:
+            self.arrived((chunk.name, name), chunk.final.at[chunk.quarter(quarter)], device)
+
+
+def squares(value):
     total = jnp.zeros((8, LANES), F32)
-    rows = ref.shape[0]
+    rows, cols = value.shape
     for start in range(0, cols, LANES):
-        tile = ref[:, start : start + LANES].astype(F32)
+        tile = value[:, start : start + LANES].astype(F32)
         total = total + jnp.sum((tile * tile).reshape(rows // 8, 8, LANES), axis=0)
     return total
+
+
+def head_groups(heads):
+    return (heads // 3, heads // 3, heads // 6, heads // 6)
 
 
 def reduce_kernel(
@@ -871,7 +863,7 @@
 ):
     step = pl.program_id(0)
     rows, width = x_ref.shape
-    heads = groups * CHUNK_HEADS
+    heads = sum(groups)
     share, inner = t1_ref.shape[1:]
     here = Place(narrow)
     scratch = list(scratch)
@@ -882,14 +874,15 @@
         taken, scratch[:count] = scratch[:count], []
         return taken
 
-    chunk_w = Chunk("w", True, (deep, width), take(1)[0], None, take(2))
-    chunk_1 = Chunk("1", False, (share, inner), take(1)[0], take(4), take(2))
+    chunk_w = Chunk("w", (deep, width), take(1)[0], None, take(2))
+    chunk_1 = Chunk("1", (share, inner), take(1)[0], take(4), take(2))
     gw, chunk_a = [], []
-    for j in range(groups):
+    for j in range(len(groups)):
         gw += take(1)
-        chunk_a.append(Chunk(("a", j), False, (share, gw[j].shape[1]), take(1)[0], take(4), take(2)))
-    v0, v1, v2, vs, vx, vy, vz, n0, ns, nz = take(10)
-    wide = CHUNK_HEADS * GROUP
+        chunk_a.append(Chunk(("a", j), (share, gw[j].shape[1]), take(1)[0], take(4), take(2)))
+    v0, v1, v2, vs, vx, vy, vz, n0, np, n1, ns, nz = take(12)
+    begin = [sum(groups[:j]) for j in range(len(groups) + 1)]
+    wide = groups[0] * GROUP
 
     def sources_a(j):
         return lambda owner: [(gw[j].at[spot(owner * share, share, 16), :], slice(0, gw[j].shape[1]))]
@@ -906,9 +899,9 @@
     def stores():
         copies = [(chunk_w.final, fw_ref), (chunk_1.final, f1_ref)]
         copies += [(chunk_a[0].final.at[:, wide : wide + width], fo_ref)]
-        copies += [
-            (chunk.final.at[:, 0:wide], fa_ref.at[:, j * wide : (j + 1) * wide]) for j, chunk in enumerate(chunk_a)
-        ]
+        for j, chunk in enumerate(chunk_a):
+            cols = slice(begin[j] * GROUP, begin[j + 1] * GROUP)
+            copies.append((chunk.final.at[:, 0 : groups[j] * GROUP], fa_ref.at[:, cols]))
         return [pltpu.make_async_copy(a, b, local.at[4 + i]) for i, (a, b) in enumerate(copies)]
 
     def merge(j):
@@ -935,8 +928,7 @@
         load(1).wait()
         red.depth_send(chunk_w)
         v0[...] = gvec_ref[...]
-        pad = gw[0].shape[1] - wide - width
-        gw[0][:, wide + width :] = jnp.zeros((width, pad), BF16)
+        n0[...] = jnp.zeros_like(n0)
         xt[...] = jnp.transpose(x_ref[...])
 
     def at(when):
@@ -948,15 +940,56 @@
 
         return run
 
-    at(2)(lambda: load(2).wait())
-    at(3)(lambda: red.plane_turn(chunk_1))
-    at(4)(lambda: red.share_send(chunk_w))
-    at(5)(lambda: merge(0))
-    at(6)(lambda: [turn_z(chunk_1), red.share_pass(chunk_w)])
-    at(8)(lambda: [red.plane_turn(chunk_a[0]), red.share_wait(chunk_w)])
-    at(9)(lambda: [merge(1), red.share_send(chunk_1)])
-    at(10)(lambda: turn_z(chunk_a[0]))
-    at(11)(lambda: [red.plane_turn(chunk_a[1]), red.share_pass(chunk_1)])
+    def finish(chunk):
+        n0[...] += red.share_send(chunk)
+
+    def vec_pair():
+        red.arrived(("v", "s"), vs, here.sib_dev)
+        v1[...] = v0[...] + vs[...]
+        red.send(("v", "x"), lambda: (v1, vx, here.x_dev))
+
+    def vec_plane():
+        red.arrived(("v", "x"), vx, here.x_dev)
+        v2[...] = v1[...] + vx[...]
+        red.send(("v", "y"), lambda: (v2, vy, here.y_dev))
+
+    def vec_depth():
+        red.arrived(("v", "y"), vy, here.y_dev)
+        vz[here.z] = v2[...] + vy[...]
+        for k in range(1, here.depth):
+            red.send(("v", "z", k), lambda k=k: (vz.at[here.z], vz.at[here.z], here.z_dev(k)))
+
+    def vec_done():
+        for k in range(1, here.depth):
+            red.arrived(("v", "z", k), vz.at[here.behind(k) // 2], here.z_dev(k))
+        vec = vz[0]
+        for z in range(1, here.depth):
+            vec = vec + vz[z]
+        v_ref[...] = vec
+
+    a = chunk_a
+    last = len(groups) - 1
+    plan = {
+        2: [lambda: load(2).wait()],
+        3: [lambda: red.plane_turn(chunk_1)],
+        4: [lambda: finish(chunk_w)],
+        5: [lambda: merge(0)],
+        6: [lambda: turn_z(chunk_1)],
+        8: [lambda: red.plane_turn(a[0])],
+        9: [lambda: merge(1), lambda: finish(chunk_1)],
+        10: [lambda: turn_z(a[0])],
+        11: [lambda: red.plane_turn(a[1]), lambda: merge(2)],
+        12: [lambda: turn_z(a[1])],
+        13: [lambda: merge(3), lambda: vec_pair(), lambda: red.plane_turn(a[2])],
+        15: [lambda: turn_z(a[2]), lambda: finish(a[0])],
+        17: [lambda: red.plane_turn(a[3]), lambda: vec_plane()],
+        19: [lambda: turn_z(a[3]), lambda: finish(a[1]), lambda: vec_depth()],
+        21: [lambda: finish(a[2]), lambda: vec_done()],
+        22: [lambda: red.share_wait(chunk_w), lambda: red.share_wait(chunk_1), lambda: red.share_wait(a[0])],
+    }
+    for when, actions in plan.items():
+        for action in actions:
+            at(when)(action)
 
     @pl.when(step < heads)
     def _():
@@ -973,12 +1006,11 @@
                 gp[step, here_rows, index * LANES : (index + 1) * LANES] = tile
         grads = gp[step]
         product = mm(xt[...], grads).astype(BF16)
-        inside = spot(lax.rem(step, CHUNK_HEADS) * GROUP, GROUP, LANES)
-        for j in range(groups):
-
-            @pl.when(step // CHUNK_HEADS == j)
+        for j in range(len(groups)):
+
+            @pl.when((step >= begin[j]) & (step < begin[j + 1]))
             def _():
-                gw[j][:, inside] = product
+                gw[j][:, spot((step - begin[j]) * GROUP, GROUP, LANES)] = product
 
         sums = jnp.sum(jnp.sum(grads.astype(F32).reshape(rows // 8, 8, GROUP), axis=0), axis=0, keepdims=True)
 
@@ -996,34 +1028,8 @@
             else:
                 v0[4:5, pair] = jnp.where(mine, second, v0[4:5, pair])
 
-    for j in range(groups):
-        at((j + 1) * CHUNK_HEADS - 1)(lambda j=j: red.pair_send(chunk_a[j], sources_a(j)))
-
-    last = chunk_a[-1]
-
-    def vec_pair():
-        red.arrived(("v", "s"), vs, here.sib_dev)
-        v1[...] = v0[...] + vs[...]
-        red.send(("v", "x"), lambda: (v1, vx, here.x_dev))
-
-    def vec_plane():
-        red.arrived(("v", "x"), vx, here.x_dev)
-        v2[...] = v1[...] + vx[...]
-        red.send(("v", "y"), lambda: (v2, vy, here.y_dev))
-
-    def vec_depth():
-        red.arrived(("v", "y"), vy, here.y_dev)
-        vz[here.z] = v2[...] + vy[...]
-        for k in range(1, here.depth):
-            red.send(("v", "z", k), lambda k=k: (vz.at[here.z], vz.at[here.z], here.z_dev(k)))
-
-    def vec_done():
-        for k in range(1, here.depth):
-            red.arrived(("v", "z", k), vz.at[here.behind(k) // 2], here.z_dev(k))
-        vec = vz[0]
-        for z in range(1, here.depth):
-            vec = vec + vz[z]
-        v_ref[...] = vec
+    for j in range(len(groups)):
+        at(begin[j + 1] - 1)(lambda j=j: red.pair_send(chunk_a[j], sources_a(j)))
 
     at(heads - 1)(lambda: red.send(("v", "s"), lambda: (v0, vs, here.sib_dev)))
     at(heads)(lambda: load(3).wait())
@@ -1032,34 +1038,26 @@
     def _():
         ig[...] += mm_nt(gp[step - heads], wp_ref[...])
 
-    at(heads + 1)(lambda: [merge(groups - 1), vec_pair()])
-    at(heads + 2)(lambda: [red.share_send(chunk_a[0]), red.share_wait(chunk_1)])
-    at(heads + 3)(lambda: turn_z(chunk_a[1]))
-    at(heads + 4)(lambda: [red.share_pass(chunk_a[0]), vec_plane()])
-    at(heads + 6)(lambda: [red.plane_turn(last), red.share_wait(chunk_a[0])])
-    at(heads + 8)(lambda: [red.share_send(chunk_a[1]), vec_depth()])
-    at(heads + 9)(lambda: turn_z(last))
-    at(heads + 10)(lambda: [red.share_pass(chunk_a[1]), vec_done()])
-
     @pl.when(step == 2 * heads - 1)
     def _():
-        ig_ref[...] = ig[...].astype(BF16)
-        red.share_wait(chunk_a[1])
-        norm = squares(chunk_w.final, width) + squares(chunk_1.final, inner)
-        norm = norm + squares(chunk_a[0].final, wide + width)
-        for chunk in chunk_a[1:-1]:
-            norm = norm + squares(chunk.final, wide)
-        red.share_send(last)
+        finish(a[last])
+        np[here.wide] = n0[...]
+        for name, device in (("nx", here.x_dev), ("ny", here.y_dev), ("nd", here.d_dev)):
+            red.send((name,), lambda device=device: (np.at[here.wide], np.at[here.wide], device))
         vec = v_ref[...]
         square = jnp.sum(jnp.sum(vec * vec, axis=0, keepdims=True), axis=1, keepdims=True)
-        red.share_pass(last)
-        red.share_wait(last)
+        ig_ref[...] = ig[...].astype(BF16)
+        ways = (("nx", here.x_quarter, here.x_dev), ("ny", here.y_quarter, here.y_dev), ("nd", here.d_quarter, here.d_dev))
+        for name, quarter, device in ways:
+            red.arrived((name,), np.at[quarter], device)
+        n1[...] = (np[0] + np[1]) + (np[2] + np[3])
+        red.send(("n", "s"), lambda: (n1, ns, here.sib_dev))
+        for chunk in a[1:]:
+            red.share_wait(chunk)
         for copy in stores():
             copy.start()
-        n0[...] = norm + squares(last.final, wide)
-        red.send(("n", "s"), lambda: (n0, ns, here.sib_dev))
         red.arrived(("n", "s"), ns, here.sib_dev)
-        nz[here.z] = n0[...] + ns[...]
+        nz[here.z] = n1[...] + ns[...]
         for k in range(1, here.depth):
             red.send(("n", "z", k), lambda k=k: (nz.at[here.z], nz.at[here.z], here.z_dev(k)))
         for k in range(1, here.depth):
@@ -1077,9 +1075,8 @@
 def reduce_call(narrow, x, q, kv, aug, gc, ctx, wp, ka, km, word, gvec, gr1, t1, tw, gwo, deep, length):
     rows, width = x.shape
     heads = q.shape[1] // LANES
-    groups = heads // CHUNK_HEADS
+    groups = head_groups(heads)
     depth, share, inner = t1.shape
-    acols = CHUNK_HEADS * GROUP
 
     def now(h):
         return jnp.minimum(h, heads - 1)
@@ -1096,23 +1093,24 @@
     vec = pltpu.VMEM((16, width), F32)
     tile = pltpu.VMEM((8, LANES), F32)
     scratch = [pltpu.VMEM((width, rows), BF16), pltpu.VMEM((heads, rows, GROUP), BF16), pltpu.VMEM((rows, width), F32)]
-    scratch += [pltpu.VMEM(tw.shape, BF16), *end_scratch(depth, deep, width, True)]
+    scratch += [pltpu.VMEM(tw.shape, BF16), *end_scratch(depth, deep, width)]
     scratch += [
         pltpu.VMEM(t1.shape, BF16),
-        *plane_scratch(depth, share, inner, False),
-        *end_scratch(depth, share, inner, False),
+        *plane_scratch(depth, share, inner),
+        *end_scratch(depth, share, inner),
     ]
-    for j in range(groups):
-        cols = acols + (width + 2 * LANES if j == 0 else 0)
+    for j, size in enumerate(groups):
+        cols = size * GROUP + (width if j == 0 else 0)
         scratch += [
             pltpu.VMEM((width, cols), BF16),
             pltpu.VMEM((depth, share, cols), BF16),
-            *plane_scratch(depth, share, cols, False),
-            *end_scratch(depth, share, cols, False),
+            *plane_scratch(depth, share, cols),
+            *end_scratch(depth, share, cols),
         ]
-    scratch += [vec] * 6 + [pltpu.VMEM((depth, 16, width), F32), tile, tile, pltpu.VMEM((depth, 8, LANES), F32)]
-    count = (2 + groups) * (depth + 10 + depth - 1) + 2 * (3 + depth)
-    scratch += [pltpu.SemaphoreType.DMA((count,))] * 2 + [pltpu.SemaphoreType.DMA((7 + groups,))]
+    several = pltpu.VMEM((depth, 8, LANES), F32)
+    scratch += [vec] * 6 + [pltpu.VMEM((depth, 16, width), F32), tile, pltpu.VMEM((4, 8, LANES), F32), tile, tile, several]
+    count = (2 + len(groups)) * (2 * depth + 6) + 2 * (4 + depth)
+    scratch += [pltpu.SemaphoreType.DMA((count,))] * 2 + [pltpu.SemaphoreType.DMA((7 + len(groups),))]
     return pl.pallas_call(
         functools.partial(reduce_kernel, narrow, length, groups, deep),
         grid=(2 * heads,),
@@ -1176,7 +1174,7 @@
             (sum_s, gr1_hbm),
             (io, gctx_hbm),
             (gwo_s, gwo_hbm),
-            (gw2_s, gw2_hbm) if red is None else (chunk.total.at[:, chunk.cut(here.wide)[0], :], gw2_hbm),
+            (gw2_s, gw2_hbm) if red is None else (chunk.total.at[(slice(None), *chunk.quarter(here.wide))], gw2_hbm),
             (act_s.at[0:width, :] if red is None else chunk_1.total, gw1_hbm),
         )[index]
         return pltpu.make_async_copy(source, target, sems.at[6 + index])
@@ -1205,8 +1203,8 @@
         here = Place(narrow)
         red = Reducer(here, scratch[0], scratch[1])
         deep, share = scratch[2].shape[1], scratch[7].shape[1]
-        chunk = Chunk("w", True, (deep, width), scratch[2], scratch[3:7])
-        chunk_1 = Chunk("1", False, (share, inner), scratch[7])
+        chunk = Chunk("w", (deep, width), scratch[2], scratch[3:7])
+        chunk_1 = Chunk("1", (share, inner), scratch[7])
         here.greet()
 
         def sources(owner):
@@ -1355,9 +1353,9 @@
     shape_w, shape_1 = (inner, width), (width, inner)
     if narrow is not None:
         depth, deep, share = narrow // 2, inner // narrow, width // narrow
-        shape_w, shape_1 = (depth, deep // 4, width), (depth, share, inner)
+        shape_w, shape_1 = (depth, deep // 2, width // 2), (depth, share, inner)
         scratch = [pltpu.SemaphoreType.DMA((2 * depth + 6,))] * 2
-        scratch += [pltpu.VMEM((depth, deep, width), BF16), *plane_scratch(depth, deep, width, True)]
+        scratch += [pltpu.VMEM((depth, deep, width), BF16), *plane_scratch(depth, deep, width)]
         scratch += [pltpu.VMEM((depth, share, inner), BF16)]
         params = dict(collective_id=2, has_side_effects=True)
     return pl.pallas_call(

time: 300 us -> 287 us (0.957)
  Pallas kernels: 288 us -> 275 us
    pallas_call x1, Pallas kernels: 95.9 us -> 87.8 us  [gather_call(): pl.pallas_call(functools.partial(gather_kernel, narrow), in_specs=[vmem]...]
    pallas_call x1, Pallas kernels: 107 us -> 104 us  [reduce_call(): pl.pallas_call(functools.partial(reduce_kernel, narrow, length, groups, d...]
where the time goes in v2:
time: 287 us; the launch traced here: 283 us
  Pallas kernels  275 us (96%)
  local copies, waits for them, and re-layouts  4.71 us (2%)
    pallas_call x1, Pallas kernels, reduce_call(): pl.pallas_call(functools.partial(reduce_kernel, narrow, length, groups, d...  104 us
    pallas_call x1, Pallas kernels, gather_call(): pl.pallas_call(functools.partial(gather_kernel, narrow), in_specs=[vmem]...  87.8 us
    pallas_call x1, Pallas kernels, middle_call(): pl.pallas_call(functools.partial(middle_kernel, narrow), in_specs=[hbm, h...  69.3 us
    pallas_call x1, Pallas kernels, update_call(): pl.pallas_call(functools.partial(update_kernel, narrow), grid=(steps,), i...  14.9 us

profile of v2, /device:TPU:0, one launch (start us, length us, event | category | flops | bytes accessed | tf_op | source)
XLA Modules:
  0.0 282.9 jit_solution(6148413607144370834)
XLA Ops:
  0.7 87.8 %gather.1 = (bf16[1280,1536]{1,0:T(8,128)(2,1)}, bf16[1280,1536]{1,0:T(8,128)(2,1)}, bf16[1280,768]{1,0:T(8,128)(2,1)}, bf16[1280,1536]{1,0:T(8,128)(2,1)}, bf16...) custom-call(bf16[1280,768]{1,0:T(8,128)(2,1)} %bitcast.5, ...), custom_call_target="tpu_custom_call" | custom-call | tf_op jit(solution)/shard_map/gather/pallas_call | solution.py:541
  88.5 69.3 %middle.1 = (bf16[1280,768]{1,0:T(8,128)(2,1)}, f32[1280,768]{1,0:T(8,128)}, bf16[1280,768]{1,0:T(8,128)(2,1)}, bf16[4,96,3072]{2,1,0:T(8,128)(2,1)}, bf16[768,7...) custom-call(bf16[1280,768]{1,0:T(8,128)(2,1)} %bitcast.6, ...), custom_call_target="tpu_custom_call" | custom-call | tf_op jit(solution)/shard_map/middle/pallas_call | solution.py:1361
  157.7 103.6 %reduce.1 = (bf16[1280,768]{1,0:T(8,128)(2,1)}, bf16[96,3072]{1,0:T(8,128)(2,1)}, bf16[96,768]{1,0:T(8,128)(2,1)}, bf16[384,768]{1,0:T(8,128)(2,1)}, bf16[96,460...) custom-call(bf16[1280,768]{1,0:T(8,128)(2,1)} %bitcast.7, bf16[1280,1536]{1,0:T(8,128)(2,1)} %get-tuple-element.73.q_ref, ...), custom_call_target="tpu_custom_call" | custom-call | tf_op jit(solution)/shard_map/reduce/pallas_call | solution.py:1114
  261.3 1.2 slice.3
  263.2 0.0 copy-start
  263.2 14.9 %update.1 = (f32[96,4608]{1,0:T(8,128)}, f32[96,768]{1,0:T(8,128)}, f32[96,3072]{1,0:T(8,128)}, f32[384,768]{1,0:T(8,128)}, f32[15,96]{1,0:T(8,128)}, /*index=5*...) custom-call(f32[8,128]{1,0:T(8,128)} %get-tuple-element.87.n_ref, ...), custom_call_target="tpu_custom_call" | custom-call | tf_op jit(solution)/shard_map/update/pallas_call | solution.py:1492
  278.1 0.0 copy-done
  278.1 0.0 copy-start.1
  278.1 1.3 copy.44
  279.4 1.0 copy-done.1
  280.3 1.3 copy.45
Async XLA Ops:
  263.2 14.9 %copy-start = (bf16[1280,768]{1,0:T(8,128)(2,1)S(1)}, bf16[1280,768]{1,0:T(8,128)(2,1)}, u32[]{:S(2)}) copy-start(bf16[1280,768]{1,0:T(8,128)(2,1)} %get-tuple-element.72) | copy-start | bytes 5898244
  278.1 2.3 copy-start.1

commit v3 on v2

--- a/solution.py
+++ b/solution.py
@@ -201,7 +201,7 @@
 
 def gather_kernel(
     narrow, x_ref, proj_ref, wo_ref, w1_ref, w2_ref, vec_ref, seg_ref, type_ref,
-    q_out, kv_out, ctx_out, aug_out, a_out, e_out, w2_out, vec_out, word_ref, km_ref, ka_ref,
+    q_out, kv_out, ctx_out, aug_out, a_out, e_out, w2_out, vec_out, word_ref, km_ref, ka_ref, xt_ref,
     a_full, e_own, w2_own, v_all, bias, q_s, kv_s, ctx_s, aug_s, qa_ref, send, recv, local,
 ):
     rows, width = x_ref.shape
@@ -362,6 +362,8 @@
     copy_w = pltpu.make_async_copy(w2_own, whole("w", me), local.at[1])
     copy_e.start()
     copy_w.start()
+
+    xt_ref[...] = jnp.transpose(x_ref[...])
 
     length = seg_ref.shape[1]
     lane = lax.broadcasted_iota(jnp.int32, (length, LANES), 1)
@@ -541,7 +543,7 @@
     return pl.pallas_call(
         functools.partial(gather_kernel, narrow),
         in_specs=[vmem] * 8,
-        out_specs=[hbm] * 7 + [vmem] * 4,
+        out_specs=[hbm] * 7 + [vmem] * 5,
         out_shape=[
             shape((rows, heads * LANES), BF16),
             shape((rows, heads * LANES), BF16),
@@ -554,6 +556,7 @@
             shape((rows, LANES), BF16),
             shape((rows, LANES), BF16),
             shape((rows, LANES), BF16),
+            shape((width, rows), BF16),
         ],
         scratch_shapes=[
             pltpu.VMEM((width, proj.shape[1]), BF16),
@@ -633,15 +636,20 @@
     probs_t = jnp.exp2(scores_t * LOG2E)
     gwide = gcon.astype(F32)
     prod = gwide * con.astype(F32)
-    mine = low != odd
-    delta = jnp.sum(jnp.where(mine, prod, 0.0), axis=1, keepdims=True)
-    high, mid, rest = split_three(delta)
+    prod = jnp.where(low, 0.0, prod) if odd else jnp.where(low, prod, 0.0)
+    high, mid, rest = split_three(jnp.sum(prod, axis=1, keepdims=True))
     extra = jnp.where(lane == 0, -high, jnp.where(lane == 1, -mid, jnp.where(lane == 2, -rest, 0.0)))
-    ghead = jnp.where(low, extra, jnp.where(odd, gwide, swap_halves(gwide))).astype(BF16)
+    ghead = jnp.where(low, extra, gwide if odd else swap_halves(gwide)).astype(BF16)
     ones_val = jnp.where(low, jnp.where(lane < 3, 1.0, 0.0), keyval.astype(F32)).astype(BF16)
     gscores_t = (probs_t * mm_nt(ones_val, ghead)).astype(BF16)
-    gval = mm(probs_t.astype(BF16), ghead)
-    gkey = mm(gscores_t, query)
+    blank = jnp.zeros_like(ghead)
+    both = mm(
+        jnp.concatenate([probs_t.astype(BF16), gscores_t], axis=1),
+        jnp.concatenate(
+            [jnp.concatenate([ghead, blank], axis=1), jnp.concatenate([blank, query], axis=1)], axis=0
+        ),
+    )
+    gval, gkey = both[:, 0:LANES], both[:, LANES:]
     gquery = (jnp.transpose(mm_tn(keys, gscores_t)) * (HEAD**-0.5)).astype(BF16)
     zero = jnp.zeros_like(gquery)
     gkey = jnp.where(kmask.astype(F32) > 0, gkey, 0.0)
@@ -656,49 +664,49 @@
 def attend_back_kernel(
     length, x_ref, q_ref, kv_ref, aug_ref, gc_ref, ctx_ref, ka_ref, km_ref, word_ref, gp_ref, gw_ref, sum_ref, xt
 ):
-    step = pl.program_id(0)
     rows = x_ref.shape[0]
 
-    @pl.when(step == 0)
+    @pl.when(pl.program_id(0) == 0)
     def _():
         xt[...] = jnp.transpose(x_ref[...])
 
     low = low_lanes(length)
     lane = lax.broadcasted_iota(jnp.int32, (length, LANES), 1)
-    odd = lax.rem(step, 2) == 1
-    for seq in range(rows // length):
-        here = slice(seq * length, (seq + 1) * length)
-        tiles = attend_back_head(
-            q_ref[here], kv_ref[here], aug_ref[here], gc_ref[here], ctx_ref[here],
-            ka_ref[here], km_ref[here], word_ref[here] > 0, odd, low, lane,
-        )
-        for index, tile in enumerate(tiles):
-            gp_ref[here, index * LANES : (index + 1) * LANES] = tile
+    for part in range(2):
+        cols = slice(part * LANES, (part + 1) * LANES)
+        for seq in range(rows // length):
+            here = slice(seq * length, (seq + 1) * length)
+            tiles = attend_back_head(
+                q_ref[here, cols], kv_ref[here, cols], aug_ref[here, cols], gc_ref[here], ctx_ref[here],
+                ka_ref[here], km_ref[here], word_ref[here] > 0, part == 1, low, lane,
+            )
+            for index, tile in enumerate(tiles):
+                at = part * GROUP + index * LANES
+                gp_ref[here, at : at + LANES] = tile
     grads = gp_ref[...]
     gw_ref[...] = mm(xt[...], grads).astype(BF16)
-    sums = jnp.sum(grads.astype(F32).reshape(rows // 8, 8, GROUP), axis=0)
-    sum_ref[...] = jnp.sum(sums, axis=0, keepdims=True)
+    sum_ref[...] = jnp.sum(fold(grads.astype(F32)), axis=0, keepdims=True)
 
 
 def attend_back_call(x, q, kv, aug, gc, ctx, ka, km, word, length):
     rows, width = x.shape
-    heads = q.shape[1] // LANES
-    head = pl.BlockSpec((rows, LANES), lambda h: (0, h))
-    pair = pl.BlockSpec((rows, LANES), lambda h: (0, h // 2))
+    pairs = q.shape[1] // (2 * LANES)
+    head = pl.BlockSpec((rows, 2 * LANES), lambda h: (0, h))
+    pair = pl.BlockSpec((rows, LANES), lambda h: (0, h))
     one = pl.BlockSpec((rows, LANES), lambda h: (0, 0))
     return pl.pallas_call(
         functools.partial(attend_back_kernel, length),
-        grid=(heads,),
+        grid=(pairs,),
         in_specs=[pl.BlockSpec((rows, width), lambda h: (0, 0)), head, head, head, pair, pair, one, one, one],
         out_specs=[
-            pl.BlockSpec((rows, GROUP), lambda h: (0, h)),
-            pl.BlockSpec((width, GROUP), lambda h: (0, h)),
-            pl.BlockSpec((1, GROUP), lambda h: (0, h)),
+            pl.BlockSpec((rows, 2 * GROUP), lambda h: (0, h)),
+            pl.BlockSpec((width, 2 * GROUP), lambda h: (0, h)),
+            pl.BlockSpec((1, 2 * GROUP), lambda h: (0, h)),
         ],
         out_shape=[
-            jax.ShapeDtypeStruct((rows, heads * GROUP), BF16),
-            jax.ShapeDtypeStruct((width, heads * GROUP), BF16),
-            jax.ShapeDtypeStruct((1, heads * GROUP), F32),
+            jax.ShapeDtypeStruct((rows, pairs * 2 * GROUP), BF16),
+            jax.ShapeDtypeStruct((width, pairs * 2 * GROUP), BF16),
+            jax.ShapeDtypeStruct((1, pairs * 2 * GROUP), F32),
         ],
         scratch_shapes=[pltpu.VMEM((width, rows), BF16)],
         compiler_params=pltpu.CompilerParams(vmem_limit_bytes=VMEM_LIMIT),
@@ -707,12 +715,12 @@
 
 
 class Chunk:
-    def __init__(self, name, shape, total, plane=None, end=None):
+    def __init__(self, name, shape, total, plane=(), end=None, via=None):
         self.name = name
         self.rows, self.cols = shape
-        self.total = total
-        if plane is not None:
-            self.r1a, self.r1b, self.r2a, self.r2b = plane
+        self.total, self.via = total, via
+        for label, ref in zip(("r1a", "r1b", "r2a", "r2b"), plane):
+            setattr(self, label, ref)
         if end is not None:
             self.rz, self.final = end
 
@@ -779,7 +787,7 @@
         self.send((chunk.name, "1a"), lambda: (chunk.total.at[self.lower(), :, cols()], chunk.r1a, here.x_dev))
         self.send((chunk.name, "1b"), lambda: (chunk.total.at[self.upper(), rows(), :], chunk.r1b, here.y_dev))
 
-    def plane_turn(self, chunk):
+    def plane_add(self, chunk):
         here = self.here
         total = chunk.total
         self.arrived((chunk.name, "1a"), chunk.r1a, here.x_dev)
@@ -788,6 +796,10 @@
         total[self.lower(), :, cols] = total[self.lower(), :, cols] + chunk.r1a[...]
         total[self.upper(), rows, :] = total[self.upper(), rows, :] + chunk.r1b[...]
 
+    def plane_next(self, chunk):
+        here = self.here
+        total = chunk.total
+
         def first():
             return total.at[(self.lower(), *chunk.quarter(here.y_quarter))], chunk.r2a, here.y_dev
 
@@ -796,6 +808,10 @@
 
         self.send((chunk.name, "2a"), first)
         self.send((chunk.name, "2b"), second)
+
+    def plane_turn(self, chunk):
+        self.plane_add(chunk)
+        self.plane_next(chunk)
 
     def plane_done(self, chunk):
         here = self.here
@@ -826,19 +842,29 @@
         rows, cols = chunk.quarter(here.wide)
         chunk.final[rows, cols] = done
 
-        def build(device):
-            piece = chunk.final.at[chunk.quarter(here.wide)]
-            return piece, piece, device
-
-        for name, device in (("fx", here.x_dev), ("fy", here.y_dev), ("fd", here.d_dev)):
-            self.send((chunk.name, name), lambda device=device: build(device))
+        ways = [("fx", here.x_dev), ("fy", here.y_dev)] + ([] if chunk.via else [("fd", here.d_dev)])
+        for name, device in ways:
+            self.send((chunk.name, name), lambda device=device: self.share_copy(chunk, here.wide, device))
         return squares(done)
+
+    def share_copy(self, chunk, quarter, device):
+        piece = chunk.final.at[chunk.quarter(quarter)]
+        return piece, piece, device
+
+    def share_pass(self, chunk):
+        here = self.here
+        by_x = chunk.via == "x"
+        name, quarter, device = ("fy", here.y_quarter, here.x_dev) if by_x else ("fx", here.x_quarter, here.y_dev)
+        self.arrived((chunk.name, name), chunk.final.at[chunk.quarter(quarter)], device)
+        self.send((chunk.name, "fd"), lambda: self.share_copy(chunk, quarter, device))
 
     def share_wait(self, chunk):
         here = self.here
         ways = (("fx", here.x_quarter, here.x_dev), ("fy", here.y_quarter, here.y_dev), ("fd", here.d_quarter, here.d_dev))
+        seen = {"x": "fy", "y": "fx"}.get(chunk.via)
         for name, quarter, device in ways:
-            self.arrived((chunk.name, name), chunk.final.at[chunk.quarter(quarter)], device)
+            if name != seen:
+                self.arrived((chunk.name, name), chunk.final.at[chunk.quarter(quarter)], device)
 
 
 def squares(value):
@@ -850,21 +876,21 @@
     return total
 
 
-def head_groups(heads):
-    return (heads // 3, heads // 3, heads // 6, heads // 6)
+def pair_groups(pairs):
+    return (pairs // 3, pairs // 3, pairs // 6, pairs // 6)
 
 
 def reduce_kernel(
     narrow, length, groups, deep,
-    x_ref, q_ref, kv_ref, aug_ref, gc_ref, ctx_ref, wp_ref, ka_ref, km_ref, word_ref, gvec_ref,
+    xt, q_ref, kv_ref, aug_ref, gc_ref, ctx_ref, wp_ref, ka_ref, km_ref, word_ref, gvec_ref,
     gr1_ref, t1_ref, tw_ref, gwo_ref,
     ig_ref, f1_ref, fo_ref, fw_ref, fa_ref, v_ref, n_ref,
-    xt, gp, ig, *scratch,
+    gp, ig, *scratch,
 ):
     step = pl.program_id(0)
-    rows, width = x_ref.shape
-    heads = sum(groups)
-    share, inner = t1_ref.shape[1:]
+    width, rows = xt.shape
+    pairs = sum(groups)
+    _, _, share, part = t1_ref.shape
     here = Place(narrow)
     scratch = list(scratch)
     red = Reducer(here, scratch[-3], scratch[-2])
@@ -874,22 +900,25 @@
         taken, scratch[:count] = scratch[:count], []
         return taken
 
-    chunk_w = Chunk("w", (deep, width), take(1)[0], None, take(2))
-    chunk_1 = Chunk("1", (share, inner), take(1)[0], take(4), take(2))
+    chunk_w = Chunk("w", (deep, width), take(1)[0], (), take(2), "x")
+    chunk_1 = [Chunk(("1", j), (share, part), take(1)[0], take(4), take(2), "yx"[j]) for j in range(2)]
     gw, chunk_a = [], []
     for j in range(len(groups)):
         gw += take(1)
-        chunk_a.append(Chunk(("a", j), (share, gw[j].shape[1]), take(1)[0], take(4), take(2)))
+        via = ("y", "x", None, None)[j]
+        chunk_a.append(Chunk(("a", j), (share, gw[j].shape[1]), take(1)[0], take(4), take(2), via))
     v0, v1, v2, vs, vx, vy, vz, n0, np, n1, ns, nz = take(12)
     begin = [sum(groups[:j]) for j in range(len(groups) + 1)]
-    wide = groups[0] * GROUP
+    both = 2 * GROUP
+    wide = groups[0] * both
 
     def sources_a(j):
         return lambda owner: [(gw[j].at[spot(owner * share, share, 16), :], slice(0, gw[j].shape[1]))]
 
     def load(index):
         source, target = (
-            (t1_ref, chunk_1.total),
+            (t1_ref.at[0], chunk_1[0].total),
+            (t1_ref.at[1], chunk_1[1].total),
             (tw_ref, chunk_w.total),
             (gwo_ref, gw[0].at[:, wide : wide + width]),
             (gr1_ref, ig),
@@ -897,12 +926,13 @@
         return pltpu.make_async_copy(source, target, local.at[index])
 
     def stores():
-        copies = [(chunk_w.final, fw_ref), (chunk_1.final, f1_ref)]
+        copies = [(chunk_w.final, fw_ref)]
+        copies += [(chunk.final, f1_ref.at[:, j * part : (j + 1) * part]) for j, chunk in enumerate(chunk_1)]
         copies += [(chunk_a[0].final.at[:, wide : wide + width], fo_ref)]
         for j, chunk in enumerate(chunk_a):
-            cols = slice(begin[j] * GROUP, begin[j + 1] * GROUP)
-            copies.append((chunk.final.at[:, 0 : groups[j] * GROUP], fa_ref.at[:, cols]))
-        return [pltpu.make_async_copy(a, b, local.at[4 + i]) for i, (a, b) in enumerate(copies)]
+            cols = slice(begin[j] * both, begin[j + 1] * both)
+            copies.append((chunk.final.at[:, 0 : groups[j] * both], fa_ref.at[:, cols]))
+        return [pltpu.make_async_copy(a, b, local.at[5 + i]) for i, (a, b) in enumerate(copies)]
 
     def merge(j):
         def one(z, carry):
@@ -920,16 +950,17 @@
 
     @pl.when(step == 0)
     def _():
-        for index in range(4):
+        for index in range(5):
             load(index).start()
         here.greet()
         load(0).wait()
-        red.plane_send(chunk_1)
+        red.plane_next(chunk_1[0])
         load(1).wait()
+        red.plane_send(chunk_1[1])
+        load(2).wait()
         red.depth_send(chunk_w)
         v0[...] = gvec_ref[...]
         n0[...] = jnp.zeros_like(n0)
-        xt[...] = jnp.transpose(x_ref[...])
 
     def at(when):
         def run(action):
@@ -970,75 +1001,84 @@
     a = chunk_a
     last = len(groups) - 1
     plan = {
-        2: [lambda: load(2).wait()],
-        3: [lambda: red.plane_turn(chunk_1)],
+        2: [lambda: load(3).wait(), lambda: turn_z(chunk_1[0])],
+        3: [lambda: red.plane_turn(chunk_1[1])],
         4: [lambda: finish(chunk_w)],
-        5: [lambda: merge(0)],
-        6: [lambda: turn_z(chunk_1)],
+        5: [lambda: merge(0), lambda: turn_z(chunk_1[1])],
+        6: [lambda: red.share_pass(chunk_w)],
+        7: [lambda: finish(chunk_1[0])],
         8: [lambda: red.plane_turn(a[0])],
-        9: [lambda: merge(1), lambda: finish(chunk_1)],
+        9: [lambda: merge(1), lambda: finish(chunk_1[1]), lambda: red.share_pass(chunk_1[0])],
         10: [lambda: turn_z(a[0])],
-        11: [lambda: red.plane_turn(a[1]), lambda: merge(2)],
-        12: [lambda: turn_z(a[1])],
-        13: [lambda: merge(3), lambda: vec_pair(), lambda: red.plane_turn(a[2])],
-        15: [lambda: turn_z(a[2]), lambda: finish(a[0])],
-        17: [lambda: red.plane_turn(a[3]), lambda: vec_plane()],
-        19: [lambda: turn_z(a[3]), lambda: finish(a[1]), lambda: vec_depth()],
-        21: [lambda: finish(a[2]), lambda: vec_done()],
-        22: [lambda: red.share_wait(chunk_w), lambda: red.share_wait(chunk_1), lambda: red.share_wait(a[0])],
+        11: [lambda: red.plane_turn(a[1]), lambda: merge(2), lambda: red.share_pass(chunk_1[1])],
     }
-    for when, actions in plan.items():
+    tail = [
+        [lambda: turn_z(a[1])],
+        [lambda: merge(3), vec_pair, lambda: red.plane_turn(a[2])],
+        [lambda: turn_z(a[2]), lambda: finish(a[0])],
+        [lambda: red.plane_turn(a[3]), vec_plane],
+        [lambda: turn_z(a[3]), lambda: finish(a[1]), lambda: red.share_pass(a[0]), vec_depth],
+        [lambda: finish(a[2]), vec_done, lambda: red.share_pass(a[1])],
+    ]
+
+    def advance(half):
+        for when, actions in plan.items():
+            if when % 2 == half:
+                for action in actions:
+                    at(when // 2)(action)
+
+    for index, actions in enumerate(tail):
         for action in actions:
-            at(when)(action)
-
-    @pl.when(step < heads)
+            at(pairs + index)(action)
+
+    @pl.when(step < pairs)
     def _():
         low = low_lanes(length)
         lane = lax.broadcasted_iota(jnp.int32, (length, LANES), 1)
-        odd = lax.rem(step, 2) == 1
-        for seq in range(rows // length):
-            here_rows = slice(seq * length, (seq + 1) * length)
-            tiles = attend_back_head(
-                q_ref[here_rows], kv_ref[here_rows], aug_ref[here_rows], gc_ref[here_rows], ctx_ref[here_rows],
-                ka_ref[here_rows], km_ref[here_rows], word_ref[here_rows] > 0, odd, low, lane,
-            )
-            for index, tile in enumerate(tiles):
-                gp[step, here_rows, index * LANES : (index + 1) * LANES] = tile
+        for part in range(2):
+            advance(part)
+            cols = slice(part * LANES, (part + 1) * LANES)
+            for seq in range(rows // length):
+                mine = slice(seq * length, (seq + 1) * length)
+                tiles = attend_back_head(
+                    q_ref[mine, cols], kv_ref[mine, cols], aug_ref[mine, cols], gc_ref[mine], ctx_ref[mine],
+                    ka_ref[mine], km_ref[mine], word_ref[mine] > 0, part == 1, low, lane,
+                )
+                for index, tile in enumerate(tiles):
+                    start = part * GROUP + index * LANES
+                    gp[step, mine, start : start + LANES] = tile
         grads = gp[step]
         product = mm(xt[...], grads).astype(BF16)
         for j in range(len(groups)):
 
             @pl.when((step >= begin[j]) & (step < begin[j + 1]))
             def _():
-                gw[j][:, spot((step - begin[j]) * GROUP, GROUP, LANES)] = product
-
-        sums = jnp.sum(jnp.sum(grads.astype(F32).reshape(rows // 8, 8, GROUP), axis=0), axis=0, keepdims=True)
-
+                gw[j][:, spot((step - begin[j]) * both, both, LANES)] = product
+
+        sums = jnp.sum(fold(grads.astype(F32)), axis=0, keepdims=True)
         low1 = low_lanes(1)
-        pair = spot(step // 2 * LANES, LANES, LANES)
-        mine = low1 != odd
+        place = spot(step * LANES, LANES, LANES)
         for b in range(3):
-            tile = sums[:, b * LANES : (b + 1) * LANES]
-            turned = swap_halves(tile)
-            first = jnp.where(odd, turned, tile)
-            second = jnp.where(odd, tile, turned)
+            even = sums[:, b * LANES : (b + 1) * LANES]
+            odd = sums[:, GROUP + b * LANES : GROUP + (b + 1) * LANES]
+            second = jnp.where(low1, swap_halves(even), odd)
             if b < 2:
-                v0[2 * b : 2 * b + 1, pair] = jnp.where(mine, first, v0[2 * b : 2 * b + 1, pair])
-                v0[2 * b + 1 : 2 * b + 2, pair] = jnp.where(mine, second, v0[2 * b + 1 : 2 * b + 2, pair])
+                v0[2 * b : 2 * b + 1, place] = jnp.where(low1, even, swap_halves(odd))
+                v0[2 * b + 1 : 2 * b + 2, place] = second
             else:
-                v0[4:5, pair] = jnp.where(mine, second, v0[4:5, pair])
+                v0[4:5, place] = second
 
     for j in range(len(groups)):
         at(begin[j + 1] - 1)(lambda j=j: red.pair_send(chunk_a[j], sources_a(j)))
 
-    at(heads - 1)(lambda: red.send(("v", "s"), lambda: (v0, vs, here.sib_dev)))
-    at(heads)(lambda: load(3).wait())
-
-    @pl.when(step >= heads)
+    at(pairs - 1)(lambda: red.send(("v", "s"), lambda: (v0, vs, here.sib_dev)))
+    at(pairs)(lambda: load(4).wait())
+
+    @pl.when(step >= pairs)
     def _():
-        ig[...] += mm_nt(gp[step - heads], wp_ref[...])
-
-    @pl.when(step == 2 * heads - 1)
+        ig[...] += mm_nt(gp[step - pairs], wp_ref[...])
+
+    @pl.when(step == 2 * pairs - 1)
     def _():
         finish(a[last])
         np[here.wide] = n0[...]
@@ -1052,7 +1092,7 @@
             red.arrived((name,), np.at[quarter], device)
         n1[...] = (np[0] + np[1]) + (np[2] + np[3])
         red.send(("n", "s"), lambda: (n1, ns, here.sib_dev))
-        for chunk in a[1:]:
+        for chunk in (chunk_w, *chunk_1, *a):
             red.share_wait(chunk)
         for copy in stores():
             copy.start()
@@ -1072,35 +1112,33 @@
             copy.wait()
 
 
-def reduce_call(narrow, x, q, kv, aug, gc, ctx, wp, ka, km, word, gvec, gr1, t1, tw, gwo, deep, length):
-    rows, width = x.shape
-    heads = q.shape[1] // LANES
-    groups = head_groups(heads)
-    depth, share, inner = t1.shape
+def reduce_call(narrow, xt, q, kv, aug, gc, ctx, wp, ka, km, word, gvec, gr1, t1, tw, gwo, deep, length):
+    width, rows = xt.shape
+    pairs = q.shape[1] // (2 * LANES)
+    groups = pair_groups(pairs)
+    _, depth, share, inner = t1.shape
 
     def now(h):
-        return jnp.minimum(h, heads - 1)
+        return jnp.minimum(h, pairs - 1)
 
     def fixed(shape):
         return pl.BlockSpec(shape, lambda h: (0, 0), pipeline_mode=pl.Buffered(1))
 
-    head = pl.BlockSpec((rows, LANES), lambda h: (0, now(h)))
-    pair = pl.BlockSpec((rows, LANES), lambda h: (0, now(h) // 2))
-    later = pl.BlockSpec((width, GROUP), lambda h: (0, jnp.maximum(h - heads, 0)))
+    head = pl.BlockSpec((rows, 2 * LANES), lambda h: (0, now(h)))
+    pair = pl.BlockSpec((rows, LANES), lambda h: (0, now(h)))
+    later = pl.BlockSpec((width, 2 * GROUP), lambda h: (0, jnp.maximum(h - pairs, 0)))
     one = fixed((rows, LANES))
     hbm = pl.BlockSpec(memory_space=pl.ANY)
     shape = jax.ShapeDtypeStruct
     vec = pltpu.VMEM((16, width), F32)
     tile = pltpu.VMEM((8, LANES), F32)
-    scratch = [pltpu.VMEM((width, rows), BF16), pltpu.VMEM((heads, rows, GROUP), BF16), pltpu.VMEM((rows, width), F32)]
+    scratch = [pltpu.VMEM((pairs, rows, 2 * GROUP), BF16), pltpu.VMEM((rows, width), F32)]
     scratch += [pltpu.VMEM(tw.shape, BF16), *end_scratch(depth, deep, width)]
-    scratch += [
-        pltpu.VMEM(t1.shape, BF16),
-        *plane_scratch(depth, share, inner),
-        *end_scratch(depth, share, inner),
-    ]
+    for _ in range(2):
+        scratch += [pltpu.VMEM((depth, share, inner), BF16)]
+        scratch += [*plane_scratch(depth, share, inner), *end_scratch(depth, share, inner)]
     for j, size in enumerate(groups):
-        cols = size * GROUP + (width if j == 0 else 0)
+        cols = size * 2 * GROUP + (width if j == 0 else 0)
         scratch += [
             pltpu.VMEM((width, cols), BF16),
             pltpu.VMEM((depth, share, cols), BF16),
@@ -1109,22 +1147,22 @@
         ]
     several = pltpu.VMEM((depth, 8, LANES), F32)
     scratch += [vec] * 6 + [pltpu.VMEM((depth, 16, width), F32), tile, pltpu.VMEM((4, 8, LANES), F32), tile, tile, several]
-    count = (2 + len(groups)) * (2 * depth + 6) + 2 * (4 + depth)
-    scratch += [pltpu.SemaphoreType.DMA((count,))] * 2 + [pltpu.SemaphoreType.DMA((7 + len(groups),))]
+    count = (3 + len(groups)) * (2 * depth + 6) + 2 * (4 + depth)
+    scratch += [pltpu.SemaphoreType.DMA((count,))] * 2 + [pltpu.SemaphoreType.DMA((9 + len(groups),))]
     return pl.pallas_call(
         functools.partial(reduce_kernel, narrow, length, groups, deep),
-        grid=(2 * heads,),
+        grid=(2 * pairs,),
         in_specs=[
-            fixed((rows, width)), head, head, head, pair, pair, later, one, one, one, fixed((16, width)),
+            fixed((width, rows)), head, head, head, pair, pair, later, one, one, one, fixed((16, width)),
             hbm, hbm, hbm, hbm,
         ],
         out_specs=[fixed((rows, width)), hbm, hbm, hbm, hbm, fixed((16, width)), fixed((8, LANES))],
         out_shape=[
             shape((rows, width), BF16),
-            shape((share, inner), BF16),
+            shape((share, 2 * inner), BF16),
             shape((share, width), BF16),
             shape((deep, width), BF16),
-            shape((share, heads * GROUP), BF16),
+            shape((share, pairs * 2 * GROUP), BF16),
             shape((16, width), F32),
             shape((8, LANES), F32),
         ],
@@ -1133,7 +1171,7 @@
             vmem_limit_bytes=VMEM_LIMIT, collective_id=1, has_side_effects=True
         ),
         name="reduce",
-    )(x, q, kv, aug, gc, ctx, wp, ka, km, word, gvec, gr1, t1, tw, gwo)
+    )(xt, q, kv, aug, gc, ctx, wp, ka, km, word, gvec, gr1, t1, tw, gwo)
 
 
 def gelu_pair(pre):
@@ -1175,7 +1213,8 @@
             (io, gctx_hbm),
             (gwo_s, gwo_hbm),
             (gw2_s, gw2_hbm) if red is None else (chunk.total.at[(slice(None), *chunk.quarter(here.wide))], gw2_hbm),
-            (act_s.at[0:width, :] if red is None else chunk_1.total, gw1_hbm),
+            (act_s.at[0:width, :], gw1_hbm) if red is None else (chunk_1[0].total, gw1_hbm.at[0]),
+            None if red is None else (chunk_1[1].total, gw1_hbm.at[1]),
         )[index]
         return pltpu.make_async_copy(source, target, sems.at[6 + index])
 
@@ -1204,14 +1243,16 @@
         red = Reducer(here, scratch[0], scratch[1])
         deep, share = scratch[2].shape[1], scratch[7].shape[1]
         chunk = Chunk("w", (deep, width), scratch[2], scratch[3:7])
-        chunk_1 = Chunk("1", (share, inner), scratch[7])
+        part = inner // 2
+        chunk_1 = [Chunk(("1", j), (share, part), scratch[7 + 3 * j], scratch[8:10] if j == 0 else ()) for j in range(2)]
         here.greet()
 
         def sources(owner):
             return [(gw2_s.at[spot(owner * deep, deep, 16), :], slice(0, width))]
 
-        def sources_1(owner):
-            return [(act_s.at[spot(owner * share, share, 16), :], slice(0, inner))]
+        def sources_1(j):
+            cols = slice(j * part, (j + 1) * part)
+            return lambda owner: [(act_s.at[spot(owner * share, share, 16), cols], slice(0, part))]
 
     for index in (1, 2, 0):
         load(index).wait()
@@ -1303,29 +1344,38 @@
     def merge(target, source, size):
         def one(z, carry):
             mine = spot((2 * z + here.core) * size, size, 16)
-            target[z] = target[z] + source[mine, :]
+            target[z] = target[z] + source(mine)
             return carry
 
         lax.fori_loop(0, here.depth, one, 0)
+
+    def merge_1(j):
+        red.pair_wait(chunk_1[j], sources_1(j))
+        merge(chunk_1[j].total, lambda mine: act_s[mine, j * part : (j + 1) * part], share)
 
     count = inner // block
     over_cols(0, count // 3, expand_back)
     if red is not None:
         red.pair_wait(chunk, sources)
-        merge(chunk.total, gw2_s, deep)
+        merge(chunk.total, lambda mine: gw2_s[mine, :], deep)
         red.plane_send(chunk)
     over_cols(count // 3, count, expand_back)
     for c in range(blocks):
         cols = slice(c * width, (c + 1) * width)
         act_s[0:width, cols] = mm_tn(h1_s[...], slope_s[:, cols]).astype(BF16)
+        if red is not None and (c + 1) % (blocks // 2) == 0:
+            red.pair_send(chunk_1[c // (blocks // 2)], sources_1(c // (blocks // 2)))
+    over_cols(0, 1, hidden_back)
     if red is not None:
-        red.pair_send(chunk_1, sources_1)
-    over_cols(0, per, hidden_back)
+        merge_1(0)
+        red.plane_send(chunk_1[0])
+    over_cols(1, per, hidden_back)
     if red is not None:
         red.plane_turn(chunk)
-        red.pair_wait(chunk_1, sources_1)
-        merge(chunk_1.total, act_s, share)
-    store(5).start()
+        merge_1(1)
+        store(6).start()
+    else:
+        store(5).start()
     over_rows(norm_one_back)
     store(1).start()
     store(0).wait()
@@ -1339,8 +1389,10 @@
         red.plane_done(chunk)
     store(4).start()
     if red is not None:
+        red.plane_add(chunk_1[0])
+        store(5).start()
         red.finish()
-    for index in range(1, 6):
+    for index in range(1, 6 if red is None else 7):
         store(index).wait()
 
 
@@ -1353,10 +1405,12 @@
     shape_w, shape_1 = (inner, width), (width, inner)
     if narrow is not None:
         depth, deep, share = narrow // 2, inner // narrow, width // narrow
-        shape_w, shape_1 = (depth, deep // 2, width // 2), (depth, share, inner)
-        scratch = [pltpu.SemaphoreType.DMA((2 * depth + 6,))] * 2
+        part = inner // 2
+        shape_w, shape_1 = (depth, deep // 2, width // 2), (2, depth, share, part)
+        scratch = [pltpu.SemaphoreType.DMA((3 * depth + 8,))] * 2
         scratch += [pltpu.VMEM((depth, deep, width), BF16), *plane_scratch(depth, deep, width)]
-        scratch += [pltpu.VMEM((depth, share, inner), BF16)]
+        scratch += [pltpu.VMEM((depth, share, part), BF16), *plane_scratch(depth, share, part)[0:2]]
+        scratch += [pltpu.VMEM((depth, share, part), BF16)]
         params = dict(collective_id=2, has_side_effects=True)
     return pl.pallas_call(
         functools.partial(middle_kernel, narrow),
@@ -1387,7 +1441,7 @@
             pltpu.VMEM((inner, width), BF16),
             pltpu.VMEM((width, width), BF16),
             pltpu.VMEM((vec.shape[0], 8, width), F32),
-            pltpu.SemaphoreType.DMA((12,)),
+            pltpu.SemaphoreType.DMA((13,)),
             *scratch,
         ],
         compiler_params=pltpu.CompilerParams(vmem_limit_bytes=VMEM_LIMIT, **params),
@@ -1475,7 +1529,7 @@
 
 def update_call(narrow, norm, shards, vec, masters, firsts, seconds):
     share = shards[0].shape[0]
-    steps = share // 16
+    steps = share // 48 if share % 48 == 0 else share // 16
 
     def rows_of(array_in):
         return pl.BlockSpec((array_in.shape[0] // steps, array_in.shape[1]), lambda i: (i, 0))
@@ -1534,7 +1588,7 @@
     narrow = lax.axis_size("narrow")
     pieces = can_pass_pieces(lax.axis_size("wide"), narrow, width, reduce_weight.shape[0])
     if pieces:
-        query, keyval, context, aug, proj_w, mid_w, reduce_w, vec_rows, word, kmask, kaug = gather_call(
+        query, keyval, context, aug, proj_w, mid_w, reduce_w, vec_rows, word, kmask, kaug, turned = gather_call(
             narrow, hidden, projection, context_out, expand_weight, reduce_weight, vector_params,
             segment_ids, type_ids,
         )
@@ -1565,7 +1619,7 @@
     out_shape = (seq_count, seq_len, width)
     if pieces:
         input_grad, shard_1, shard_o, shard_w, shard_a, grad_vectors, norm = reduce_call(
-            narrow, hidden, query, keyval, aug, grad_context, context, proj_w, kaug, kmask, word, grad_mid,
+            narrow, turned, query, keyval, aug, grad_context, context, proj_w, kaug, kmask, word, grad_mid,
             grad_r1, grad_expand, grad_reduce, grad_ctx_w, reduce_weight.shape[0], seq_len,
         )
         shards = (shard_a, shard_o, shard_1, shard_w)

time: 287 us -> 283 us (0.986)
  Pallas kernels: 275 us -> 271 us
    pallas_call x1, Pallas kernels: 104 us -> 97.7 us  [reduce_call(): pl.pallas_call(functools.partial(reduce_kernel, narrow, length, groups, d...]
where the time goes in v3:
time: 283 us; the launch traced here: 279 us
  Pallas kernels  271 us (96%)
  local copies, waits for them, and re-layouts  4.71 us (2%)
    pallas_call x1, Pallas kernels, reduce_call(): pl.pallas_call(functools.partial(reduce_kernel, narrow, length, groups, d...  97.7 us
    pallas_call x1, Pallas kernels, gather_call(): pl.pallas_call(functools.partial(gather_kernel, narrow), in_specs=[vmem]...  88.6 us
    pallas_call x1, Pallas kernels, middle_call(): pl.pallas_call(functools.partial(middle_kernel, narrow), in_specs=[hbm, h...  71.5 us
    pallas_call x1, Pallas kernels, update_call(): pl.pallas_call(functools.partial(update_kernel, narrow), grid=(steps,), i...  13.6 us

profile of v3, /device:TPU:0, one launch (start us, length us, event | category | flops | bytes accessed | tf_op | source)
XLA Modules:
  0.0 278.8 jit_solution(13454040866107426436)
XLA Ops:
  0.7 88.6 %gather.1 = (bf16[1280,1536]{1,0:T(8,128)(2,1)}, bf16[1280,1536]{1,0:T(8,128)(2,1)}, bf16[1280,768]{1,0:T(8,128)(2,1)}, bf16[1280,1536]{1,0:T(8,128)(2,1)}, bf16...) custom-call(bf16[1280,768]{1,0:T(8,128)(2,1)} %bitcast.5, ...), custom_call_target="tpu_custom_call" | custom-call | tf_op jit(solution)/shard_map/gather/pallas_call | solution.py:543
  89.2 71.5 %middle.1 = (bf16[1280,768]{1,0:T(8,128)(2,1)}, f32[1280,768]{1,0:T(8,128)}, bf16[1280,768]{1,0:T(8,128)(2,1)}, bf16[2,4,96,1536]{3,2,1,0:T(8,128)(2,1)}, bf16[7...) custom-call(bf16[1280,768]{1,0:T(8,128)(2,1)} %bitcast.6, ...), custom_call_target="tpu_custom_call" | custom-call | tf_op jit(solution)/shard_map/middle/pallas_call | solution.py:1415
  160.7 97.7 %reduce.1 = (bf16[1280,768]{1,0:T(8,128)(2,1)}, bf16[96,3072]{1,0:T(8,128)(2,1)}, bf16[96,768]{1,0:T(8,128)(2,1)}, bf16[384,768]{1,0:T(8,128)(2,1)}, bf16[96,460...) custom-call(bf16[768,1280]{1,0:T(8,128)(2,1)} %get-tuple-element.74.xt, ...), custom_call_target="tpu_custom_call" | custom-call | tf_op jit(solution)/shard_map/reduce/pallas_call | solution.py:1152
  258.4 1.2 slice.3
  260.3 0.0 copy-start
  260.3 13.6 %update.1 = (f32[96,4608]{1,0:T(8,128)}, f32[96,768]{1,0:T(8,128)}, f32[96,3072]{1,0:T(8,128)}, f32[384,768]{1,0:T(8,128)}, f32[15,96]{1,0:T(8,128)}, /*index=5*...) custom-call(f32[8,128]{1,0:T(8,128)} %get-tuple-element.89.n_ref, ...), custom_call_target="tpu_custom_call" | custom-call | tf_op jit(solution)/shard_map/update/pallas_call | solution.py:1546
  273.9 0.0 copy-done
  273.9 0.0 copy-start.1
  274.0 1.3 copy.44
  275.2 1.0 copy-done.1
  276.2 1.3 copy.45
Async XLA Ops:
  260.3 13.7 %copy-start = (bf16[1280,768]{1,0:T(8,128)(2,1)S(1)}, bf16[1280,768]{1,0:T(8,128)(2,1)}, u32[]{:S(2)}) copy-start(bf16[1280,768]{1,0:T(8,128)(2,1)} %get-tuple-element.73) | copy-start | bytes 5898244
  273.9 2.3 copy-start.1

commit v4 on v3

--- a/solution.py
+++ b/solution.py
@@ -200,9 +200,9 @@
 
 
 def gather_kernel(
-    narrow, x_ref, proj_ref, wo_ref, w1_ref, w2_ref, vec_ref, seg_ref, type_ref,
+    narrow, proj_ref, vec_ref, seg_ref, type_ref, x_hbm, wo_hbm, w1_hbm, w2_hbm,
     q_out, kv_out, ctx_out, aug_out, a_out, e_out, w2_out, vec_out, word_ref, km_ref, ka_ref, xt_ref,
-    a_full, e_own, w2_own, v_all, bias, q_s, kv_s, ctx_s, aug_s, qa_ref, send, recv, local,
+    a_full, e_own, w2_own, v_all, bias, q_s, kv_s, ctx_s, aug_s, qa_ref, x_ref, wo_ref, w1_ref, w2_ref, send, recv, local,
 ):
     rows, width = x_ref.shape
     share = proj_ref.shape[0]
@@ -211,6 +211,15 @@
     heads = width // HEAD
     here = Place(narrow)
     links = Links(send, recv)
+    last = local.shape[0]
+    loads = [
+        pltpu.make_async_copy(source, target, local.at[last - 4 + index])
+        for index, (source, target) in enumerate(
+            ((x_hbm, x_ref), (w1_hbm, w1_ref), (wo_hbm, wo_ref), (w2_hbm, w2_ref))
+        )
+    ]
+    for copy in loads:
+        copy.start()
     me, hops = here.me, range(1, here.depth)
     routes = [(way, hop) for hop in hops for way in range(2)]
 
@@ -353,6 +362,8 @@
     send_own("v")
     send_own("a")
 
+    for copy in loads:
+        copy.wait()
     inner = w1_ref.shape[1]
     e_own[:, 0:inner] = w1_ref[...].astype(BF16)
     e_own[:, inner : inner + width] = wo_ref[...].astype(BF16)
@@ -542,7 +553,7 @@
     part = heads // 4 * LANES
     return pl.pallas_call(
         functools.partial(gather_kernel, narrow),
-        in_specs=[vmem] * 8,
+        in_specs=[vmem] * 4 + [hbm] * 4,
         out_specs=[hbm] * 7 + [vmem] * 5,
         out_shape=[
             shape((rows, heads * LANES), BF16),
@@ -569,15 +580,19 @@
             pltpu.VMEM((rows, width), BF16),
             pltpu.VMEM((rows, heads * LANES), BF16),
             pltpu.VMEM((rows, LANES), BF16),
+            pltpu.VMEM(x.shape, x.dtype),
+            pltpu.VMEM(wo.shape, F32),
+            pltpu.VMEM(w1.shape, F32),
+            pltpu.VMEM(w2.shape, F32),
             pltpu.SemaphoreType.DMA((count,)),
             pltpu.SemaphoreType.DMA((count,)),
-            pltpu.SemaphoreType.DMA((11 + heads,)),
+            pltpu.SemaphoreType.DMA((15 + heads,)),
         ],
         compiler_params=pltpu.CompilerParams(
             vmem_limit_bytes=VMEM_LIMIT, collective_id=0, has_side_effects=True
         ),
         name="gather",
-    )(x, proj, wo, w1, w2, vec, segments, types)
+    )(proj, vec, segments, types, x, wo, w1, w2)
 
 
 def key_pair(keyval, kmask, low):
@@ -1490,11 +1505,15 @@
 
 
 def update_kernel(narrow, n_ref, fa_ref, fo_ref, f1_ref, fw_ref, v_ref, *refs):
-    ins, outs = refs[0:15], refs[15:35]
+    ins, whole, outs, norm_ref, copied = refs[0:15], refs[15:17], refs[17:37], refs[37], refs[38:40]
+    step = pl.program_id(0)
+    for source, target in zip(whole, copied):
+        target[...] = source[...]
     heads = fa_ref.shape[1] // GROUP
     width = heads * HEAD
     norm = jnp.sqrt(n_ref[0:1, 0:1])
     factor = jnp.minimum(1.0, clip_limit / (norm + 1e-06))
+    norm_ref[...] = norm
 
     def store(index, rows, cols, grad):
         news = update_tile(*(ins[5 * t + index][rows, cols] for t in range(3)), grad, factor, index)
@@ -1519,7 +1538,7 @@
     store(2, every, every, f1_ref[...])
     store(3, every, every, fw_ref[...])
 
-    @pl.when(pl.program_id(0) == 0)
+    @pl.when(step == 0)
     def _():
         count, span = ins[4].shape
         me = lax.axis_index("narrow")
@@ -1527,7 +1546,7 @@
         store(4, every, every, turned[0:count, 0:span])
 
 
-def update_call(narrow, norm, shards, vec, masters, firsts, seconds):
+def update_call(narrow, norm, shards, vec, masters, firsts, seconds, whole):
     share = shards[0].shape[0]
     steps = share // 48 if share % 48 == 0 else share // 16
 
@@ -1546,12 +1565,15 @@
     return pl.pallas_call(
         functools.partial(update_kernel, narrow),
         grid=(steps,),
-        in_specs=[fixed(norm), *(rows_of(a) for a in shards), fixed(vec)] + group(masters) * 3,
-        out_specs=group(masters) * 4,
-        out_shape=shapes(masters, F32) * 3 + shapes(masters, BF16),
+        in_specs=[fixed(norm), *(rows_of(a) for a in shards), fixed(vec)] + group(masters) * 3 + [rows_of(a) for a in whole],
+        out_specs=group(masters) * 4 + [pl.BlockSpec((1, 1), lambda i: (0, 0))] + [rows_of(a) for a in whole],
+        out_shape=shapes(masters, F32) * 3
+        + shapes(masters, BF16)
+        + [jax.ShapeDtypeStruct((1, 1), F32)]
+        + [jax.ShapeDtypeStruct(a.shape, a.dtype) for a in whole],
         compiler_params=pltpu.CompilerParams(vmem_limit_bytes=VMEM_LIMIT),
         name="update",
-    )(norm, *shards, vec, *masters, *firsts, *seconds)
+    )(norm, *shards, vec, *masters, *firsts, *seconds, *whole)
 
 
 def by_head(array_in):
@@ -1623,11 +1645,13 @@
             grad_r1, grad_expand, grad_reduce, grad_ctx_w, reduce_weight.shape[0], seq_len,
         )
         shards = (shard_a, shard_o, shard_1, shard_w)
-        updated = update_call(narrow, norm, shards, grad_vectors, masters, firsts, seconds)
+        *updated, grad_norm, block_out, input_grad = update_call(
+            narrow, norm, shards, grad_vectors, masters, firsts, seconds, (block_out, input_grad)
+        )
         return (
             block_out.reshape(out_shape),
             input_grad.reshape(out_shape),
-            jnp.sqrt(norm[0, 0]),
+            grad_norm.reshape(()),
             *updated,
         )
     grad_proj, grad_proj_w, grad_sums = attend_back_call(

time: 283 us -> 276 us (0.975)
  local copies, waits for them, and re-layouts: 4.71 us -> 0 us
    unnamed x6 -> x0, local copies, waits for them, and re-layouts: 3.52 us -> none
where the time goes in v4:
time: 276 us; the launch traced here: 272 us
  Pallas kernels  271 us (98%)
    pallas_call x1, Pallas kernels, reduce_call(): pl.pallas_call(functools.partial(reduce_kernel, narrow, length, groups, d...  97.7 us
    pallas_call x1, Pallas kernels, gather_call(): pl.pallas_call(functools.partial(gather_kernel, narrow), in_specs=[vmem]...  87.2 us
    pallas_call x1, Pallas kernels, middle_call(): pl.pallas_call(functools.partial(middle_kernel, narrow), in_specs=[hbm, h...  71.5 us
    pallas_call x1, Pallas kernels, update_call(): pl.pallas_call(functools.partial(update_kernel, narrow), grid=(steps,), i...  14.8 us

profile of v4, /device:TPU:0, one launch (start us, length us, event | category | flops | bytes accessed | tf_op | source)
XLA Modules:
  0.0 272.1 jit_solution(3180164268585559779)
XLA Ops:
  0.7 87.2 %gather.1 = (bf16[1280,1536]{1,0:T(8,128)(2,1)}, bf16[1280,1536]{1,0:T(8,128)(2,1)}, bf16[1280,768]{1,0:T(8,128)(2,1)}, bf16[1280,1536]{1,0:T(8,128)(2,1)}, bf16...) custom-call(f32[96,4608]{1,0:T(8,128)} %refs_0_.1, ...), custom_call_target="tpu_custom_call" | custom-call | tf_op jit(solution)/shard_map/gather/pallas_call | solution.py:554
  87.9 71.5 %middle.1 = (bf16[1280,768]{1,0:T(8,128)(2,1)}, f32[1280,768]{1,0:T(8,128)}, bf16[1280,768]{1,0:T(8,128)(2,1)}, bf16[2,4,96,1536]{3,2,1,0:T(8,128)(2,1)}, bf16[7...) custom-call(bf16[1280,768]{1,0:T(8,128)(2,1)} %bitcast.6, ...), custom_call_target="tpu_custom_call" | custom-call | tf_op jit(solution)/shard_map/middle/pallas_call | solution.py:1430
  159.4 97.7 %reduce.1 = (bf16[1280,768]{1,0:T(8,128)(2,1)}, bf16[96,3072]{1,0:T(8,128)(2,1)}, bf16[96,768]{1,0:T(8,128)(2,1)}, bf16[384,768]{1,0:T(8,128)(2,1)}, bf16[96,460...) custom-call(bf16[768,1280]{1,0:T(8,128)(2,1)} %get-tuple-element.72.xt, ...), custom_call_target="tpu_custom_call" | custom-call | tf_op jit(solution)/shard_map/reduce/pallas_call | solution.py:1167
  257.1 14.8 %update.1 = (f32[96,4608]{1,0:T(8,128)}, f32[96,768]{1,0:T(8,128)}, f32[96,3072]{1,0:T(8,128)}, f32[384,768]{1,0:T(8,128)}, f32[15,96]{1,0:T(8,128)}, /*index=5*...) custom-call(f32[8,128]{1,0:T(8,128)} %get-tuple-element.90.n_ref, ...), custom_call_target="tpu_custom_call" | custom-call | tf_op jit(solution)/shard_map/update/pallas_call | solution.py:1565

commit v5 on v4

--- a/solution.py
+++ b/solution.py
@@ -1023,15 +1023,15 @@
         6: [lambda: red.share_pass(chunk_w)],
         7: [lambda: finish(chunk_1[0])],
         8: [lambda: red.plane_turn(a[0])],
-        9: [lambda: merge(1), lambda: finish(chunk_1[1]), lambda: red.share_pass(chunk_1[0])],
-        10: [lambda: turn_z(a[0])],
-        11: [lambda: red.plane_turn(a[1]), lambda: merge(2), lambda: red.share_pass(chunk_1[1])],
+        9: [lambda: merge(1), lambda: red.share_pass(chunk_1[0])],
+        10: [lambda: turn_z(a[0]), lambda: finish(chunk_1[1])],
+        11: [lambda: merge(2), lambda: red.plane_turn(a[1]), lambda: red.share_pass(chunk_1[1])],
     }
     tail = [
         [lambda: turn_z(a[1])],
         [lambda: merge(3), vec_pair, lambda: red.plane_turn(a[2])],
-        [lambda: turn_z(a[2]), lambda: finish(a[0])],
-        [lambda: red.plane_turn(a[3]), vec_plane],
+        [lambda: turn_z(a[2])],
+        [lambda: red.plane_turn(a[3]), lambda: finish(a[0]), vec_plane],
         [lambda: turn_z(a[3]), lambda: finish(a[1]), lambda: red.share_pass(a[0]), vec_depth],
         [lambda: finish(a[2]), vec_done, lambda: red.share_pass(a[1])],
     ]

time: 276 us -> 279 us (1.011)
  Pallas kernels: 271 us -> 274 us
    pallas_call x1, Pallas kernels: 97.7 us -> 101 us  [reduce_call(): pl.pallas_call(functools.partial(reduce_kernel, narrow, length, groups, d...]
where the time goes in v5:
time: 279 us; the launch traced here: 275 us
  Pallas kernels  274 us (98%)
    pallas_call x1, Pallas kernels, reduce_call(): pl.pallas_call(functools.partial(reduce_kernel, narrow, length, groups, d...  101 us
    pallas_call x1, Pallas kernels, gather_call(): pl.pallas_call(functools.partial(gather_kernel, narrow), in_specs=[vmem]...  87.2 us
    pallas_call x1, Pallas kernels, middle_call(): pl.pallas_call(functools.partial(middle_kernel, narrow), in_specs=[hbm, h...  71.5 us
    pallas_call x1, Pallas kernels, update_call(): pl.pallas_call(functools.partial(update_kernel, narrow), grid=(steps,), i...  14.8 us

profile of v5, /device:TPU:0, one launch (start us, length us, event | category | flops | bytes accessed | tf_op | source)
XLA Modules:
  0.0 274.9 jit_solution(12454827722999486745)
XLA Ops:
  0.7 87.2 %gather.1 = (bf16[1280,1536]{1,0:T(8,128)(2,1)}, bf16[1280,1536]{1,0:T(8,128)(2,1)}, bf16[1280,768]{1,0:T(8,128)(2,1)}, bf16[1280,1536]{1,0:T(8,128)(2,1)}, bf16...) custom-call(f32[96,4608]{1,0:T(8,128)} %refs_0_.1, ...), custom_call_target="tpu_custom_call" | custom-call | tf_op jit(solution)/shard_map/gather/pallas_call | solution.py:554
  87.9 71.5 %middle.1 = (bf16[1280,768]{1,0:T(8,128)(2,1)}, f32[1280,768]{1,0:T(8,128)}, bf16[1280,768]{1,0:T(8,128)(2,1)}, bf16[2,4,96,1536]{3,2,1,0:T(8,128)(2,1)}, bf16[7...) custom-call(bf16[1280,768]{1,0:T(8,128)(2,1)} %bitcast.6, ...), custom_call_target="tpu_custom_call" | custom-call | tf_op jit(solution)/shard_map/middle/pallas_call | solution.py:1430
  159.4 100.5 %reduce.1 = (bf16[1280,768]{1,0:T(8,128)(2,1)}, bf16[96,3072]{1,0:T(8,128)(2,1)}, bf16[96,768]{1,0:T(8,128)(2,1)}, bf16[384,768]{1,0:T(8,128)(2,1)}, bf16[96,460...) custom-call(bf16[768,1280]{1,0:T(8,128)(2,1)} %get-tuple-element.72.xt, ...), custom_call_target="tpu_custom_call" | custom-call | tf_op jit(solution)/shard_map/reduce/pallas_call | solution.py:1167
  259.9 14.8 %update.1 = (f32[96,4608]{1,0:T(8,128)}, f32[96,768]{1,0:T(8,128)}, f32[96,3072]{1,0:T(8,128)}, f32[384,768]{1,0:T(8,128)}, f32[15,96]{1,0:T(8,128)}, /*index=5*...) custom-call(f32[8,128]{1,0:T(8,128)} %get-tuple-element.90.n_ref, ...), custom_call_target="tpu_custom_call" | custom-call | tf_op jit(solution)/shard_map/update/pallas_call | solution.py:1565
